TPU v7x, 256 devices: a whole 4x4x8 slice. The times are simulated.
256 devices in a mesh: seq: 32 (over x, z_hi, y), slide: 8 (over z_lo, core).
Axes of the slice: x: 4, y: 4, z: 8 (z_hi: 2, z_lo: 4; z = z_hi * 4 + z_lo), core: 2. Of those that a mesh axis runs over, the one named last changes fastest.
Arguments:
- tiles: bfloat16 [8, 16384, 1536], P('slide', 'seq'), may hold values from -6 to 6
- w_embed: bfloat16 [1536, 768], replicated, may hold values from -0.15625 to 0.15625
- attn_gain: float32 [768], replicated, may hold values from 0.5 to 1.5
- w_query: bfloat16 [768, 768], replicated, may hold values from -8 to 8, as said below
- w_key: bfloat16 [768, 768], replicated, may hold values from -8 to 8, as said below
- w_value: bfloat16 [768, 768], replicated, may hold values from -0.21875 to 0.21875
- w_out: bfloat16 [768, 768], replicated, may hold values from -0.21875 to 0.21875
- w_head: bfloat16 [768, 768], replicated, may hold values from -0.21875 to 0.21875
- head_offset: int32 [16], replicated, may hold values from 0 to 31
- slide_code: int32 [8], P('slide'), may hold values from 0 to 3, as said below
- report_emb: bfloat16 [8, 768], P('slide'), may hold values from -6 to 6
- report_code: int32 [8], P('slide'), may hold values from 0 to 3, as said below
Outputs:
- encoded: bfloat16 [8, 16384, 768], P('slide', 'seq')
- slide_unit_vectors: float32 [8, 768], P('slide')
- logits: float32 [8, 8], replicated
- loss: float32 [], replicated
Inputs may be any that keep to these rules, and one draw needn't show every extreme that they name: `w_query`: entries of a projection of 768 features. `w_key`: entries of a projection of 768 features. `slide_code`: diagnosis code of a slide. `report_code`: diagnosis code of a report; the report of each index has a code different from the slide of the same index.
All inputs are finite; a program needn't handle non-finite values.
Results may differ from a plain program's by a relative error of at most 0.02.
Values may be sent and summed in bfloat16 or wider, within the bound.
No kernel may reach another device: no remote copies, remote signals or barrier semaphores. Data moves between devices by JAX's collectives and lax.ppermute only.
A program may use at most 128 MiB of HBM per device.

v0:
```python
import math

import jax
import jax.numpy as jnp
from jax import lax
from jax.sharding import PartitionSpec as P

RATE = 32


SOFTMAX_TEMPER = 1.0 / 0.07
NORM_EPS = 1e-05


def from_partner(x, axis, distance):
    return lax.ppermute(x, axis, [(i, i ^ 1 << distance) for i in range(lax.axis_size(axis))])


def layer_norm(inputs, gain):
    floats = inputs.astype(jnp.float32)
    centre = jnp.mean(floats, axis=-1, keepdims=True)
    spread = jnp.mean(jnp.square(floats - centre), axis=-1, keepdims=True)
    return (floats - centre) * lax.rsqrt(spread + NORM_EPS) * gain


def unit_rows(matrix):
    return matrix * lax.rsqrt(jnp.sum(matrix * matrix, axis=-1, keepdims=True) + 1e-06)


def project_rows(pooled, w_head):
    return unit_rows(jnp.dot(pooled, w_head.astype(jnp.float32), precision=lax.Precision.HIGHEST))


def contrastive(slide_unit_vectors, report_vectors, slide_codes, report_codes):
    logits = SOFTMAX_TEMPER * jnp.dot(
        slide_unit_vectors, report_vectors.T, precision=lax.Precision.HIGHEST
    )
    count = logits.shape[0]
    same = (slide_codes[:, None] == report_codes[None, :]) | jnp.eye(count, dtype=bool)
    positive = jnp.where(same, 1.0, 0.0).astype(logits.dtype)
    row_peak = jnp.max(logits, axis=1, keepdims=True)
    row_lse = row_peak + jnp.log(jnp.sum(jnp.exp(logits - row_peak), axis=1, keepdims=True))
    col_peak = jnp.max(logits, axis=0, keepdims=True)
    col_lse = col_peak + jnp.log(jnp.sum(jnp.exp(logits - col_peak), axis=0, keepdims=True))
    slide_terms = -jnp.sum(positive * (logits - row_lse), axis=1) / jnp.sum(positive, axis=1)
    report_terms = -jnp.sum(positive * (logits - col_lse), axis=0) / jnp.sum(positive, axis=0)
    loss = 0.5 * (jnp.mean(slide_terms) + jnp.mean(report_terms))
    return (logits, loss)


def dilated_rows(tensor, head_offset):
    slides_here, tok_here, heads_count, head_width = tensor.shape
    grouped = tensor.reshape(slides_here, tok_here // RATE, RATE, heads_count, head_width)
    chosen = jnp.arange(RATE, dtype=jnp.int32)[:, None] == head_offset[None, :]
    picked = jnp.where(chosen[None, None, :, :, None], grouped, jnp.zeros((), tensor.dtype))
    summed = jnp.sum(picked, axis=2)
    return summed.reshape(slides_here, tok_here // RATE, heads_count * head_width)


def near_state(block_items, score_scale):
    seg_queries, seg_keys, seg_values = block_items
    scores = (
        jnp.einsum("qhd,khd->qhk", seg_queries, seg_keys, preferred_element_type=jnp.float32)
        * score_scale
    )
    peak = jnp.max(scores, axis=-1)
    weights = jnp.exp(scores - peak[..., None])
    accum = jnp.einsum(
        "qhk,khd->qhd", weights.astype(jnp.bfloat16), seg_values, preferred_element_type=jnp.float32
    )
    return (peak, jnp.sum(weights, axis=-1), accum)


def far_update(softmax_state, pieces, queries, score_scale):
    peak, total_weight, accum = softmax_state
    piece_keys, piece_values = pieces
    piece_shape = (piece_keys.shape[0], piece_keys.shape[1], queries.shape[2], queries.shape[3])
    scores = (
        jnp.einsum(
            "sqhd,skhd->sqhk",
            queries,
            piece_keys.reshape(piece_shape),
            preferred_element_type=jnp.float32,
        )
        * score_scale
    )
    new_peak = jnp.max(scores, axis=-1)
    shrink = jnp.exp(peak - new_peak)
    weights = jnp.exp(scores - new_peak[..., None])
    total_weight = total_weight * shrink + jnp.sum(weights, axis=-1)
    update = jnp.einsum(
        "sqhk,skhd->sqhd",
        weights.astype(jnp.bfloat16),
        piece_values.reshape(piece_shape),
        preferred_element_type=jnp.float32,
    )
    accum = accum * shrink[..., None] + update
    return (new_peak, total_weight, accum)


def on_device(
    tiles,
    w_embed,
    attn_gain,
    w_query,
    w_key,
    w_value,
    w_out,
    w_head,
    head_offset,
    slide_code,
    report_emb,
    report_code,
):
    slides_here, tok_here, in_width = tiles.shape
    model_width = w_embed.shape[1]
    heads_count = head_offset.shape[0]
    head_width = model_width // heads_count
    seq_ranks = lax.axis_size("seq")
    seq_length = tok_here * seq_ranks
    score_scale = 1.0 / math.sqrt(head_width)
    head_shape = (slides_here, tok_here, heads_count, head_width)
    tile_rows = tiles.reshape(slides_here * tok_here, in_width)
    embedded = jnp.dot(tile_rows, w_embed, preferred_element_type=jnp.float32).astype(jnp.bfloat16)
    normed = layer_norm(embedded, attn_gain).astype(jnp.bfloat16)
    queries = (
        jnp.dot(normed, w_query, preferred_element_type=jnp.float32)
        .astype(jnp.bfloat16)
        .reshape(head_shape)
    )
    keys_all = (
        jnp.dot(normed, w_key, preferred_element_type=jnp.float32)
        .astype(jnp.bfloat16)
        .reshape(head_shape)
    )
    values_all = (
        jnp.dot(normed, w_value, preferred_element_type=jnp.float32)
        .astype(jnp.bfloat16)
        .reshape(head_shape)
    )
    far_key = dilated_rows(keys_all, head_offset)
    far_value = dilated_rows(values_all, head_offset)
    stacked = jnp.stack((keys_all, values_all))
    partner = from_partner(stacked, "seq", 0)
    upper_half = lax.axis_index("seq") % 2 == 1
    segment_couple = jnp.where(
        upper_half,
        jnp.concatenate((partner, stacked), axis=2),
        jnp.concatenate((stacked, partner), axis=2),
    )

    def near_block(block_items):
        return near_state(block_items, score_scale)

    near_peak, near_total, near_accum = lax.map(
        near_block, (queries, segment_couple[0], segment_couple[1])
    )
    initial = (
        jnp.full((slides_here, tok_here, heads_count), -jnp.inf, jnp.float32),
        jnp.zeros((slides_here, tok_here, heads_count), jnp.float32),
        jnp.zeros(head_shape, jnp.float32),
    )
    gathered = (
        lax.all_gather(far_key, "seq", axis=1, tiled=True),
        lax.all_gather(far_value, "seq", axis=1, tiled=True),
    )
    distant_peak, far_total, far_accum = far_update(initial, gathered, queries, score_scale)
    highest = jnp.maximum(near_peak, distant_peak)
    near_factor = jnp.exp(near_peak - highest)
    far_factor = jnp.exp(distant_peak - highest)
    mixed = (near_accum * near_factor[..., None] + far_accum * far_factor[..., None]) / (
        near_total * near_factor + far_total * far_factor
    )[..., None]
    attended = mixed.astype(jnp.bfloat16).reshape(slides_here * tok_here, model_width)
    encoded = (
        embedded.astype(jnp.float32) + jnp.dot(attended, w_out, preferred_element_type=jnp.float32)
    ).astype(jnp.bfloat16)
    encoded = encoded.reshape(slides_here, tok_here, model_width)
    local_sum = jnp.sum(encoded, axis=1, dtype=jnp.float32)
    report_local = unit_rows(report_emb.astype(jnp.float32))
    slide_codes = slide_code.astype(jnp.float32)
    report_codes = report_code.astype(jnp.float32)
    pooled = lax.psum(local_sum, "seq") / seq_length
    slide_unit_vectors = project_rows(pooled, w_head)
    all_vecs, all_reports, all_slide_codes, all_report_codes = (
        lax.all_gather(slide_unit_vectors, "slide", axis=0, tiled=True),
        lax.all_gather(report_local, "slide", axis=0, tiled=True),
        lax.all_gather(slide_codes, "slide", axis=0, tiled=True),
        lax.all_gather(report_codes, "slide", axis=0, tiled=True),
    )
    logits, loss = contrastive(all_vecs, all_reports, all_slide_codes, all_report_codes)
    return (encoded, slide_unit_vectors, logits, loss)


def solution(mesh):
    return jax.shard_map(
        on_device,
        mesh=mesh,
        in_specs=(
            P("slide", "seq", None),
            P(),
            P(),
            P(),
            P(),
            P(),
            P(),
            P(),
            P(),
            P("slide"),
            P("slide", None),
            P("slide"),
        ),
        out_specs=(P("slide", "seq", None), P("slide", None), P(), P()),
        check_vma=False,
    )
```

profile of v0, /device:TPU:1, one launch (start us, length us, event | category | flops | bytes accessed | tf_op | source)
XLA Modules:
  0.0 508.1 jit_solution(15953012690753790730)
XLA Ops:
  0.7 1.6 copy-done
  2.3 2.9 convert_reduce_fusion
  5.6 0.9 convolution_convert_fusion.1
  6.9 0.9 convolution_convert_fusion.2
  8.3 1.3 pad_maximum_fusion
  9.6 2.1 collective-permute-start
  11.7 3.5 reshape_reshape.7
  15.2 3.5 reshape_reshape.6
  21.4 16.1 %all-gather.2 = f32[8,1,768]{2,1,0:T(1,128)} all-gather(f32[1,1,768]{2,1,0:T(1,128)S(1)} %multiply_bitcast_fusion), channel_id=1, replica_groups=mesh['seq'=32,'slide'=8] {'slide'}, dimensions={0}, use_global_device_ids=true | all-gather | bytes 27648 | tf_op jit(solution)/shard_map/all_gather | solution.py:187
  37.4 3.0 convolution_convert_fusion
  40.4 1.4 copy.29
  41.9 3.4 select_reduce_fusion.1
  45.5 112.3 %all_gather.19 = bf16[1,512,768]{2,1,0:T(8,128)(2,1)} all-gather(bf16[1,16,768]{2,1,0:T(8,128)(2,1)S(1)} %reshape.285), channel_id=1, replica_groups=mesh['seq'=32,'slide'=8] {'seq'}, dimensions={1}, use_global_device_ids=true | all-gather | bytes 811008 | tf_op jit(solution)/shard_map/all_gather | solution.py:165
  157.8 1.4 copy.32
  159.2 102.4 %all_gather.18 = bf16[1,512,768]{2,1,0:T(8,128)(2,1)} all-gather(bf16[1,16,768]{2,1,0:T(8,128)(2,1)S(1)} %reshape.283), channel_id=1, replica_groups=mesh['seq'=32,'slide'=8] {'seq'}, dimensions={1}, use_global_device_ids=true | all-gather | bytes 811008 | tf_op jit(solution)/shard_map/all_gather | solution.py:164
  262.2 0.7 convert_dynamic-update-slice_fusion
  263.0 0.7 convert_dynamic-update-slice_fusion.1
  263.7 2.3 copy.31
  266.0 40.3 %all-reduce.2 = (f32[8]{0:T(128)S(1)}, f32[8]{0:T(128)S(1)}) all-reduce(f32[8]{0:T(128)S(1)} %convert_dynamic-update-slice_fusion, f32[8]{0:T(128)S(1)} %convert_dynamic-update-slice_fusion.1), channel_id=1, replica_groups=mesh['seq'=32,'slide'=8] {'slide'}, use_global_device_ids=true, to_apply=%add.1 | all-reduce | flops 16 | bytes 128
  306.3 3.5 bitcast_reduce_fusion.1
  309.9 5.7 %copy-done.2 = f32[16,512,512]{2,1,0:T(8,128)} copy-done((f32[16,512,512]{2,1,0:T(8,128)}, f32[16,512,512]{2,1,0:T(8,128)S(1)}, u32[]{:S(2)}) %copy-start.2) | copy-done | bytes 16777240
  315.6 4.0 fusion.9
  319.6 8.6 %fusion.6 = f32[512,16]{0,1:T(8,128)S(1)} fusion(f32[16,512,512]{2,1,0:T(8,128)} %copy-done.2, f32[512,16]{0,1:T(8,128)S(1)} %get-tuple-element.43), kind=kLoop, calls=%fused_computation.9 | loop fusion | flops 12574720 | bytes 16842752 | tf_op jit(solution)/shard_map/reduce_sum | solution.py:90
  328.1 2.5 maximum_select_fusion
  330.6 13.1 %bitcast_reduce_fusion = (f32[512,16]{0,1:T(8,128)S(1)}, f32[16,1024,512]{2,1,0:T(8,128)}) fusion(bf16[512,16,48]{0,2,1:T(8,128)(2,1)S(1)} %bitcast.103, bf16[2,1,1024,16,48]{2,4,3,1,0:T(8,128)(2,1)S(1)} %maximum_select_fusion), kind=kOutput, calls=%fused_computation.1 | convolution fusion | flops 822075392 | bytes 35946496 | tf_op jit(solution)/shard_map/while/body/eval_jaxpr/qhd,khd->qhk/dot_general | solution.py:63
  343.7 13.7 %fusion.1 = f32[512,16]{0,1:T(8,128)S(1)} fusion(f32[16,1024,512]{2,1,0:T(8,128)} %get-tuple-element.46, f32[512,16]{0,1:T(8,128)S(1)} %get-tuple-element.45), kind=kLoop, calls=%fused_computation.3 | loop fusion | flops 25157632 | bytes 33619968 | tf_op jit(solution)/shard_map/while/body/eval_jaxpr/reduce_sum | solution.py:71
  357.5 14.8 %fusion.25 = bf16[1,512,16,48]{1,3,2,0:T(8,128)(2,1)} fusion(f32[16,48,512]{2,1,0:T(8,128)S(1)} %copy-done.3, f32[16,1024,512]{2,1,0:T(8,128)} %get-tuple-element.46, f32[512,16]{0,1:T(8,128)S(1)} %get-tuple-element.45, bf16[2,1,1024,16,48]{2,4,3,1,0:T(8,128)(2,1)S(1)} %maximum_select_fusion, f32[512,16]{0,1:T(8,128)S(1)} %get-tuple-element.37, ...), kind=kOutput, calls=%fused_computation.39 | convolution fusion | flops 832831488 | bytes 37650432 | tf_op jit(solution)/shard_map/while/body/eval_jaxpr/qhk,khd->qhd/dot_general | solution.py:68
  372.3 3.6 convert_reduce_fusion.1
  375.9 96.3 %psum.7 = f32[1,768]{1,0:T(1,128)S(1)} all-reduce(f32[1,768]{1,0:T(1,128)S(1)} %reduce_sum.169), channel_id=1, replica_groups=mesh['seq'=32,'slide'=8] {'seq'}, use_global_device_ids=true, to_apply=%region_9.10 | all-reduce | flops 768 | bytes 6144 | tf_op jit(solution)/shard_map/psum | solution.py:183
  474.7 28.2 %all-gather.1 = f32[8,1,768]{2,1,0:T(1,128)S(1)} all-gather(f32[1,1,768]{2,1,0:T(1,128)S(1)} %reshape.298), channel_id=2, replica_groups=mesh['seq'=32,'slide'=8] {'slide'}, dimensions={0}, use_global_device_ids=true | all-gather | bytes 27648 | tf_op jit(solution)/shard_map/all_gather | solution.py:186
  502.9 1.0 fusion.51
  504.9 0.7 fusion.44
  (51 shorter events, 5.7 us)
Async XLA Ops:
  0.6 1.7 copy-start
  0.6 4.9 copy-start.12
  0.7 4.9 copy-start.10
  5.2 1.3 copy-start.5
  5.6 1.3 copy-start.11
  9.6 318.5 %collective-permute-start = (bf16[2,1,512,16,48]{2,4,3,1,0:T(8,128)(2,1)}, bf16[2,1,512,16,48]{2,4,3,1,0:T(8,128)(2,1)}, u32[]{:S(2)}, u32[]{:S(2)}) collective-permute-start(bf16[2,1,512,16,48]{2,4,3,1,0:T(8,128)(2,1)} %pad_maximum_fusion), channel_id=1, source_target_pairs={{0,8},{8,0},{16,24},{24,16},{32,40},{40,32},{48,56},{56,48},{64,72... | collective-permute-start | bytes 4718600 | tf_op jit(solution)/shard_map/ppermute | solution.py:16
  15.2 4.8 copy-start.8
  15.2 6.2 %copy-start.9 = (s32[16]{0:T(128)S(1)}, s32[16]{0:T(128)}, u32[]{:S(2)}) copy-start(s32[16]{0:T(128)} %param.20) | copy-start | bytes 196
  15.2 22.3 %copy-start.6 = (bf16[512,768]{1,0:T(8,128)(2,1)S(1)}, bf16[512,768]{1,0:T(8,128)(2,1)}, u32[]{:S(2)}) copy-start(bf16[512,768]{1,0:T(8,128)(2,1)} %copy-done.5) | copy-start | bytes 2359300
  45.5 216.2 %copy-start.13 = (u32[256]{0:T(256)S(1)}, u32[256]{0:T(256)}, u32[]{:S(2)}) copy-start(u32[256]{0:T(256)} %constant.83) | copy-start | bytes 3076
  309.9 5.7 %copy-start.2 = (f32[16,512,512]{2,1,0:T(8,128)}, f32[16,512,512]{2,1,0:T(8,128)S(1)}, u32[]{:S(2)}) copy-start(f32[16,512,512]{2,1,0:T(8,128)S(1)} %get-tuple-element.44) | copy-start | bytes 50331652
  343.7 13.7 %copy-start.3 = (f32[16,48,512]{2,1,0:T(8,128)S(1)}, f32[16,48,512]{2,1,0:T(8,128)}, u32[]{:S(2)}) copy-start(f32[16,48,512]{2,1,0:T(8,128)} %fusion.9) | copy-start | bytes 4718596
  372.3 99.9 %copy-start.4 = (bf16[768,768]{1,0:T(8,128)(2,1)S(1)}, bf16[768,768]{1,0:T(8,128)(2,1)}, u32[]{:S(2)}) copy-start(bf16[768,768]{1,0:T(8,128)(2,1)} %param.19) | copy-start | bytes 3538948
  372.3 134.7 %copy-start.1 = (bf16[1536,768]{1,0:T(8,128)(2,1)S(1)}, bf16[1536,768]{1,0:T(8,128)(2,1)}, u32[]{:S(2)}) copy-start(bf16[1536,768]{1,0:T(8,128)(2,1)} %param.13) | copy-start | bytes 7077892
  503.9 3.1 copy-start.7
where the time goes:
time: 509 us; the launch traced here: 508 us
  blocking collectives  396 us (78%)
  matrix products  48.2 us (9%)
  other arithmetic  34.2 us (7%)
  local copies, waits for them, and re-layouts  21.9 us (4%)
  between operations  6.06 us (1%)
    all_gather x1, blocking collectives, on_device(): lax.all_gather(far_value, 'seq', axis=1, tiled=True)  112 us
    all_gather x1, blocking collectives, on_device(): lax.all_gather(far_key, 'seq', axis=1, tiled=True)  102 us
    psum x1, blocking collectives, on_device(): pooled = lax.psum(local_sum, 'seq') / seq_length  96.3 us
    unnamed x1, blocking collectives  40.3 us
    all_gather x1, blocking collectives, on_device(): lax.all_gather(slide_unit_vectors, 'slide', axis=0, tiled=True)  28.2 us
    all_gather x1, blocking collectives, on_device(): lax.all_gather(report_local, 'slide', axis=0, tiled=True)  16.1 us
    dot_general x1, matrix products, near_state(): jnp.einsum('qhk,khd->qhd', weights.astype(jnp.bfloat16), seg_values, pref...  14.8 us
    reduce_sum x1, other arithmetic, near_state(): return (peak, jnp.sum(weights, axis=-1), accum)  13.7 us
  transfers between devices with their start and end apart: 1, of which 0 were waited for; matrix products, arithmetic and copies ran while one was open for 7% of the time, Pallas kernels for 0%

commit v1 on v0

v1 whole, which is shorter than its diff:
```python
import functools
import math

import jax
import jax.numpy as jnp
from jax import lax
from jax.experimental import pallas as pl
from jax.experimental.pallas import tpu as pltpu
from jax.sharding import PartitionSpec as P

RATE = 32
LANES = 128
SOFTMAX_TEMPER = 1.0 / 0.07
NORM_EPS = 1e-05
NT = (((1,), (1,)), ((), ()))
NN = (((1,), (0,)), ((), ()))
VMEM_LIMIT = 48 << 20


def layer_norm(inputs, gain):
    floats = inputs.astype(jnp.float32)
    centre = jnp.mean(floats, axis=-1, keepdims=True)
    spread = jnp.mean(jnp.square(floats - centre), axis=-1, keepdims=True)
    return (floats - centre) * lax.rsqrt(spread + NORM_EPS) * gain


def unit_rows(matrix):
    return matrix * lax.rsqrt(jnp.sum(matrix * matrix, axis=-1, keepdims=True) + 1e-06)


def contrastive(slide_unit_vectors, report_vectors, slide_codes, report_codes):
    logits = SOFTMAX_TEMPER * jnp.dot(
        slide_unit_vectors, report_vectors.T, precision=lax.Precision.HIGHEST
    )
    count = logits.shape[0]
    same = (slide_codes[:, None] == report_codes[None, :]) | jnp.eye(count, dtype=bool)
    positive = jnp.where(same, 1.0, 0.0).astype(logits.dtype)
    row_peak = jnp.max(logits, axis=1, keepdims=True)
    row_lse = row_peak + jnp.log(jnp.sum(jnp.exp(logits - row_peak), axis=1, keepdims=True))
    col_peak = jnp.max(logits, axis=0, keepdims=True)
    col_lse = col_peak + jnp.log(jnp.sum(jnp.exp(logits - col_peak), axis=0, keepdims=True))
    slide_terms = -jnp.sum(positive * (logits - row_lse), axis=1) / jnp.sum(positive, axis=1)
    report_terms = -jnp.sum(positive * (logits - col_lse), axis=0) / jnp.sum(positive, axis=0)
    loss = 0.5 * (jnp.mean(slide_terms) + jnp.mean(report_terms))
    return (logits, loss)


def share_with_group(row, axis):
    size = lax.axis_size(axis)
    copies = jnp.broadcast_to(row[None], (size,) + row.shape)
    return lax.all_to_all(copies, axis, 0, 0, tiled=True)


def swap_halves(x, axis):
    return lax.ppermute(x, axis, [(i, i ^ 1) for i in range(lax.axis_size(axis))])


def head_window(head, width):
    first = head * width // LANES * LANES
    last = -(-(head * width + width) // LANES) * LANES
    return first, last, head * width - first


def in_head_lanes(head, width):
    first, last, offset = head_window(head, width)
    lane = lax.broadcasted_iota(jnp.int32, (1, last - first), 1)
    return (lane >= offset) & (lane < offset + width)


def head_softmax(queries, keys, values, head, width):
    first, last, offset = head_window(head, width)
    mine = in_head_lanes(head, width)
    masked = jnp.where(mine, queries[:, first:last], jnp.zeros((), queries.dtype))
    scores = lax.dot_general(masked, keys[:, first:last], NT, preferred_element_type=jnp.float32)
    peak = jnp.max(scores, axis=1, keepdims=True)
    weights = jnp.exp(scores - peak).astype(jnp.bfloat16)
    padded = jnp.where(mine, values[:, first:last], jnp.ones((), values.dtype))
    mixed = lax.dot_general(weights, padded, NN, preferred_element_type=jnp.float32)
    spare = offset + width if offset + width < last - first else 0
    return peak, mixed[:, spare : spare + 1], mixed


def far_rows_kernel(x_ref, wk_ref, wv_ref, chosen_ref, out_ref):
    rows, width = x_ref.shape
    half = width // 2
    chosen = chosen_ref[...]
    for place, w_ref in enumerate((wk_ref, wv_ref)):
        full = jnp.dot(x_ref[...], w_ref[...], preferred_element_type=jnp.float32)
        grouped = full.reshape(rows // RATE, RATE, width) * chosen[None]
        picked = jnp.sum(grouped, axis=1).astype(out_ref.dtype)
        for part in range(2):
            out_ref[part, :, place * half : (place + 1) * half] = picked[
                :, part * half : (part + 1) * half
            ]


def near_kernel(part_ref, own_ref, other_ref, wq_ref, wk_ref, wv_ref, q_ref, mixed_ref, stats_ref,
                k_scr, v_scr, *, head_width, score_scale):
    step = pl.program_id(0)
    rows = own_ref.shape[0]
    half = wq_ref.shape[1]
    heads = half // head_width

    @pl.when(step == 0)
    def _():
        for place, x_ref in enumerate((own_ref, other_ref)):
            span = slice(place * rows, (place + 1) * rows)
            x = x_ref[...]
            q = jnp.dot(x, wq_ref[...], preferred_element_type=jnp.float32) * score_scale
            q_ref[span, :] = q.astype(q_ref.dtype)
            k = jnp.dot(x, wk_ref[...], preferred_element_type=jnp.float32)
            k_scr[span, :] = k.astype(k_scr.dtype)
            v = jnp.dot(x, wv_ref[...], preferred_element_type=jnp.float32)
            v_scr[span, :] = v.astype(v_scr.dtype)

    queries = q_ref[pl.ds(pl.multiple_of(step * rows, rows), rows), :]
    lane = lax.broadcasted_iota(jnp.int32, (1, LANES), 1)
    stats = jnp.zeros((rows, LANES), jnp.float32)
    for head in range(heads):
        first, last, _ = head_window(head, head_width)
        peak, total, mixed = head_softmax(queries, k_scr[...], v_scr[...], head, head_width)
        mine = in_head_lanes(head, head_width)
        if head == 0:
            mixed_ref[:, first:last] = mixed
        else:
            mixed_ref[:, first:last] = jnp.where(mine, mixed, mixed_ref[:, first:last])
        stats = jnp.where(lane == head, peak, stats)
        stats = jnp.where(lane == heads + head, total, stats)
    stats_ref[...] = stats


def far_kernel(q_ref, far_ref, near_ref, stats_ref, out_ref, sum_ref, acc_scr, *, head_width):
    half = q_ref.shape[1]
    heads = half // head_width
    keys, values = far_ref[:, :half], far_ref[:, half:]
    queries = q_ref[...]
    for head in range(heads):
        first, last, _ = head_window(head, head_width)
        peak, total, mixed = head_softmax(queries, keys, values, head, head_width)
        near_peak = stats_ref[:, head : head + 1]
        near_total = stats_ref[:, heads + head : heads + head + 1]
        highest = jnp.maximum(peak, near_peak)
        far_factor = jnp.exp(peak - highest)
        near_factor = jnp.exp(near_peak - highest)
        share = 1.0 / (total * far_factor + near_total * near_factor)
        mine = in_head_lanes(head, head_width)
        joined = mixed * (far_factor * share) + near_ref[:, first:last] * (near_factor * share)
        if head == 0:
            acc_scr[:, first:last] = joined
        else:
            acc_scr[:, first:last] = jnp.where(mine, joined, acc_scr[:, first:last])
    out_ref[...] = acc_scr[...].astype(out_ref.dtype)

    @pl.when(pl.program_id(0) == 0)
    def _():
        sum_ref[...] = jnp.zeros_like(sum_ref)

    sum_ref[...] += jnp.sum(acc_scr[...], axis=0, keepdims=True)


def on_device(
    tiles,
    w_embed,
    attn_gain,
    w_query,
    w_key,
    w_value,
    w_out,
    w_head,
    head_offset,
    slide_code,
    report_emb,
    report_code,
):
    _, rows, in_width = tiles.shape
    width = w_embed.shape[1]
    half = width // 2
    heads_count = head_offset.shape[0]
    head_width = width // heads_count
    ranks = lax.axis_size("seq")
    score_scale = 1.0 / math.sqrt(head_width)
    part = lax.axis_index("seq") % 2
    params = pltpu.CompilerParams(vmem_limit_bytes=VMEM_LIMIT)

    embedded = jnp.dot(
        tiles.reshape(rows, in_width), w_embed, preferred_element_type=jnp.float32
    ).astype(jnp.bfloat16)
    normed = layer_norm(embedded, attn_gain).astype(jnp.bfloat16)
    other_normed = swap_halves(normed, "seq")

    lane_offset = jnp.broadcast_to(head_offset[:, None], (heads_count, head_width)).reshape(1, width)
    chosen = (jnp.arange(RATE, dtype=jnp.int32)[:, None] == lane_offset).astype(jnp.float32)
    far_rows = rows // RATE
    payload = pl.pallas_call(
        far_rows_kernel,
        out_shape=jax.ShapeDtypeStruct((2, far_rows, width), jnp.bfloat16),
        compiler_params=params,
        name="far_rows",
    )(normed, w_key, w_value, chosen)
    payload = jnp.broadcast_to(payload[None], (ranks // 2, 2, far_rows, width))
    payload = payload.reshape(ranks, far_rows, width)
    far = lax.all_to_all(payload, "seq", 0, 0, tiled=True).reshape(ranks * far_rows, width)

    weight_spec = pl.BlockSpec((width, half), lambda i, p: (0, p[0]))
    whole = pl.BlockSpec((rows, width), lambda i, p: (0, 0))
    queries, near_mixed, stats = pl.pallas_call(
        functools.partial(near_kernel, head_width=head_width, score_scale=score_scale),
        grid_spec=pltpu.PrefetchScalarGridSpec(
            num_scalar_prefetch=1,
            grid=(2,),
            in_specs=[whole, whole, weight_spec, weight_spec, weight_spec],
            out_specs=[
                pl.BlockSpec((2 * rows, half), lambda i, p: (0, 0)),
                pl.BlockSpec((rows, half), lambda i, p: (i, 0)),
                pl.BlockSpec((rows, LANES), lambda i, p: (i, 0)),
            ],
            scratch_shapes=[
                pltpu.VMEM((2 * rows, half), jnp.bfloat16),
                pltpu.VMEM((2 * rows, half), jnp.bfloat16),
            ],
        ),
        out_shape=[
            jax.ShapeDtypeStruct((2 * rows, half), jnp.bfloat16),
            jax.ShapeDtypeStruct((2 * rows, half), jnp.float32),
            jax.ShapeDtypeStruct((2 * rows, LANES), jnp.float32),
        ],
        compiler_params=params,
        cost_estimate=pl.CostEstimate(
            flops=12_000_000_000, bytes_accessed=8_000_000, transcendentals=8_000_000
        ),
        name="near_attention",
    )(part.reshape(1), normed, other_normed, w_query, w_key, w_value)

    attended, attended_sum = pl.pallas_call(
        functools.partial(far_kernel, head_width=head_width),
        grid=(2,),
        in_specs=[
            pl.BlockSpec((rows, half), lambda i: (i, 0)),
            pl.BlockSpec((ranks * far_rows, width), lambda i: (0, 0)),
            pl.BlockSpec((rows, half), lambda i: (i, 0)),
            pl.BlockSpec((rows, LANES), lambda i: (i, 0)),
        ],
        out_specs=[
            pl.BlockSpec((rows, half), lambda i: (i, 0)),
            pl.BlockSpec((1, half), lambda i: (0, 0)),
        ],
        out_shape=[
            jax.ShapeDtypeStruct((2 * rows, half), jnp.bfloat16),
            jax.ShapeDtypeStruct((1, half), jnp.float32),
        ],
        scratch_shapes=[pltpu.VMEM((rows, half), jnp.float32)],
        compiler_params=params,
        cost_estimate=pl.CostEstimate(
            flops=6_000_000_000, bytes_accessed=6_000_000, transcendentals=4_000_000
        ),
        name="far_attention",
    )(queries, far, near_mixed, stats)

    local_sum = jnp.sum(embedded, axis=0, dtype=jnp.float32, keepdims=True)
    sums = share_with_group(jnp.concatenate((local_sum, attended_sum), axis=1), "seq")
    sums = jnp.sum(sums.reshape(ranks // 2, 2, width + half), axis=0)
    embedded_sum = jnp.sum(sums[:, :width], axis=0, keepdims=True)
    attended_total = sums[:, width:].reshape(1, width)
    mixed_total = jnp.dot(
        attended_total, w_out.astype(jnp.float32), precision=lax.Precision.HIGHEST
    )
    pooled = (embedded_sum + mixed_total) / (rows * ranks)
    slide_unit_vectors = unit_rows(
        jnp.dot(pooled, w_head.astype(jnp.float32), precision=lax.Precision.HIGHEST)
    )

    own_half, lent_half = attended[:rows], attended[rows:]
    other_half = swap_halves(lent_half, "seq")
    joined = jnp.where(
        part == 1,
        jnp.concatenate((other_half, own_half), axis=1),
        jnp.concatenate((own_half, other_half), axis=1),
    )
    encoded = embedded.astype(jnp.float32) + jnp.dot(
        joined, w_out, preferred_element_type=jnp.float32
    )
    encoded = encoded.astype(jnp.bfloat16).reshape(1, rows, width)

    report_local = unit_rows(report_emb.astype(jnp.float32))
    codes = jnp.stack((slide_code, report_code), axis=1).astype(jnp.float32)
    early = share_with_group(
        jnp.concatenate((report_local, jnp.pad(codes, ((0, 0), (0, LANES - 2)))), axis=1), "slide"
    )[:, 0]
    all_vecs = share_with_group(slide_unit_vectors, "slide")[:, 0]
    logits, loss = contrastive(all_vecs, early[:, :width], early[:, width], early[:, width + 1])
    return (encoded, slide_unit_vectors, logits, loss)


def solution(mesh):
    return jax.shard_map(
        on_device,
        mesh=mesh,
        in_specs=(
            P("slide", "seq", None),
            P(),
            P(),
            P(),
            P(),
            P(),
            P(),
            P(),
            P(),
            P("slide"),
            P("slide", None),
            P("slide"),
        ),
        out_specs=(P("slide", "seq", None), P("slide", None), P(), P()),
        check_vma=False,
    )
```

time: 509 us -> 128 us (0.25)
  blocking collectives: 396 us -> 0 us
  matrix products: 48.2 us -> 10.8 us
  starting transfers between devices: 2.13 us -> 39.3 us
  Pallas kernels: 0 us -> 32.7 us
  other arithmetic: 34.2 us -> 4.22 us
  waiting for transfers between devices: 0.01 us -> 16.6 us
    all_gather x4 -> x0, blocking collectives: 259 us -> none  [the longest x1 112 us: on_device(): lax.all_gather(far_value, 'seq', axis=1, tiled=True)]
    psum x1 -> x0, blocking collectives: 96.3 us -> none  [on_device(): pooled = lax.psum(local_sum, 'seq') / seq_length]
    unnamed x1 -> x0, blocking collectives: 40.3 us -> none
    dot_general x10 -> x4, matrix products: 47.2 us -> 9.78 us  [the longest x1 3.18 us: on_device(): jnp.dot(joined, w_out, preferred_element_type=jnp.float32)]
    all_to_all x0 -> x4, starting transfers between devices: none -> 36.6 us  [the longest x3 23.1 us: share_with_group(): return lax.all_to_all(copies, axis, 0, 0, tiled=True)]
    pallas_call x0 -> x3, Pallas kernels: none -> 32.7 us  [the longest x1 16.1 us: on_device(): pl.pallas_call(functools.partial(near_kernel, head_width=head_width, scor...]
    reduce_sum x4 -> x3, other arithmetic: 26 us -> 0.52 us  [the longest x1 0.44 us: on_device(): local_sum = jnp.sum(embedded, axis=0, dtype=jnp.float32, keepdims=True)]
    all_to_all x0 -> x4, waiting for transfers between devices: none -> 13.9 us  [the longest x3 13.9 us: share_with_group(): return lax.all_to_all(copies, axis, 0, 0, tiled=True)]
  transfers between devices with their start and end apart: 1 -> 6, of which waited for: 0 -> 3; matrix products, arithmetic and copies ran while one was open for 7% -> 5% of each run, Pallas kernels for 0% -> 26%
where the time goes in v1:
time: 128 us; the launch traced here: 127 us
  starting transfers between devices  39.3 us (31%)
  Pallas kernels  32.7 us (26%)
  local copies, waits for them, and re-layouts  17.8 us (14%)
  waiting for transfers between devices  16.6 us (13%)
  matrix products  10.8 us (8%)
  between operations  6.02 us (5%)
  other arithmetic  4.22 us (3%)
    all_to_all x3, starting transfers between devices, share_with_group(): return lax.all_to_all(copies, axis, 0, 0, tiled=True)  23.1 us
    pallas_call x1, Pallas kernels, on_device(): pl.pallas_call(functools.partial(near_kernel, head_width=head_width, scor...  16.1 us
    pallas_call x1, Pallas kernels, on_device(): pl.pallas_call(functools.partial(far_kernel, head_width=head_width), grid...  15.3 us
    all_to_all x3, waiting for transfers between devices, share_with_group(): return lax.all_to_all(copies, axis, 0, 0, tiled=True)  13.9 us
    all_to_all x1, starting transfers between devices, on_device(): lax.all_to_all(payload, 'seq', 0, 0, tiled=True)  13.5 us
    unnamed x35, local copies, waits for them, and re-layouts  13 us
    dot_general x1, matrix products, on_device(): jnp.dot(joined, w_out, preferred_element_type=jnp.float32)  3.18 us
    dot_general x1, matrix products, on_device(): jnp.dot(tiles.reshape(rows, in_width), w_embed, preferred_element_type=jn...  2.87 us
  transfers between devices with their start and end apart: 6, of which 3 were waited for; matrix products, arithmetic and copies ran while one was open for 5% of the time, Pallas kernels for 26%

profile of v1, /device:TPU:1, one launch (start us, length us, event | category | flops | bytes accessed | tf_op | source)
XLA Modules:
  0.0 127.4 jit_solution(2074077423221036939)
XLA Ops:
  0.7 1.6 %copy-done = bf16[1536,768]{1,0:T(8,128)(2,1)S(1)} copy-done((bf16[1536,768]{1,0:T(8,128)(2,1)S(1)}, bf16[1536,768]{1,0:T(8,128)(2,1)}, u32[]{:S(2)}) %copy-start) | copy-done | bytes 2359320
  2.3 2.9 %convert_reduce_fusion.1 = (f32[512]{0:T(512)S(1)}, bf16[512,768]{1,0:T(8,128)(2,1)S(1)}) fusion(bf16[1536,768]{1,0:T(8,128)(2,1)S(1)} %copy-done, bf16[1,512,1536]{2,1,0:T(8,128)(2,1)} %param.12), kind=kOutput, calls=%fused_computation.3 | convolution fusion | flops 1209138688 | bytes 4720640 | tf_op jit(solution)/shard_map/dot_general | solution.py:185
  6.4 2.2 %collective-permute-start = (bf16[512,768]{1,0:T(8,128)(2,1)S(1)}, bf16[512,768]{1,0:T(8,128)(2,1)}, u32[]{:S(2)}, u32[]{:S(2)}) collective-permute-start(bf16[512,768]{1,0:T(8,128)(2,1)S(1)} %fusion.4.own_ref.x_ref), channel_id=1, source_target_pairs={{0,8},{8,0},{16,24},{24,16},{32,40},{40,32},{48,56},{56,48},{64,72... | collective-permute-start | bytes 2359304 | tf_op jit(solution)/shard_map/ppermute | solution.py:55
  8.8 1.3 copy-done.1
  10.0 1.3 copy-done.3
  11.3 1.4 %far_rows.1 = bf16[2,16,768]{2,1,0:T(8,128)(2,1)S(1)} custom-call(bf16[512,768]{1,0:T(8,128)(2,1)S(1)} %fusion.4.own_ref.x_ref, bf16[768,768]{1,0:T(8,128)(2,1)S(1)} %copy-done.1, bf16[768,768]{1,0:T(8,128)(2,1)S(1)} %copy-done.3, f32[32,768]{1,0:T(8,128)S(1)} %fusion.18.chosen_ref), custom_call_target="tpu_custom_call" | custom-call | tf_op jit(solution)/shard_map/far_rows/pallas_call | solution.py:194
  12.7 1.0 broadcast_in_dim.23
  13.7 13.5 %all-to-all-start = ((bf16[32,16,768]{2,1,0:T(8,128)(2,1)}), bf16[32,16,768]{2,1,0:T(8,128)(2,1)}, u32[]{:S(2)}, u32[]{:S(2)}) async-start(bf16[32,16,768]{2,1,0:T(8,128)(2,1)} %bitcast.35), calls=%async_computation | async-start | bytes 1572864 | tf_op jit(solution)/shard_map/all_to_all | solution.py:202
  29.9 1.3 copy-done.2
  31.2 1.3 copy-done.4
  32.5 16.1 %near_attention.1 = (bf16[1024,384]{1,0:T(8,128)(2,1)S(1)}, f32[1024,384]{1,0:T(8,128)}, f32[1024,128]{1,0:T(8,128)S(1)}) custom-call(s32[1]{0:T(128)} %bitcast.1.part_ref, bf16[512,768]{1,0:T(8,128)(2,1)S(1)} %fusion.4.own_ref.x_ref, bf16[512,768]{1,0:T(8,128)(2,1)} %collective-permute-done.other_ref, bf16[768,768]{1,0:T(8,128)(2,1)S(1)} %copy-done.4, ...), custom_call_target="tpu_custom_call" | custom-call | flops 12000000000 | bytes 8000000 | tf_op jit(solution)/shard_map/near_attention/pallas_call | solution.py:206
  48.5 0.9 copy-done.6
  49.4 0.8 copy-done.8
  50.2 0.6 broadcast_in_dim.29
  50.8 6.5 %all-to-all-start.3 = ((f32[8,1,896]{2,1,0:T(1,128)}), f32[8,1,896]{2,1,0:T(1,128)S(1)}, u32[]{:S(2)}, u32[]{:S(2)}) async-start(f32[8,1,896]{2,1,0:T(1,128)} %broadcast_in_dim.29), calls=%async_computation.3 | async-start | bytes 57344 | tf_op jit(solution)/shard_map/all_to_all | solution.py:51
  57.3 1.4 %copy-done.5 = f32[1024,384]{1,0:T(8,128)S(1)} copy-done((f32[1024,384]{1,0:T(8,128)S(1)}, f32[1024,384]{1,0:T(8,128)}, u32[]{:S(2)}) %copy-start.5) | copy-done | bytes 1572888
  58.7 1.1 copy-done.7
  59.9 1.0 copy-done.9
  60.9 15.3 %far_attention.1 = (bf16[1024,384]{1,0:T(8,128)(2,1)S(1)}, f32[1,384]{1,0:T(1,128)S(1)}) custom-call(bf16[1024,384]{1,0:T(8,128)(2,1)S(1)} %copy-done.7, bf16[512,768]{1,0:T(8,128)(2,1)} %bitcast.3.far_ref, f32[1024,384]{1,0:T(8,128)S(1)} %copy-done.5, f32[1024,128]{1,0:T(8,128)S(1)} %copy-done.9), custom_call_target="tpu_custom_call" | custom-call | flops 6000000000 | bytes 6000000 | tf_op jit(solution)/shard_map/far_attention/pallas_call | solution.py:234
  76.2 0.7 broadcast_in_dim.26
  76.9 10.0 %all-to-all-start.1 = ((f32[32,1,1152]{2,1,0:T(1,128)}), f32[32,1,1152]{2,1,0:T(1,128)S(1)}, u32[]{:S(2)}, u32[]{:S(2)}) async-start(f32[32,1,1152]{2,1,0:T(1,128)} %broadcast_in_dim.26), calls=%async_computation.1 | async-start | bytes 294912 | tf_op jit(solution)/shard_map/all_to_all | solution.py:51
  87.8 10.7 %all-to-all-done.1 = f32[32,1,1152]{2,1,0:T(1,128)S(1)} async-done(((f32[32,1,1152]{2,1,0:T(1,128)}), f32[32,1,1152]{2,1,0:T(1,128)S(1)}, u32[]{:S(2)}, u32[]{:S(2)}) %all-to-all-start.1) | async-done | bytes 147488 | tf_op jit(solution)/shard_map/all_to_all | solution.py:51
  99.1 1.9 %convolution_reduce_fusion.1 = f32[768]{0:T(1024)S(1)} fusion(f32[768,1]{0,1:T(1,128)S(1)} %bitcast.38, bf16[768,768]{1,0:T(8,128)(2,1)} %param.18), kind=kOutput, calls=%fused_computation.16 | convolution fusion | flops 7077888 | bytes 1185792 | tf_op jit(solution)/shard_map/dot_general | solution.py:264
  101.0 1.9 %convolution_reduce_fusion = f32[768]{0:T(1024)S(1)} fusion(f32[768,1]{0,1:T(1,128)S(1)} %reshape.146, bf16[768,768]{1,0:T(8,128)(2,1)} %param.19), kind=kOutput, calls=%fused_computation.15 | convolution fusion | flops 7077888 | bytes 1185792 | tf_op jit(solution)/shard_map/dot_general | solution.py:269
  104.1 0.6 broadcast_in_dim.27
  104.7 6.6 %all-to-all-start.2 = ((f32[8,1,768]{2,1,0:T(1,128)}), f32[8,1,768]{2,1,0:T(1,128)}, u32[]{:S(2)}, u32[]{:S(2)}) async-start(f32[8,1,768]{2,1,0:T(1,128)} %broadcast_in_dim.27), calls=%async_computation.2 | async-start | bytes 49152 | tf_op jit(solution)/shard_map/all_to_all | solution.py:51
  111.4 0.8 fusion.31
  113.3 3.2 %all-to-all-done.2 = f32[8,1,768]{2,1,0:T(1,128)} async-done(((f32[8,1,768]{2,1,0:T(1,128)}), f32[8,1,768]{2,1,0:T(1,128)}, u32[]{:S(2)}, u32[]{:S(2)}) %all-to-all-start.2) | async-done | bytes 24608 | tf_op jit(solution)/shard_map/all_to_all | solution.py:51
  116.4 1.0 fusion.30
  117.9 0.7 fusion.28
  120.4 2.7 %collective-permute-done.1 = bf16[512,384]{1,0:T(8,128)(2,1)S(1)} collective-permute-done((bf16[512,384]{1,0:T(8,128)(2,1)}, bf16[512,384]{1,0:T(8,128)(2,1)S(1)}, u32[]{:S(2)}, u32[]{:S(2)}) %collective-permute-start.1) | collective-permute-done | bytes 393248 | tf_op jit(solution)/shard_map/ppermute | solution.py:55
  123.1 3.2 %fusion.11 = bf16[1,512,768]{2,1,0:T(8,128)(2,1)} fusion(bf16[768,768]{1,0:T(8,128)(2,1)} %param.18, bf16[512,768]{1,0:T(8,128)(2,1)} %copy-done.10, bf16[512,384]{1,0:T(8,128)(2,1)S(1)} %get-tuple-element.27, bf16[512,384]{1,0:T(8,128)(2,1)S(1)} %collective-permute-done.1, pred[]{:T(512)S(6)} %eq.40), kind=kOutput, calls=%fused_computation.13 | convolution fusion | flops 608698368 | bytes 3538945 | tf_op jit(solution)/shard_map/dot_general | solution.py:279
  (56 shorter events, 6.1 us)
Async XLA Ops:
  0.6 1.7 %copy-start = (bf16[1536,768]{1,0:T(8,128)(2,1)S(1)}, bf16[1536,768]{1,0:T(8,128)(2,1)}, u32[]{:S(2)}) copy-start(bf16[1536,768]{1,0:T(8,128)(2,1)} %param.13) | copy-start | bytes 7077892
  0.6 5.4 %copy-start.14 = (f32[768]{0:T(1024)S(1)}, f32[768]{0:T(1024)}, u32[]{:S(2)}) copy-start(f32[768]{0:T(1024)} %param.14) | copy-start | bytes 9220
  5.2 0.9 copy-start.10
  5.2 3.4 %copy-start.15 = (s32[16]{0:T(128)S(1)}, s32[16]{0:T(128)}, u32[]{:S(2)}) copy-start(s32[16]{0:T(128)} %param.20) | copy-start | bytes 196
  6.4 23.6 %collective-permute-start = (bf16[512,768]{1,0:T(8,128)(2,1)S(1)}, bf16[512,768]{1,0:T(8,128)(2,1)}, u32[]{:S(2)}, u32[]{:S(2)}) collective-permute-start(bf16[512,768]{1,0:T(8,128)(2,1)S(1)} %fusion.4.own_ref.x_ref), channel_id=1, source_target_pairs={{0,8},{8,0},{16,24},{24,16},{32,40},{40,32},{48,56},{56,48},{64,72... | collective-permute-start | bytes 2359304 | tf_op jit(solution)/shard_map/ppermute | solution.py:55
  8.8 1.3 copy-start.1
  10.0 1.3 copy-start.3
  12.7 14.5 %copy-start.13 = (bf16[1,768]{1,0:T(2,128)(2,1)S(1)}, bf16[1,768]{1,0:T(2,128)(2,1)}, u32[]{:S(2)}) copy-start(bf16[1,768]{1,0:T(2,128)(2,1)} %param.22) | copy-start | bytes 4612
  13.7 36.5 %all-to-all-start = ((bf16[32,16,768]{2,1,0:T(8,128)(2,1)}), bf16[32,16,768]{2,1,0:T(8,128)(2,1)}, u32[]{:S(2)}, u32[]{:S(2)}) async-start(bf16[32,16,768]{2,1,0:T(8,128)(2,1)} %bitcast.35), calls=%async_computation | async-start | bytes 1572864 | tf_op jit(solution)/shard_map/all_to_all | solution.py:202
  29.9 1.3 copy-start.2
  31.2 1.3 copy-start.4
  48.5 0.9 copy-start.6
  49.4 0.8 copy-start.8
  50.8 25.4 %all-to-all-start.3 = ((f32[8,1,896]{2,1,0:T(1,128)}), f32[8,1,896]{2,1,0:T(1,128)S(1)}, u32[]{:S(2)}, u32[]{:S(2)}) async-start(f32[8,1,896]{2,1,0:T(1,128)} %broadcast_in_dim.29), calls=%async_computation.3 | async-start | bytes 57344 | tf_op jit(solution)/shard_map/all_to_all | solution.py:51
  57.3 1.4 %copy-start.5 = (f32[1024,384]{1,0:T(8,128)S(1)}, f32[1024,384]{1,0:T(8,128)}, u32[]{:S(2)}) copy-start(f32[1024,384]{1,0:T(8,128)} %get-tuple-element.10.near_ref) | copy-start | bytes 4718596
  58.7 1.1 copy-start.7
  59.8 1.0 copy-start.9
  76.9 21.6 %all-to-all-start.1 = ((f32[32,1,1152]{2,1,0:T(1,128)}), f32[32,1,1152]{2,1,0:T(1,128)S(1)}, u32[]{:S(2)}, u32[]{:S(2)}) async-start(f32[32,1,1152]{2,1,0:T(1,128)} %broadcast_in_dim.26), calls=%async_computation.1 | async-start | bytes 294912 | tf_op jit(solution)/shard_map/all_to_all | solution.py:51
  87.0 0.6 copy-start.11
  104.7 11.7 %all-to-all-start.2 = ((f32[8,1,768]{2,1,0:T(1,128)}), f32[8,1,768]{2,1,0:T(1,128)}, u32[]{:S(2)}, u32[]{:S(2)}) async-start(f32[8,1,768]{2,1,0:T(1,128)} %broadcast_in_dim.27), calls=%async_computation.2 | async-start | bytes 49152 | tf_op jit(solution)/shard_map/all_to_all | solution.py:51
  112.2 11.0 %collective-permute-start.1 = (bf16[512,384]{1,0:T(8,128)(2,1)}, bf16[512,384]{1,0:T(8,128)(2,1)S(1)}, u32[]{:S(2)}, u32[]{:S(2)}) collective-permute-start(bf16[512,384]{1,0:T(8,128)(2,1)} %get-tuple-element.26), channel_id=1, source_target_pairs={{0,8},{8,0},{16,24},{24,16},{32,40},{40,32},{48,56},{56,48},{64,72... | collective-permute-start | bytes 1179656 | tf_op jit(solution)/shard_map/ppermute | solution.py:55
  117.4 8.9 %copy-start.12 = (f32[8,8]{1,0:T(8,128)}, f32[8,8]{1,0:T(8,128)S(1)}, u32[]{:S(2)}) copy-start(f32[8,8]{1,0:T(8,128)S(1)} %get-tuple-element.30) | copy-start | bytes 772

commit v2 on v1

v2 whole, which is shorter than its diff:
```python
import functools
import math

import jax
import jax.numpy as jnp
from jax import lax
from jax.experimental import pallas as pl
from jax.experimental.pallas import tpu as pltpu
from jax.sharding import Mesh, PartitionSpec as P

RATE = 32
LANES = 128
PACK = (8, 256)
SOFTMAX_TEMPER = 1.0 / 0.07
NORM_EPS = 1e-05
NT = (((1,), (1,)), ((), ()))
NN = (((1,), (0,)), ((), ()))
VMEM_LIMIT = 56 << 20
SEQ_AXES = ("x", "z_hi", "y")
F32 = jnp.float32
BF16 = jnp.bfloat16


def swap_with(x, axis):
    return lax.ppermute(x, axis, [(i, i ^ 1) for i in range(lax.axis_size(axis))])


def head_window(head, width):
    first = head * width // LANES * LANES
    last = -(-(head * width + width) // LANES) * LANES
    return first, last, head * width - first


def in_head_lanes(head, width):
    first, last, offset = head_window(head, width)
    lane = lax.broadcasted_iota(jnp.int32, (1, last - first), 1)
    return (lane >= offset) & (lane < offset + width)


def attend(queries, keys, values, head_width, mixed_ref, lse_ref, rows):
    for head in range(queries.shape[1] // head_width):
        first, last, _ = head_window(head, head_width)
        mine = in_head_lanes(head, head_width)
        masked = jnp.where(mine, queries[:, first:last], jnp.zeros((), queries.dtype))
        scores = lax.dot_general(masked, keys[:, first:last], NT, preferred_element_type=F32)
        peak = jnp.max(scores, axis=1, keepdims=True)
        weights = jnp.exp(scores - peak)
        total = jnp.sum(weights, axis=1, keepdims=True)
        mixed = lax.dot_general(
            weights.astype(BF16), values[:, first:last], NN, preferred_element_type=F32
        )
        mixed = mixed * (1.0 / total)
        lse = jnp.broadcast_to(peak + jnp.log(total), mixed.shape)
        if head > 0:
            mixed = jnp.where(mine, mixed, mixed_ref[rows, first:last])
            lse = jnp.where(mine, lse, lse_ref[rows, first:last])
        mixed_ref[rows, first:last] = mixed
        lse_ref[rows, first:last] = lse


def embed_kernel(x_ref, w_ref, gain_ref, embedded_ref, normed_ref, sum_ref, acc_scr):
    step = pl.program_id(0)

    @pl.when(step == 0)
    def _():
        acc_scr[...] = jnp.dot(x_ref[...], w_ref[...], preferred_element_type=F32)

    @pl.when(step > 0)
    def _():
        acc_scr[...] += jnp.dot(x_ref[...], w_ref[...], preferred_element_type=F32)

    @pl.when(step == pl.num_programs(0) - 1)
    def _():
        embedded = acc_scr[...].astype(BF16)
        embedded_ref[...] = embedded
        floats = embedded.astype(F32)
        centred = floats - jnp.mean(floats, axis=1, keepdims=True)
        spread = jnp.mean(centred * centred, axis=1, keepdims=True)
        normed = centred * lax.rsqrt(spread + NORM_EPS) * gain_ref[...]
        normed_ref[...] = normed.astype(BF16)
        sum_ref[...] = jnp.sum(floats, axis=0, keepdims=True)


def own_rows_kernel(part_ref, x_ref, wk_ref, wv_ref, offset_ref, far_ref, k_ref, v_ref):
    rows, width = x_ref.shape
    half = width // 2
    phase = lax.broadcasted_iota(jnp.int32, (RATE, width), 0)
    chosen = jnp.where(phase == offset_ref[...], 1.0, 0.0)
    upper = part_ref[0] == 1
    for place, (w_ref, half_ref) in enumerate(((wk_ref, k_ref), (wv_ref, v_ref))):
        full = jnp.dot(x_ref[...], w_ref[...], preferred_element_type=F32)
        half_ref[...] = jnp.where(upper, full[:, half:], full[:, :half]).astype(BF16)
        grouped = full.reshape(rows // RATE, RATE, width) * chosen[None]
        picked = jnp.sum(grouped, axis=1).astype(BF16)
        for part in range(2):
            far_ref[part, :, place * half : (place + 1) * half] = picked[
                :, part * half : (part + 1) * half
            ]


def near_kernel(part_ref, own_ref, other_ref, k_ref, v_ref, wq_ref, wk_ref, wv_ref,
                q_ref, mixed_ref, lse_ref, k_scr, v_scr, *, head_width, score_scale):
    step = pl.program_id(0)
    rows = own_ref.shape[0]

    @pl.when(step == 0)
    def _():
        for place, x_ref in enumerate((own_ref, other_ref)):
            q = jnp.dot(x_ref[...], wq_ref[...], preferred_element_type=F32) * score_scale
            q_ref[place * rows : (place + 1) * rows, :] = q.astype(BF16)
        for scr, own_half_ref, w_ref in ((k_scr, k_ref, wk_ref), (v_scr, v_ref, wv_ref)):
            scr[:rows, :] = own_half_ref[...]
            other = jnp.dot(other_ref[...], w_ref[...], preferred_element_type=F32)
            scr[rows:, :] = other.astype(BF16)

    queries = q_ref[pl.ds(pl.multiple_of(step * rows, rows), rows), :]
    attend(queries, k_scr[...], v_scr[...], head_width, mixed_ref, lse_ref, slice(None))


def far_kernel(q_ref, far_ref, near_ref, near_lse_ref, embedded_sum_ref, out_ref, pack_ref,
               mixed_scr, lse_scr, sum_scr, *, head_width):
    step = pl.program_id(0)
    half = q_ref.shape[1]
    attend(
        q_ref[...], far_ref[:, :half], far_ref[:, half:], head_width, mixed_scr, lse_scr, slice(None)
    )
    near_share = 1.0 / (1.0 + jnp.exp(lse_scr[...] - near_lse_ref[...]))
    far_mixed = mixed_scr[...]
    attended = far_mixed + (near_ref[...] - far_mixed) * near_share
    out_ref[...] = attended.astype(BF16)

    @pl.when(step == 0)
    def _():
        sum_scr[...] = jnp.zeros_like(sum_scr)

    sum_scr[...] += jnp.sum(attended, axis=0, keepdims=True)

    @pl.when(step == pl.num_programs(0) - 1)
    def _():
        pad = jnp.zeros((1, pack_ref.shape[1] * pack_ref.shape[2] - 3 * half), F32)
        packed = pack_row((embedded_sum_ref[...], sum_scr[...], pad))
        pack_ref[...] = jnp.broadcast_to(packed[None], pack_ref.shape)


def pack_row(pieces):
    flat = jnp.concatenate(pieces, axis=1)
    rows, lanes = PACK
    return jnp.concatenate([flat[:, r * lanes : (r + 1) * lanes] for r in range(rows)], axis=0)


def exact_row_times(row, matrix):
    top = row.astype(BF16).astype(F32)
    middle = (row - top).astype(BF16).astype(F32)
    low = row - top - middle
    parts = jnp.concatenate((top, middle, low, jnp.zeros((13, row.shape[1]), F32)), axis=0)
    product = jnp.dot(parts.astype(BF16), matrix, preferred_element_type=F32)
    return jnp.sum(product, axis=0, keepdims=True)


def unit_row(row):
    return row * lax.rsqrt(jnp.sum(row * row, axis=1, keepdims=True) + 1e-06)


def pooled_kernel(slide_code_ref, report_code_ref, sums_ref, w_out_ref, w_head_ref, report_ref,
                  unit_ref, pack_ref, *, length):
    peers = sums_ref.shape[0]
    width = w_out_ref.shape[0]
    half = width // 2
    lanes = PACK[1]
    even = sums_ref[0]
    odd = sums_ref[1]
    for peer in range(2, peers, 2):
        even = even + sums_ref[peer]
        odd = odd + sums_ref[peer + 1]

    def flat(packed):
        return jnp.concatenate([packed[r : r + 1, :] for r in range(PACK[0])], axis=1)

    even, odd = flat(even), flat(odd)
    embedded_sum = even[:, :width] + odd[:, :width]
    attended_sum = jnp.concatenate(
        (even[:, width : width + half], odd[:, width : width + half]), axis=1
    )
    pooled = (embedded_sum + exact_row_times(attended_sum, w_out_ref[...])) * (1.0 / length)
    unit = unit_row(exact_row_times(pooled, w_head_ref[...]))
    unit_ref[...] = unit
    lane = lax.broadcasted_iota(jnp.int32, (1, 2 * lanes), 1)
    codes = jnp.where(
        lane == 0,
        slide_code_ref[0].astype(F32),
        jnp.where(lane == 1, report_code_ref[0].astype(F32), 0.0),
    )
    packed = pack_row((unit, unit_row(report_ref[...].astype(F32)), codes))
    pack_ref[...] = jnp.broadcast_to(packed[None], pack_ref.shape)


def contrast_kernel(all_ref, logits_ref, loss_ref):
    count = all_ref.shape[0]
    lanes = PACK[1]
    logits = jnp.zeros((count, count), F32)
    parts = 768 // lanes
    for r in range(parts):
        logits += lax.dot_general(
            all_ref[:, r, :], all_ref[:, parts + r, :], NT,
            precision=lax.Precision.HIGHEST, preferred_element_type=F32,
        )
    logits = logits * SOFTMAX_TEMPER
    logits_ref[...] = logits
    codes = all_ref[:, 2 * parts, :]
    down = lax.broadcasted_iota(jnp.int32, (count, count), 0)
    across = lax.broadcasted_iota(jnp.int32, (count, count), 1)
    diagonal = down == across
    slide_codes = codes[:, 0:1]
    report_codes = jnp.sum(jnp.where(diagonal, codes[:, 1:2], 0.0), axis=0, keepdims=True)
    positive = jnp.where((slide_codes == report_codes) | diagonal, 1.0, 0.0)

    def terms(axis):
        peak = jnp.max(logits, axis=axis, keepdims=True)
        lse = peak + jnp.log(jnp.sum(jnp.exp(logits - peak), axis=axis, keepdims=True))
        picked = jnp.sum(positive * (logits - lse), axis=axis, keepdims=True)
        return -picked / jnp.sum(positive, axis=axis, keepdims=True)

    both = jnp.sum(terms(1), axis=0, keepdims=True) + jnp.sum(terms(0), axis=1, keepdims=True)
    loss_ref[...] = both * (0.5 / count)


def on_device(
    tiles,
    w_embed,
    attn_gain,
    w_query,
    w_key,
    w_value,
    w_out,
    w_head,
    head_offset,
    slide_code,
    report_emb,
    report_code,
):
    _, rows, in_width = tiles.shape
    width = w_embed.shape[1]
    half = width // 2
    heads_count = head_offset.shape[0]
    head_width = width // heads_count
    ranks = lax.axis_size(SEQ_AXES)
    plane = lax.axis_size(("x", "y"))
    score_scale = 1.0 / math.sqrt(head_width)
    part = lax.axis_index("y") % 2
    parts = part.reshape(1)
    params = pltpu.CompilerParams(vmem_limit_bytes=VMEM_LIMIT)

    steps = 3
    depth = in_width // steps
    embedded, normed, embedded_sum = pl.pallas_call(
        embed_kernel,
        grid=(steps,),
        in_specs=[
            pl.BlockSpec((rows, depth), lambda i: (0, i)),
            pl.BlockSpec((depth, width), lambda i: (i, 0)),
            pl.BlockSpec((1, width), lambda i: (0, 0)),
        ],
        out_specs=[
            pl.BlockSpec((rows, width), lambda i: (0, 0)),
            pl.BlockSpec((rows, width), lambda i: (0, 0)),
            pl.BlockSpec((1, width), lambda i: (0, 0)),
        ],
        out_shape=[
            jax.ShapeDtypeStruct((rows, width), BF16),
            jax.ShapeDtypeStruct((rows, width), BF16),
            jax.ShapeDtypeStruct((1, width), F32),
        ],
        scratch_shapes=[pltpu.VMEM((rows, width), F32)],
        compiler_params=params,
        name="embed",
    )(tiles.reshape(rows, in_width), w_embed, attn_gain.reshape(1, width))
    other_normed = swap_with(normed, "y")

    lane_offset = jnp.broadcast_to(head_offset[:, None], (heads_count, head_width)).reshape(1, width)
    far_rows = rows // RATE
    smem = pl.BlockSpec(memory_space=pltpu.SMEM)
    vmem = pl.BlockSpec(memory_space=pltpu.VMEM)
    far_own, keys_own, values_own = pl.pallas_call(
        own_rows_kernel,
        in_specs=[smem, vmem, vmem, vmem, vmem],
        out_shape=[
            jax.ShapeDtypeStruct((2, far_rows, width), BF16),
            jax.ShapeDtypeStruct((rows, half), BF16),
            jax.ShapeDtypeStruct((rows, half), BF16),
        ],
        compiler_params=params,
        name="own_rows",
    )(parts, normed, w_key, w_value, lane_offset)
    far_pair = jnp.stack((far_own, swap_with(far_own, "z_hi")), axis=1)
    far_pair = far_pair.reshape(2, 2 * far_rows, width)
    payload = jnp.broadcast_to(far_pair[None], (plane // 2, 2, 2 * far_rows, width))
    payload = payload.reshape(plane, 2 * far_rows, width)
    far = lax.all_to_all(payload, ("x", "y"), 0, 0, tiled=True).reshape(ranks * far_rows, width)

    weight_spec = pl.BlockSpec((width, half), lambda i, p: (0, p[0]))
    whole = pl.BlockSpec((rows, width), lambda i, p: (0, 0))
    whole_half = pl.BlockSpec((rows, half), lambda i, p: (0, 0))
    row_block = pl.BlockSpec((rows, half), lambda i, p: (i, 0))
    queries, near_mixed, near_lse = pl.pallas_call(
        functools.partial(near_kernel, head_width=head_width, score_scale=score_scale),
        grid_spec=pltpu.PrefetchScalarGridSpec(
            num_scalar_prefetch=1,
            grid=(2,),
            in_specs=[whole, whole, whole_half, whole_half, weight_spec, weight_spec, weight_spec],
            out_specs=[pl.BlockSpec((2 * rows, half), lambda i, p: (0, 0)), row_block, row_block],
            scratch_shapes=[
                pltpu.VMEM((2 * rows, half), BF16),
                pltpu.VMEM((2 * rows, half), BF16),
            ],
        ),
        out_shape=[
            jax.ShapeDtypeStruct((2 * rows, half), BF16),
            jax.ShapeDtypeStruct((2 * rows, half), F32),
            jax.ShapeDtypeStruct((2 * rows, half), F32),
        ],
        compiler_params=params,
        cost_estimate=pl.CostEstimate(
            flops=12_000_000_000, bytes_accessed=8_000_000, transcendentals=8_000_000
        ),
        name="near_attention",
    )(parts, normed, other_normed, keys_own, values_own, w_query, w_key, w_value)

    row_block = pl.BlockSpec((rows, half), lambda i: (i, 0))
    attended, sums = pl.pallas_call(
        functools.partial(far_kernel, head_width=head_width),
        grid=(2,),
        in_specs=[
            row_block,
            pl.BlockSpec((ranks * far_rows, width), lambda i: (0, 0)),
            row_block,
            row_block,
            pl.BlockSpec((1, width), lambda i: (0, 0)),
        ],
        out_specs=[row_block, pl.BlockSpec((ranks,) + PACK, lambda i: (0, 0, 0))],
        out_shape=[
            jax.ShapeDtypeStruct((2 * rows, half), BF16),
            jax.ShapeDtypeStruct((ranks,) + PACK, F32),
        ],
        scratch_shapes=[
            pltpu.VMEM((rows, half), F32),
            pltpu.VMEM((rows, half), F32),
            pltpu.VMEM((1, half), F32),
        ],
        compiler_params=params,
        cost_estimate=pl.CostEstimate(
            flops=6_000_000_000, bytes_accessed=6_000_000, transcendentals=4_000_000
        ),
        name="far_attention",
    )(queries, far, near_mixed, near_lse, embedded_sum)

    own_half, lent_half = attended[:rows], attended[rows:]
    other_half = swap_with(lent_half, "y")
    joined = jnp.where(
        part == 1,
        jnp.concatenate((other_half, own_half), axis=1),
        jnp.concatenate((own_half, other_half), axis=1),
    )
    encoded = embedded.astype(F32) + jnp.dot(joined, w_out, preferred_element_type=F32)
    encoded = encoded.astype(BF16).reshape(1, rows, width)

    sums = lax.all_to_all(sums, SEQ_AXES, 0, 0, tiled=True)
    sums, encoded = lax.optimization_barrier((sums, encoded))
    slides = lax.axis_size("slide")
    slide_unit_vectors, packed = pl.pallas_call(
        functools.partial(pooled_kernel, length=rows * ranks),
        in_specs=[smem, smem, vmem, vmem, vmem, vmem],
        out_shape=[
            jax.ShapeDtypeStruct((1, width), F32),
            jax.ShapeDtypeStruct((slides,) + PACK, F32),
        ],
        compiler_params=params,
        name="pooled",
    )(slide_code, report_code, sums, w_out, w_head, report_emb)
    everyone = lax.all_to_all(packed, "slide", 0, 0, tiled=True)
    logits, loss = pl.pallas_call(
        contrast_kernel,
        in_specs=[vmem],
        out_shape=[
            jax.ShapeDtypeStruct((slides, slides), F32),
            jax.ShapeDtypeStruct((1, 1), F32),
        ],
        compiler_params=params,
        name="contrast",
    )(everyone)
    return (encoded, slide_unit_vectors, logits, loss.reshape(()))


def solution(mesh):
    split = Mesh(mesh.devices.reshape(4, 2, 4, 8), SEQ_AXES + ("slide",))
    rows = P("slide", SEQ_AXES, None)
    return jax.shard_map(
        on_device,
        mesh=split,
        in_specs=(
            rows,
            P(),
            P(),
            P(),
            P(),
            P(),
            P(),
            P(),
            P(),
            P("slide"),
            P("slide", None),
            P("slide"),
        ),
        out_specs=(rows, P("slide", None), P(), P()),
        check_vma=False,
    )
```

time: 128 us -> 107 us (0.84)
  blocking collectives: 0 us -> 14 us
  local copies, waits for them, and re-layouts: 17.8 us -> 6.8 us
  starting transfers between devices: 39.3 us -> 28.5 us
  matrix products: 10.8 us -> 1.67 us
  Pallas kernels: 32.7 us -> 41.5 us
  waiting for transfers between devices: 16.6 us -> 10.8 us
  between operations: 6.02 us -> 2.03 us
  other arithmetic: 4.22 us -> 0.81 us
    all_to_all x4 -> x2, starting transfers between devices: 36.6 us -> 18 us  [the longest x1 11.6 us: on_device(): sums = lax.all_to_all(sums, SEQ_AXES, 0, 0, tiled=True)]
    all_to_all x0 -> x1, blocking collectives: none -> 14 us  [on_device(): everyone = lax.all_to_all(packed, 'slide', 0, 0, tiled=True)]
    pallas_call x1 -> x4, Pallas kernels: 1.4 us -> 14.4 us  [the longest x1 5.51 us: on_device(): pl.pallas_call(embed_kernel, grid=(steps,), in_specs=[pl.BlockSpec((rows,...]
    unnamed x35 -> x12, local copies, waits for them, and re-layouts: 13 us -> 2.47 us
    dot_general x5 -> x1, matrix products: 10.8 us -> 1.67 us  [on_device(): jnp.dot(joined, w_out, preferred_element_type=F32)]
    ppermute x2 -> x3, starting transfers between devices: 2.71 us -> 10.5 us  [swap_with(): lax.ppermute(x, axis, [(i, i ^ 1) for i in range(lax.axis_size(axis))])]
    pallas_call x1, Pallas kernels: 15.3 us -> 10 us  [on_device(): pl.pallas_call(functools.partial(far_kernel, head_width=head_width), grid...]
    all_to_all x4 -> x2, waiting for transfers between devices: 13.9 us -> 9.09 us  [the longest x1 9.09 us: on_device(): sums = lax.all_to_all(sums, SEQ_AXES, 0, 0, tiled=True)]
  transfers between devices with their start and end apart: 6 -> 5, of which waited for: 3 -> 2; matrix products, arithmetic and copies ran while one was open for 5% -> 4% of each run, Pallas kernels for 26% -> 20%
where the time goes in v2:
time: 107 us; the launch traced here: 106 us
  Pallas kernels  41.5 us (39%)
  starting transfers between devices  28.5 us (27%)
  blocking collectives  14 us (13%)
  waiting for transfers between devices  10.8 us (10%)
  local copies, waits for them, and re-layouts  6.8 us (6%)
  between operations  2.03 us (2%)
  matrix products  1.67 us (2%)
    pallas_call x1, Pallas kernels, on_device(): pl.pallas_call(functools.partial(near_kernel, head_width=head_width, scor...  17.1 us
    all_to_all x1, blocking collectives, on_device(): everyone = lax.all_to_all(packed, 'slide', 0, 0, tiled=True)  14 us
    all_to_all x1, starting transfers between devices, on_device(): sums = lax.all_to_all(sums, SEQ_AXES, 0, 0, tiled=True)  11.6 us
    ppermute x3, starting transfers between devices, swap_with(): lax.ppermute(x, axis, [(i, i ^ 1) for i in range(lax.axis_size(axis))])  10.5 us
    pallas_call x1, Pallas kernels, on_device(): pl.pallas_call(functools.partial(far_kernel, head_width=head_width), grid...  10 us
    all_to_all x1, waiting for transfers between devices, on_device(): sums = lax.all_to_all(sums, SEQ_AXES, 0, 0, tiled=True)  9.09 us
    all_to_all x1, starting transfers between devices, on_device(): lax.all_to_all(payload, ('x', 'y'), 0, 0, tiled=True)  6.47 us
    pallas_call x1, Pallas kernels, on_device(): pl.pallas_call(embed_kernel, grid=(steps,), in_specs=[pl.BlockSpec((rows,...  5.51 us
  transfers between devices with their start and end apart: 5, of which 2 were waited for; matrix products, arithmetic and copies ran while one was open for 4% of the time, Pallas kernels for 20%

profile of v2, /device:TPU:1, one launch (start us, length us, event | category | flops | bytes accessed | tf_op | source)
XLA Modules:
  0.0 106.0 jit_solution(9194963978831433852)
XLA Ops:
  0.6 1.3 %reshape.36.gain_ref = f32[1,768]{1,0:T(1,128)} reshape(f32[768]{0:T(1024)} %param.14) | data formatting | bytes 6144 | tf_op jit(solution)/shard_map/reshape | solution.py:276
  1.9 5.5 %embed.1 = (bf16[512,768]{1,0:T(8,128)(2,1)}, bf16[512,768]{1,0:T(8,128)(2,1)}, f32[1,768]{1,0:T(1,128)}) custom-call(bf16[512,1536]{1,0:T(8,128)(2,1)} %bitcast.11, bf16[1536,768]{1,0:T(8,128)(2,1)} %w_ref.1, f32[1,768]{1,0:T(1,128)} %reshape.36.gain_ref), custom_call_target="tpu_custom_call" | custom-call | tf_op jit(solution)/shard_map/embed/pallas_call | solution.py:255
  7.4 2.1 %collective-permute-start = (bf16[512,768]{1,0:T(8,128)(2,1)}, bf16[512,768]{1,0:T(8,128)(2,1)S(1)}, u32[]{:S(2)}, u32[]{:S(2)}) collective-permute-start(bf16[512,768]{1,0:T(8,128)(2,1)} %get-tuple-element.21.x_ref.own_ref), channel_id=1, source_target_pairs={{0,8},{8,0},{16,24},{24,16},{1,9},{9,1},{17,25},{25,17},{2,10},{10... | collective-permute-start | bytes 2359304 | tf_op jit(solution)/shard_map/ppermute | solution.py:25
  9.5 0.0 copy-done.3
  9.5 0.1 broadcast_in_dim.6
  9.6 0.7 reshape.37.offset_ref
  10.3 4.1 %own_rows.1 = (bf16[2,16,768]{2,1,0:T(8,128)(2,1)}, bf16[512,384]{1,0:T(8,128)(2,1)}, bf16[512,384]{1,0:T(8,128)(2,1)}) custom-call(s32[1]{0:T(128)} %bitcast.part_ref, bf16[512,768]{1,0:T(8,128)(2,1)} %get-tuple-element.21.x_ref.own_ref, bf16[768,768]{1,0:T(8,128)(2,1)} %wk_ref.3, bf16[768,768]{1,0:T(8,128)(2,1)} %wv_ref.3, s32[1,768]{1,0:T(1,128)} %reshape.37.offset_ref), custom_call_target="tpu_custom_call" | custom-call | tf_op jit(solution)/shard_map/own_rows/pallas_call | solution.py:283
  14.4 6.9 %collective-permute-start.1 = (bf16[2,16,768]{2,1,0:T(8,128)(2,1)}, bf16[2,16,768]{2,1,0:T(8,128)(2,1)S(1)}, u32[]{:S(2)}, u32[]{:S(2)}) collective-permute-start(bf16[2,16,768]{2,1,0:T(8,128)(2,1)} %get-tuple-element.25), channel_id=1, source_target_pairs={{0,32},{32,0},{1,33},{33,1},{2,34},{34,2},{3,35},{35,3},{4,36},{36... | collective-permute-start | bytes 147464 | tf_op jit(solution)/shard_map/ppermute | solution.py:25
  21.3 1.7 %collective-permute-done.1 = bf16[2,16,768]{2,1,0:T(8,128)(2,1)S(1)} collective-permute-done((bf16[2,16,768]{2,1,0:T(8,128)(2,1)}, bf16[2,16,768]{2,1,0:T(8,128)(2,1)S(1)}, u32[]{:S(2)}, u32[]{:S(2)}) %collective-permute-start.1) | collective-permute-done | bytes 49184 | tf_op jit(solution)/shard_map/ppermute | solution.py:25
  23.0 0.8 pad_maximum_fusion
  23.8 1.0 broadcast_in_dim.15
  24.8 6.5 %all-to-all-start = ((bf16[16,32,768]{2,1,0:T(8,128)(2,1)}), bf16[16,32,768]{2,1,0:T(8,128)(2,1)S(1)}, u32[]{:S(2)}, u32[]{:S(2)}) async-start(bf16[16,32,768]{2,1,0:T(8,128)(2,1)} %bitcast.5), calls=%async_computation | async-start | bytes 1572864 | tf_op jit(solution)/shard_map/all_to_all | solution.py:298
  31.3 0.0 collective-permute-done.other_ref
  31.3 0.0 copy-start.5
  31.3 0.9 copy-done.5
  32.2 17.1 %near_attention.1 = (bf16[1024,384]{1,0:T(8,128)(2,1)}, f32[1024,384]{1,0:T(8,128)}, f32[1024,384]{1,0:T(8,128)}) custom-call(s32[1]{0:T(128)} %bitcast.part_ref, bf16[512,768]{1,0:T(8,128)(2,1)} %get-tuple-element.21.x_ref.own_ref, bf16[512,768]{1,0:T(8,128)(2,1)} %copy-done.5, bf16[512,384]{1,0:T(8,128)(2,1)} %get-tuple-element.22.k_ref, ...), custom_call_target="tpu_custom_call" | custom-call | flops 12000000000 | bytes 8000000 | tf_op jit(solution)/shard_map/near_attention/pallas_call | solution.py:304
  49.2 0.0 all-to-all-done
  49.2 0.9 copy-done.2
  50.1 10.0 %far_attention.1 = (bf16[1024,384]{1,0:T(8,128)(2,1)}, f32[32,8,256]{2,1,0:T(8,128)}) custom-call(bf16[1024,384]{1,0:T(8,128)(2,1)} %get-tuple-element.24.q_ref, bf16[512,768]{1,0:T(8,128)(2,1)} %bitcast.12, f32[1024,384]{1,0:T(8,128)} %get-tuple-element.26.near_ref, f32[1024,384]{1,0:T(8,128)} %get-tuple-element.27.near_lse_ref, ...), custom_call_target="tpu_custom_call" | custom-call | flops 6000000000 | bytes 6000000 | tf_op jit(solution)/shard_map/far_attention/pallas_call | solution.py:329
  60.1 0.0 copy-start.4
  60.2 1.3 %fusion.8 = (bf16[512,384]{1,0:T(8,128)(2,1)S(1)}, bf16[512,384]{1,0:T(8,128)(2,1)S(1)}) fusion(bf16[1024,384]{1,0:T(8,128)(2,1)} %get-tuple-element.31), kind=kLoop, calls=%fused_computation.11 | loop fusion | bytes 1572864 | tf_op jit(solution)/shard_map/slice | solution.py:356
  61.5 1.4 %collective-permute-start.2 = (bf16[512,384]{1,0:T(8,128)(2,1)S(1)}, bf16[512,384]{1,0:T(8,128)(2,1)S(1)}, u32[]{:S(2)}, u32[]{:S(2)}) collective-permute-start(bf16[512,384]{1,0:T(8,128)(2,1)S(1)} %get-tuple-element.38), channel_id=1, source_target_pairs={{0,8},{8,0},{16,24},{24,16},{1,9},{9,1},{17,25},{25,17},{2,10},{10... | collective-permute-start | bytes 1179656 | tf_op jit(solution)/shard_map/ppermute | solution.py:25
  62.9 11.6 %all-to-all-start.1 = ((f32[32,8,256]{2,1,0:T(8,128)}), f32[32,8,256]{2,1,0:T(8,128)S(1)}, u32[]{:S(2)}, u32[]{:S(2)}) async-start(f32[32,8,256]{2,1,0:T(8,128)} %get-tuple-element.29), calls=%async_computation.1 | async-start | bytes 524288 | tf_op jit(solution)/shard_map/all_to_all | solution.py:366
  75.8 0.0 collective-permute-done.2
  75.8 0.0 copy-done
  75.8 0.0 copy-done.4
  75.8 1.7 %fusion = bf16[1,512,768]{2,1,0:T(8,128)(2,1)} fusion(bf16[768,768]{1,0:T(8,128)(2,1)S(1)} %copy-done, bf16[512,768]{1,0:T(8,128)(2,1)S(1)} %copy-done.4, bf16[512,384]{1,0:T(8,128)(2,1)S(1)} %get-tuple-element.39, bf16[512,384]{1,0:T(8,128)(2,1)S(1)} %collective-permute-done.2, pred[]{:T(512)S(6)} %eq.5), kind=kOutput, calls=%fused_computation.1 | convolution fusion | flops 608698368 | bytes 3538945 | tf_op jit(solution)/shard_map/dot_general | solution.py:363
  77.5 9.1 %all-to-all-done.1.sums_ref = f32[32,8,256]{2,1,0:T(8,128)S(1)} async-done(((f32[32,8,256]{2,1,0:T(8,128)}), f32[32,8,256]{2,1,0:T(8,128)S(1)}, u32[]{:S(2)}, u32[]{:S(2)}) %all-to-all-start.1) | async-done | bytes 262176 | tf_op jit(solution)/shard_map/all_to_all | solution.py:366
  86.6 0.7 copy-done.1
  87.3 3.0 %pooled.1 = (f32[1,768]{1,0:T(1,128)}, f32[8,8,256]{2,1,0:T(8,128)}) custom-call(s32[1]{0:T(128)S(6)} %copy.17.slide_code_ref, s32[1]{0:T(128)S(6)} %copy.18.report_code_ref, f32[32,8,256]{2,1,0:T(8,128)} %copy-done.1, bf16[768,768]{1,0:T(8,128)(2,1)} %w_out_ref.1, bf16[768,768]{1,0:T(8,128)(2,1)} %w_head_ref.1, bf16[1,768]{1,0:T(2,128)(2,1)} %report_ref.1), custom_call_target="tpu_custom_call" | custom-call | tf_op jit(solution)/shard_map/pooled/pallas_call | solution.py:369
  90.3 14.0 %all_to_all.15.all_ref = f32[8,8,256]{2,1,0:T(8,128)} all-to-all(f32[8,8,256]{2,1,0:T(8,128)} %get-tuple-element.35), channel_id=1, replica_groups=mesh['x'=4,'z_hi'=2,'y'=4,'slide'=8] {'slide'}, dimensions={0} | all-to-all | bytes 131072 | tf_op jit(solution)/shard_map/all_to_all | solution.py:379
  104.2 1.8 %contrast.1 = (f32[8,8]{1,0:T(8,128)}, f32[1,1]{1,0:T(1,128)}) custom-call(f32[8,8,256]{2,1,0:T(8,128)} %all_to_all.15.all_ref), custom_call_target="tpu_custom_call" | custom-call | tf_op jit(solution)/shard_map/contrast/pallas_call | solution.py:380
  (5 shorter events, 0.0 us)
Async XLA Ops:
  1.9 7.6 %copy-start.3 = (s32[16]{0:T(128)S(1)}, s32[16]{0:T(128)}, u32[]{:S(2)}) copy-start(s32[16]{0:T(128)} %param.20) | copy-start | bytes 196
  7.4 23.9 %collective-permute-start = (bf16[512,768]{1,0:T(8,128)(2,1)}, bf16[512,768]{1,0:T(8,128)(2,1)S(1)}, u32[]{:S(2)}, u32[]{:S(2)}) collective-permute-start(bf16[512,768]{1,0:T(8,128)(2,1)} %get-tuple-element.21.x_ref.own_ref), channel_id=1, source_target_pairs={{0,8},{8,0},{16,24},{24,16},{1,9},{9,1},{17,25},{25,17},{2,10},{10... | collective-permute-start | bytes 2359304 | tf_op jit(solution)/shard_map/ppermute | solution.py:25
  14.4 8.6 %collective-permute-start.1 = (bf16[2,16,768]{2,1,0:T(8,128)(2,1)}, bf16[2,16,768]{2,1,0:T(8,128)(2,1)S(1)}, u32[]{:S(2)}, u32[]{:S(2)}) collective-permute-start(bf16[2,16,768]{2,1,0:T(8,128)(2,1)} %get-tuple-element.25), channel_id=1, source_target_pairs={{0,32},{32,0},{1,33},{33,1},{2,34},{34,2},{3,35},{35,3},{4,36},{36... | collective-permute-start | bytes 147464 | tf_op jit(solution)/shard_map/ppermute | solution.py:25
  24.8 24.4 %all-to-all-start = ((bf16[16,32,768]{2,1,0:T(8,128)(2,1)}), bf16[16,32,768]{2,1,0:T(8,128)(2,1)S(1)}, u32[]{:S(2)}, u32[]{:S(2)}) async-start(bf16[16,32,768]{2,1,0:T(8,128)(2,1)} %bitcast.5), calls=%async_computation | async-start | bytes 1572864 | tf_op jit(solution)/shard_map/all_to_all | solution.py:298
  31.3 0.9 copy-start.5
  49.2 0.9 copy-start.2
  60.1 15.7 %copy-start = (bf16[768,768]{1,0:T(8,128)(2,1)S(1)}, bf16[768,768]{1,0:T(8,128)(2,1)}, u32[]{:S(2)}) copy-start(bf16[768,768]{1,0:T(8,128)(2,1)} %w_out_ref.1) | copy-start | bytes 3538948
  60.1 15.7 %copy-start.4 = (bf16[512,768]{1,0:T(8,128)(2,1)S(1)}, bf16[512,768]{1,0:T(8,128)(2,1)}, u32[]{:S(2)}) copy-start(bf16[512,768]{1,0:T(8,128)(2,1)} %get-tuple-element.30) | copy-start | bytes 2359300
  61.5 14.3 %collective-permute-start.2 = (bf16[512,384]{1,0:T(8,128)(2,1)S(1)}, bf16[512,384]{1,0:T(8,128)(2,1)S(1)}, u32[]{:S(2)}, u32[]{:S(2)}) collective-permute-start(bf16[512,384]{1,0:T(8,128)(2,1)S(1)} %get-tuple-element.38), channel_id=1, source_target_pairs={{0,8},{8,0},{16,24},{24,16},{1,9},{9,1},{17,25},{25,17},{2,10},{10... | collective-permute-start | bytes 1179656 | tf_op jit(solution)/shard_map/ppermute | solution.py:25
  62.9 23.7 %all-to-all-start.1 = ((f32[32,8,256]{2,1,0:T(8,128)}), f32[32,8,256]{2,1,0:T(8,128)S(1)}, u32[]{:S(2)}, u32[]{:S(2)}) async-start(f32[32,8,256]{2,1,0:T(8,128)} %get-tuple-element.29), calls=%async_computation.1 | async-start | bytes 524288 | tf_op jit(solution)/shard_map/all_to_all | solution.py:366
  86.6 0.7 copy-start.1

commit v3 on v2

--- a/solution.py
+++ b/solution.py
@@ -15,7 +15,10 @@
 NORM_EPS = 1e-05
 NT = (((1,), (1,)), ((), ()))
 NN = (((1,), (0,)), ((), ()))
-VMEM_LIMIT = 56 << 20
+ATTEND_VMEM = 32 << 20
+SMALL_VMEM = 16 << 20
+EMBED_VMEM = 58 << 20
+EMBED_STEPS = 3
 SEQ_AXES = ("x", "z_hi", "y")
 F32 = jnp.float32
 BF16 = jnp.bfloat16
@@ -58,37 +61,81 @@
         lse_ref[rows, first:last] = lse
 
 
-def embed_kernel(x_ref, w_ref, gain_ref, embedded_ref, normed_ref, sum_ref, acc_scr):
-    step = pl.program_id(0)
-
-    @pl.when(step == 0)
-    def _():
-        acc_scr[...] = jnp.dot(x_ref[...], w_ref[...], preferred_element_type=F32)
-
-    @pl.when(step > 0)
-    def _():
-        acc_scr[...] += jnp.dot(x_ref[...], w_ref[...], preferred_element_type=F32)
-
-    @pl.when(step == pl.num_programs(0) - 1)
-    def _():
-        embedded = acc_scr[...].astype(BF16)
-        embedded_ref[...] = embedded
-        floats = embedded.astype(F32)
-        centred = floats - jnp.mean(floats, axis=1, keepdims=True)
-        spread = jnp.mean(centred * centred, axis=1, keepdims=True)
-        normed = centred * lax.rsqrt(spread + NORM_EPS) * gain_ref[...]
-        normed_ref[...] = normed.astype(BF16)
-        sum_ref[...] = jnp.sum(floats, axis=0, keepdims=True)
-
-
-def own_rows_kernel(part_ref, x_ref, wk_ref, wv_ref, offset_ref, far_ref, k_ref, v_ref):
+def merge_states(one, one_lse, two, two_lse):
+    share = 1.0 / (1.0 + jnp.exp(two_lse - one_lse))
+    return two + (one - two) * share
+
+
+def embed_kernel(x_hbm, w_hbm, gain_ref, embedded_ref, normed_ref, sum_ref, x_scr, w_scr, sems):
+    depth = x_scr.shape[2]
+    halves = 2
+    part_rows, part_depth = x_scr.shape[1] // halves, depth // halves
+    copies = []
+    for step in range(EMBED_STEPS):
+        group = []
+        for i in range(halves):
+            rows = slice(i * part_rows, (i + 1) * part_rows)
+            group.append(
+                pltpu.make_async_copy(
+                    x_hbm.at[rows, step * depth : (step + 1) * depth],
+                    x_scr.at[step, rows, :],
+                    sems.at[step, i],
+                )
+            )
+            first = step * depth + i * part_depth
+            group.append(
+                pltpu.make_async_copy(
+                    w_hbm.at[first : first + part_depth, :],
+                    w_scr.at[step, i * part_depth : (i + 1) * part_depth, :],
+                    sems.at[step, halves + i],
+                )
+            )
+        for copy in group:
+            copy.start()
+        copies.append(group)
+    total = None
+    for step, group in enumerate(copies):
+        for copy in group:
+            copy.wait()
+        product = jnp.dot(x_scr[step], w_scr[step], preferred_element_type=F32)
+        total = product if total is None else total + product
+    embedded = total.astype(BF16)
+    embedded_ref[...] = embedded
+    floats = embedded.astype(F32)
+    centred = floats - jnp.mean(floats, axis=1, keepdims=True)
+    spread = jnp.mean(centred * centred, axis=1, keepdims=True)
+    normed = centred * lax.rsqrt(spread + NORM_EPS) * gain_ref[...][None, :]
+    normed_ref[...] = normed.astype(BF16)
+    sum_ref[...] = jnp.sum(floats, axis=0, keepdims=True)
+
+
+def own_rows_kernel(part_ref, offset_ref, x_ref, wk_hbm, wv_hbm, far_ref, k_ref, v_ref,
+                    w_scr, sems):
     rows, width = x_ref.shape
     half = width // 2
+    heads = offset_ref.shape[0]
+    pieces = sems.shape[1]
+    depth = width // pieces
+    copies = []
+    for place, w_hbm in enumerate((wk_hbm, wv_hbm)):
+        for i in range(pieces):
+            span = slice(i * depth, (i + 1) * depth)
+            copy = pltpu.make_async_copy(
+                w_hbm.at[span, :], w_scr.at[place, span, :], sems.at[place, i]
+            )
+            copy.start()
+            copies.append(copy)
+    lane = lax.broadcasted_iota(jnp.int32, (1, width), 1)
+    lane_offset = jnp.zeros((1, width), jnp.int32)
+    for head in range(heads):
+        lane_offset = jnp.where(lane >= head * (width // heads), offset_ref[head], lane_offset)
     phase = lax.broadcasted_iota(jnp.int32, (RATE, width), 0)
-    chosen = jnp.where(phase == offset_ref[...], 1.0, 0.0)
+    chosen = jnp.where(phase == lane_offset, 1.0, 0.0)
     upper = part_ref[0] == 1
-    for place, (w_ref, half_ref) in enumerate(((wk_ref, k_ref), (wv_ref, v_ref))):
-        full = jnp.dot(x_ref[...], w_ref[...], preferred_element_type=F32)
+    for place, half_ref in enumerate((k_ref, v_ref)):
+        for copy in copies[place * pieces : (place + 1) * pieces]:
+            copy.wait()
+        full = jnp.dot(x_ref[...], w_scr[place], preferred_element_type=F32)
         half_ref[...] = jnp.where(upper, full[:, half:], full[:, :half]).astype(BF16)
         grouped = full.reshape(rows // RATE, RATE, width) * chosen[None]
         picked = jnp.sum(grouped, axis=1).astype(BF16)
@@ -98,47 +145,65 @@
             ]
 
 
-def near_kernel(part_ref, own_ref, other_ref, k_ref, v_ref, wq_ref, wk_ref, wv_ref,
-                q_ref, mixed_ref, lse_ref, k_scr, v_scr, *, head_width, score_scale):
+def payload_kernel(own_ref, other_ref, out_ref):
+    for place, ref in enumerate((own_ref, other_ref)):
+        out_ref[:, :, place, :, :] = jnp.broadcast_to(ref[...][None], out_ref.shape[:2] + ref.shape[1:])
+
+
+def own_kernel(part_ref, x_ref, k_ref, v_ref, wq_ref, q_ref, mixed_ref, lse_ref, *, head_width,
+               score_scale):
+    q = jnp.dot(x_ref[...], wq_ref[...], preferred_element_type=F32) * score_scale
+    q_ref[...] = q.astype(BF16)
+    attend(q_ref[...], k_ref[...], v_ref[...], head_width, mixed_ref, lse_ref, slice(None))
+
+
+def near_kernel(part_ref, other_ref, k_ref, v_ref, q_own_ref, own_mixed_ref, own_lse_ref,
+                wq_ref, wk_ref, wv_ref, q_ref, mixed_ref, lse_ref, k_scr, v_scr,
+                *, head_width, score_scale):
     step = pl.program_id(0)
-    rows = own_ref.shape[0]
+    rows = other_ref.shape[0]
 
     @pl.when(step == 0)
     def _():
-        for place, x_ref in enumerate((own_ref, other_ref)):
-            q = jnp.dot(x_ref[...], wq_ref[...], preferred_element_type=F32) * score_scale
-            q_ref[place * rows : (place + 1) * rows, :] = q.astype(BF16)
+        other = other_ref[...]
         for scr, own_half_ref, w_ref in ((k_scr, k_ref, wk_ref), (v_scr, v_ref, wv_ref)):
             scr[:rows, :] = own_half_ref[...]
-            other = jnp.dot(other_ref[...], w_ref[...], preferred_element_type=F32)
-            scr[rows:, :] = other.astype(BF16)
-
-    queries = q_ref[pl.ds(pl.multiple_of(step * rows, rows), rows), :]
-    attend(queries, k_scr[...], v_scr[...], head_width, mixed_ref, lse_ref, slice(None))
-
-
-def far_kernel(q_ref, far_ref, near_ref, near_lse_ref, embedded_sum_ref, out_ref, pack_ref,
-               mixed_scr, lse_scr, sum_scr, *, head_width):
+            scr[rows:, :] = jnp.dot(other, w_ref[...], preferred_element_type=F32).astype(BF16)
+        q_ref[:rows, :] = q_own_ref[...]
+        q = jnp.dot(other, wq_ref[...], preferred_element_type=F32) * score_scale
+        q_ref[rows:, :] = q.astype(BF16)
+        attend(q_own_ref[...], k_scr[rows:, :], v_scr[rows:, :], head_width, mixed_ref, lse_ref,
+               slice(None))
+        own_lse, new_lse = own_lse_ref[...], lse_ref[...]
+        mixed_ref[...] = merge_states(own_mixed_ref[...], own_lse, mixed_ref[...], new_lse)
+        gap = jnp.exp(-jnp.abs(own_lse - new_lse))
+        lse_ref[...] = jnp.maximum(own_lse, new_lse) + jnp.log(1.0 + gap)
+
+    @pl.when(step == 1)
+    def _():
+        attend(q_ref[rows:, :], k_scr[...], v_scr[...], head_width, mixed_ref, lse_ref, slice(None))
+
+
+def far_kernel(q_ref, far_ref, near_ref, near_lse_ref, embedded_sum_ref, own_ref, lent_ref,
+               pack_ref, mixed_scr, lse_scr, sum_scr, *, head_width):
     step = pl.program_id(0)
     half = q_ref.shape[1]
     attend(
         q_ref[...], far_ref[:, :half], far_ref[:, half:], head_width, mixed_scr, lse_scr, slice(None)
     )
-    near_share = 1.0 / (1.0 + jnp.exp(lse_scr[...] - near_lse_ref[...]))
-    far_mixed = mixed_scr[...]
-    attended = far_mixed + (near_ref[...] - far_mixed) * near_share
-    out_ref[...] = attended.astype(BF16)
+    attended = merge_states(near_ref[...], near_lse_ref[...], mixed_scr[...], lse_scr[...])
+    summed = jnp.sum(attended, axis=0, keepdims=True)
 
     @pl.when(step == 0)
     def _():
-        sum_scr[...] = jnp.zeros_like(sum_scr)
-
-    sum_scr[...] += jnp.sum(attended, axis=0, keepdims=True)
-
-    @pl.when(step == pl.num_programs(0) - 1)
+        own_ref[...] = attended.astype(BF16)
+        sum_scr[...] = summed
+
+    @pl.when(step == 1)
     def _():
+        lent_ref[...] = attended.astype(BF16)
         pad = jnp.zeros((1, pack_ref.shape[1] * pack_ref.shape[2] - 3 * half), F32)
-        packed = pack_row((embedded_sum_ref[...], sum_scr[...], pad))
+        packed = pack_row((embedded_sum_ref[...], sum_scr[...] + summed, pad))
         pack_ref[...] = jnp.broadcast_to(packed[None], pack_ref.shape)
 
 
@@ -248,65 +313,87 @@
     score_scale = 1.0 / math.sqrt(head_width)
     part = lax.axis_index("y") % 2
     parts = part.reshape(1)
-    params = pltpu.CompilerParams(vmem_limit_bytes=VMEM_LIMIT)
-
-    steps = 3
-    depth = in_width // steps
+    params = pltpu.CompilerParams(vmem_limit_bytes=ATTEND_VMEM)
+    small = pltpu.CompilerParams(vmem_limit_bytes=SMALL_VMEM)
+    smem = pl.BlockSpec(memory_space=pltpu.SMEM)
+    vmem = pl.BlockSpec(memory_space=pltpu.VMEM)
+    anywhere = pl.BlockSpec(memory_space=pl.ANY)
+
+    depth = in_width // EMBED_STEPS
     embedded, normed, embedded_sum = pl.pallas_call(
         embed_kernel,
-        grid=(steps,),
-        in_specs=[
-            pl.BlockSpec((rows, depth), lambda i: (0, i)),
-            pl.BlockSpec((depth, width), lambda i: (i, 0)),
-            pl.BlockSpec((1, width), lambda i: (0, 0)),
-        ],
-        out_specs=[
-            pl.BlockSpec((rows, width), lambda i: (0, 0)),
-            pl.BlockSpec((rows, width), lambda i: (0, 0)),
-            pl.BlockSpec((1, width), lambda i: (0, 0)),
-        ],
+        in_specs=[anywhere, anywhere, vmem],
         out_shape=[
             jax.ShapeDtypeStruct((rows, width), BF16),
             jax.ShapeDtypeStruct((rows, width), BF16),
             jax.ShapeDtypeStruct((1, width), F32),
         ],
-        scratch_shapes=[pltpu.VMEM((rows, width), F32)],
-        compiler_params=params,
+        scratch_shapes=[
+            pltpu.VMEM((EMBED_STEPS, rows, depth), BF16),
+            pltpu.VMEM((EMBED_STEPS, depth, width), BF16),
+            pltpu.SemaphoreType.DMA((EMBED_STEPS, 4)),
+        ],
+        compiler_params=pltpu.CompilerParams(vmem_limit_bytes=EMBED_VMEM),
         name="embed",
-    )(tiles.reshape(rows, in_width), w_embed, attn_gain.reshape(1, width))
+    )(tiles.reshape(rows, in_width), w_embed, attn_gain)
     other_normed = swap_with(normed, "y")
 
-    lane_offset = jnp.broadcast_to(head_offset[:, None], (heads_count, head_width)).reshape(1, width)
     far_rows = rows // RATE
-    smem = pl.BlockSpec(memory_space=pltpu.SMEM)
-    vmem = pl.BlockSpec(memory_space=pltpu.VMEM)
     far_own, keys_own, values_own = pl.pallas_call(
         own_rows_kernel,
-        in_specs=[smem, vmem, vmem, vmem, vmem],
+        in_specs=[smem, smem, vmem, anywhere, anywhere],
         out_shape=[
             jax.ShapeDtypeStruct((2, far_rows, width), BF16),
             jax.ShapeDtypeStruct((rows, half), BF16),
             jax.ShapeDtypeStruct((rows, half), BF16),
         ],
-        compiler_params=params,
+        scratch_shapes=[
+            pltpu.VMEM((2, width, width), BF16),
+            pltpu.SemaphoreType.DMA((2, 2)),
+        ],
+        compiler_params=small,
         name="own_rows",
-    )(parts, normed, w_key, w_value, lane_offset)
-    far_pair = jnp.stack((far_own, swap_with(far_own, "z_hi")), axis=1)
-    far_pair = far_pair.reshape(2, 2 * far_rows, width)
-    payload = jnp.broadcast_to(far_pair[None], (plane // 2, 2, 2 * far_rows, width))
-    payload = payload.reshape(plane, 2 * far_rows, width)
+    )(parts, head_offset, normed, w_key, w_value)
+    far_other = swap_with(far_own, "z_hi")
+    payload = pl.pallas_call(
+        payload_kernel,
+        in_specs=[vmem, vmem],
+        out_shape=jax.ShapeDtypeStruct((plane // 2, 2, 2, far_rows, width), BF16),
+        compiler_params=small,
+        name="payload",
+    )(far_own, far_other).reshape(plane, 2 * far_rows, width)
     far = lax.all_to_all(payload, ("x", "y"), 0, 0, tiled=True).reshape(ranks * far_rows, width)
 
     weight_spec = pl.BlockSpec((width, half), lambda i, p: (0, p[0]))
     whole = pl.BlockSpec((rows, width), lambda i, p: (0, 0))
     whole_half = pl.BlockSpec((rows, half), lambda i, p: (0, 0))
     row_block = pl.BlockSpec((rows, half), lambda i, p: (i, 0))
+    queries_own, own_mixed, own_lse = pl.pallas_call(
+        functools.partial(own_kernel, head_width=head_width, score_scale=score_scale),
+        grid_spec=pltpu.PrefetchScalarGridSpec(
+            num_scalar_prefetch=1,
+            grid=(1,),
+            in_specs=[whole, whole_half, whole_half, weight_spec],
+            out_specs=[whole_half, whole_half, whole_half],
+        ),
+        out_shape=[
+            jax.ShapeDtypeStruct((rows, half), BF16),
+            jax.ShapeDtypeStruct((rows, half), F32),
+            jax.ShapeDtypeStruct((rows, half), F32),
+        ],
+        compiler_params=params,
+        cost_estimate=pl.CostEstimate(
+            flops=3_000_000_000, bytes_accessed=4_000_000, transcendentals=2_000_000
+        ),
+        name="own_attention",
+    )(parts, normed, keys_own, values_own, w_query)
+
     queries, near_mixed, near_lse = pl.pallas_call(
         functools.partial(near_kernel, head_width=head_width, score_scale=score_scale),
         grid_spec=pltpu.PrefetchScalarGridSpec(
             num_scalar_prefetch=1,
             grid=(2,),
-            in_specs=[whole, whole, whole_half, whole_half, weight_spec, weight_spec, weight_spec],
+            in_specs=[whole] + [whole_half] * 5 + [weight_spec] * 3,
             out_specs=[pl.BlockSpec((2 * rows, half), lambda i, p: (0, 0)), row_block, row_block],
             scratch_shapes=[
                 pltpu.VMEM((2 * rows, half), BF16),
@@ -320,13 +407,14 @@
         ],
         compiler_params=params,
         cost_estimate=pl.CostEstimate(
-            flops=12_000_000_000, bytes_accessed=8_000_000, transcendentals=8_000_000
+            flops=9_000_000_000, bytes_accessed=8_000_000, transcendentals=6_000_000
         ),
         name="near_attention",
-    )(parts, normed, other_normed, keys_own, values_own, w_query, w_key, w_value)
+    )(parts, other_normed, keys_own, values_own, queries_own, own_mixed, own_lse,
+      w_query, w_key, w_value)
 
     row_block = pl.BlockSpec((rows, half), lambda i: (i, 0))
-    attended, sums = pl.pallas_call(
+    own_half, lent_half, sums = pl.pallas_call(
         functools.partial(far_kernel, head_width=head_width),
         grid=(2,),
         in_specs=[
@@ -336,9 +424,14 @@
             row_block,
             pl.BlockSpec((1, width), lambda i: (0, 0)),
         ],
-        out_specs=[row_block, pl.BlockSpec((ranks,) + PACK, lambda i: (0, 0, 0))],
-        out_shape=[
-            jax.ShapeDtypeStruct((2 * rows, half), BF16),
+        out_specs=[
+            pl.BlockSpec((rows, half), lambda i: (0, 0)),
+            pl.BlockSpec((rows, half), lambda i: (0, 0)),
+            pl.BlockSpec((ranks,) + PACK, lambda i: (0, 0, 0)),
+        ],
+        out_shape=[
+            jax.ShapeDtypeStruct((rows, half), BF16),
+            jax.ShapeDtypeStruct((rows, half), BF16),
             jax.ShapeDtypeStruct((ranks,) + PACK, F32),
         ],
         scratch_shapes=[
@@ -353,7 +446,8 @@
         name="far_attention",
     )(queries, far, near_mixed, near_lse, embedded_sum)
 
-    own_half, lent_half = attended[:rows], attended[rows:]
+    sums = lax.all_to_all(sums, SEQ_AXES, 0, 0, tiled=True)
+    sums, lent_half = lax.optimization_barrier((sums, lent_half))
     other_half = swap_with(lent_half, "y")
     joined = jnp.where(
         part == 1,
@@ -363,8 +457,6 @@
     encoded = embedded.astype(F32) + jnp.dot(joined, w_out, preferred_element_type=F32)
     encoded = encoded.astype(BF16).reshape(1, rows, width)
 
-    sums = lax.all_to_all(sums, SEQ_AXES, 0, 0, tiled=True)
-    sums, encoded = lax.optimization_barrier((sums, encoded))
     slides = lax.axis_size("slide")
     slide_unit_vectors, packed = pl.pallas_call(
         functools.partial(pooled_kernel, length=rows * ranks),
@@ -373,10 +465,11 @@
             jax.ShapeDtypeStruct((1, width), F32),
             jax.ShapeDtypeStruct((slides,) + PACK, F32),
         ],
-        compiler_params=params,
+        compiler_params=small,
         name="pooled",
     )(slide_code, report_code, sums, w_out, w_head, report_emb)
     everyone = lax.all_to_all(packed, "slide", 0, 0, tiled=True)
+    everyone, encoded = lax.optimization_barrier((everyone, encoded))
     logits, loss = pl.pallas_call(
         contrast_kernel,
         in_specs=[vmem],
@@ -384,7 +477,7 @@
             jax.ShapeDtypeStruct((slides, slides), F32),
             jax.ShapeDtypeStruct((1, 1), F32),
         ],
-        compiler_params=params,
+        compiler_params=small,
         name="contrast",
     )(everyone)
     return (encoded, slide_unit_vectors, logits, loss.reshape(()))

time: 107 us -> 104 us (0.972)
  local copies, waits for them, and re-layouts: 6.8 us -> 15.6 us
  waiting for transfers between devices: 10.8 us -> 2.03 us
  Pallas kernels: 41.5 us -> 35.8 us
  blocking collectives: 14 us -> 19.5 us
  starting transfers between devices: 28.5 us -> 25.1 us
  matrix products: 1.67 us -> 3.05 us
    unnamed x12 -> x54, local copies, waits for them, and re-layouts: 2.47 us -> 15.6 us
    all_to_all x1, waiting for transfers between devices: 9.09 us -> 2.02 us  [on_device(): everyone = lax.all_to_all(packed, 'slide', 0, 0, tiled=True)]
    all_to_all x1, blocking collectives: 14 us -> 19.5 us  [on_device(): sums = lax.all_to_all(sums, SEQ_AXES, 0, 0, tiled=True)]
    pallas_call x1, Pallas kernels: 17.1 us -> 12.7 us  [on_device(): pl.pallas_call(functools.partial(near_kernel, head_width=head_width, scor...]
    pallas_call x2 -> x4, Pallas kernels: 9.61 us -> 13.7 us  [the longest x1 5.58 us: on_device(): pl.pallas_call(embed_kernel, in_specs=[anywhere, anywhere, vmem], out_sha...]
    pallas_call x1, Pallas kernels: 10 us -> 7.17 us  [on_device(): pl.pallas_call(functools.partial(far_kernel, head_width=head_width), grid...]
    all_to_all x1, starting transfers between devices: 11.6 us -> 8.79 us  [on_device(): everyone = lax.all_to_all(packed, 'slide', 0, 0, tiled=True)]
    reshape x2 -> x0, local copies, waits for them, and re-layouts: 1.93 us -> none  [the longest x1 1.27 us: on_device(): attn_gain.reshape(1, width)]
  transfers between devices with their start and end apart: 5 -> 5, of which waited for: 2 -> 1; matrix products, arithmetic and copies ran while one was open for 4% -> 3% of each run, Pallas kernels for 20% -> 21%
where the time goes in v3:
time: 104 us; the launch traced here: 103 us
  Pallas kernels  35.8 us (34%)
  starting transfers between devices  25.1 us (24%)
  blocking collectives  19.5 us (19%)
  local copies, waits for them, and re-layouts  15.6 us (15%)
  matrix products  3.05 us (3%)
  between operations  2.11 us (2%)
  waiting for transfers between devices  2.03 us (2%)
    all_to_all x1, blocking collectives, on_device(): sums = lax.all_to_all(sums, SEQ_AXES, 0, 0, tiled=True)  19.5 us
    unnamed x54, local copies, waits for them, and re-layouts  15.6 us
    pallas_call x1, Pallas kernels, on_device(): pl.pallas_call(functools.partial(near_kernel, head_width=head_width, scor...  12.7 us
    ppermute x3, starting transfers between devices, swap_with(): lax.ppermute(x, axis, [(i, i ^ 1) for i in range(lax.axis_size(axis))])  9.82 us
    all_to_all x1, starting transfers between devices, on_device(): everyone = lax.all_to_all(packed, 'slide', 0, 0, tiled=True)  8.79 us
    pallas_call x1, Pallas kernels, on_device(): pl.pallas_call(functools.partial(far_kernel, head_width=head_width), grid...  7.17 us
    all_to_all x1, starting transfers between devices, on_device(): lax.all_to_all(payload, ('x', 'y'), 0, 0, tiled=True)  6.47 us
    pallas_call x1, Pallas kernels, on_device(): pl.pallas_call(embed_kernel, in_specs=[anywhere, anywhere, vmem], out_sha...  5.58 us
  transfers between devices with their start and end apart: 5, of which 1 were waited for; matrix products, arithmetic and copies ran while one was open for 3% of the time, Pallas kernels for 21%

profile of v3, /device:TPU:1, one launch (start us, length us, event | category | flops | bytes accessed | tf_op | source)
XLA Modules:
  0.0 103.2 jit_solution(3249731674409687105)
XLA Ops:
  0.7 5.6 %embed.1 = (bf16[512,768]{1,0:T(8,128)(2,1)}, bf16[512,768]{1,0:T(8,128)(2,1)}, f32[1,768]{1,0:T(1,128)}) custom-call(bf16[512,1536]{1,0:T(8,128)(2,1)} %bitcast.9, bf16[1536,768]{1,0:T(8,128)(2,1)} %w_hbm.1, f32[768]{0:T(1024)} %gain_ref.1), custom_call_target="tpu_custom_call" | custom-call | tf_op jit(solution)/shard_map/embed/pallas_call | solution.py:323
  6.3 2.2 %collective-permute-start = (bf16[512,768]{1,0:T(8,128)(2,1)}, bf16[512,768]{1,0:T(8,128)(2,1)}, u32[]{:S(2)}, u32[]{:S(2)}) collective-permute-start(bf16[512,768]{1,0:T(8,128)(2,1)} %get-tuple-element.27.x_ref), channel_id=1, source_target_pairs={{0,8},{8,0},{16,24},{24,16},{1,9},{9,1},{17,25},{25,17},{2,10},{10... | collective-permute-start | bytes 2359304 | tf_op jit(solution)/shard_map/ppermute | solution.py:28
  8.5 1.2 %copy-done.4 = bf16[512,768]{1,0:T(8,128)(2,1)S(1)} copy-done((bf16[512,768]{1,0:T(8,128)(2,1)S(1)}, bf16[512,768]{1,0:T(8,128)(2,1)}, u32[]{:S(2)}) %copy-start.4) | copy-done | bytes 786456
  9.6 3.1 %own_rows.1 = (bf16[2,16,768]{2,1,0:T(8,128)(2,1)S(1)}, bf16[512,384]{1,0:T(8,128)(2,1)S(1)}, bf16[512,384]{1,0:T(8,128)(2,1)S(1)}) custom-call(s32[1]{0:T(128)} %bitcast.part_ref, s32[16]{0:T(128)S(1)} %copy-done.7, bf16[512,768]{1,0:T(8,128)(2,1)S(1)} %copy-done.4, bf16[768,768]{1,0:T(8,128)(2,1)S(1)} %copy-done.2, bf16[768,768]{1,0:T(8,128)(2,1)S(1)} %copy-done.3), custom_call_target="tpu_custom_call" | custom-call | tf_op jit(solution)/shard_map/own_rows/pallas_call | solution.py:342
  12.7 7.0 %collective-permute-start.1 = (bf16[2,16,768]{2,1,0:T(8,128)(2,1)S(1)}, bf16[2,16,768]{2,1,0:T(8,128)(2,1)S(1)}, u32[]{:S(2)}, u32[]{:S(2)}) collective-permute-start(bf16[2,16,768]{2,1,0:T(8,128)(2,1)S(1)} %get-tuple-element.34.own_ref), channel_id=1, source_target_pairs={{0,32},{32,0},{1,33},{33,1},{2,34},{34,2},{3,35},{35,3},{4,36},{36... | collective-permute-start | bytes 147464 | tf_op jit(solution)/shard_map/ppermute | solution.py:28
  19.7 4.0 %own_attention.1 = (bf16[512,384]{1,0:T(8,128)(2,1)S(1)}, f32[512,384]{1,0:T(8,128)S(1)}, f32[512,384]{1,0:T(8,128)S(1)}) custom-call(s32[1]{0:T(128)} %bitcast.part_ref, bf16[512,768]{1,0:T(8,128)(2,1)S(1)} %copy-done.5, bf16[512,384]{1,0:T(8,128)(2,1)S(1)} %get-tuple-element.28.k_ref, bf16[512,384]{1,0:T(8,128)(2,1)S(1)} %get-tuple-element.29.v_ref, ...), custom_call_target="tpu_custom_call" | custom-call | flops 3000000000 | bytes 4000000 | tf_op jit(solution)/shard_map/own_attention/pallas_call | solution.py:371
  23.8 0.9 copy-done.17
  24.6 0.7 copy-done.19
  25.4 1.0 payload.1
  26.4 0.1 copy-done.15
  26.5 6.5 %all-to-all-start = ((bf16[16,32,768]{2,1,0:T(8,128)(2,1)}), bf16[16,32,768]{2,1,0:T(8,128)(2,1)S(1)}, u32[]{:S(2)}, u32[]{:S(2)}) async-start(bf16[16,32,768]{2,1,0:T(8,128)(2,1)} %bitcast.2), calls=%async_computation | async-start | bytes 1572864 | tf_op jit(solution)/shard_map/all_to_all | solution.py:365
  33.0 0.0 copy-start.9
  33.0 1.3 %copy-done.9 = bf16[768,768]{1,0:T(8,128)(2,1)S(1)} copy-done((bf16[768,768]{1,0:T(8,128)(2,1)S(1)}, bf16[768,768]{1,0:T(8,128)(2,1)}, u32[]{:S(2)}) %copy-start.9) | copy-done | bytes 1179672
  34.3 1.0 copy-done.11
  35.3 1.1 %copy-done.16 = f32[512,384]{1,0:T(8,128)S(1)} copy-done((f32[512,384]{1,0:T(8,128)S(1)}, f32[512,384]{1,0:T(8,128)}, u32[]{:S(2)}) %copy-start.16) | copy-done | bytes 786456
  36.4 1.1 %copy-done.18 = f32[512,384]{1,0:T(8,128)S(1)} copy-done((f32[512,384]{1,0:T(8,128)S(1)}, f32[512,384]{1,0:T(8,128)}, u32[]{:S(2)}) %copy-start.18) | copy-done | bytes 786456
  37.6 1.0 copy-done.20
  38.6 12.7 %near_attention.1 = (bf16[1024,384]{1,0:T(8,128)(2,1)S(1)}, f32[1024,384]{1,0:T(8,128)S(1)}, f32[1024,384]{1,0:T(8,128)S(1)}) custom-call(s32[1]{0:T(128)} %bitcast.part_ref, bf16[512,768]{1,0:T(8,128)(2,1)} %collective-permute-done.other_ref, bf16[512,384]{1,0:T(8,128)(2,1)S(1)} %get-tuple-element.28.k_ref, bf16[512,384]{1,0:T(8,128)(2,1)S(1)} %copy-done.11, ...), custom_call_target="tpu_custom_call" | custom-call | flops 8999999488 | bytes 8000000 | tf_op jit(solution)/shard_map/near_attention/pallas_call | solution.py:391
  51.3 1.2 %copy-done.21 = f32[1024,384]{1,0:T(8,128)} copy-done((f32[1024,384]{1,0:T(8,128)}, f32[1024,384]{1,0:T(8,128)S(1)}, u32[]{:S(2)}) %copy-start.21) | copy-done | bytes 1572888
  52.4 1.1 %copy-done.23 = f32[1024,384]{1,0:T(8,128)} copy-done((f32[1024,384]{1,0:T(8,128)}, f32[1024,384]{1,0:T(8,128)S(1)}, u32[]{:S(2)}) %copy-start.23) | copy-done | bytes 1572888
  53.6 0.9 copy-done.25
  54.5 1.4 %copy-done.22 = f32[1024,384]{1,0:T(8,128)S(1)} copy-done((f32[1024,384]{1,0:T(8,128)S(1)}, f32[1024,384]{1,0:T(8,128)}, u32[]{:S(2)}) %copy-start.22) | copy-done | bytes 1572888
  55.9 1.4 %copy-done.24 = f32[1024,384]{1,0:T(8,128)S(1)} copy-done((f32[1024,384]{1,0:T(8,128)S(1)}, f32[1024,384]{1,0:T(8,128)}, u32[]{:S(2)}) %copy-start.24) | copy-done | bytes 1572888
  57.3 1.1 %copy-done.26 = bf16[1024,384]{1,0:T(8,128)(2,1)S(1)} copy-done((bf16[1024,384]{1,0:T(8,128)(2,1)S(1)}, bf16[1024,384]{1,0:T(8,128)(2,1)}, u32[]{:S(2)}) %copy-start.26) | copy-done | bytes 786456
  58.4 7.2 %far_attention.1 = (bf16[512,384]{1,0:T(8,128)(2,1)S(1)}, bf16[512,384]{1,0:T(8,128)(2,1)S(1)}, f32[32,8,256]{2,1,0:T(8,128)S(1)}) custom-call(bf16[1024,384]{1,0:T(8,128)(2,1)S(1)} %copy-done.26, bf16[512,768]{1,0:T(8,128)(2,1)S(1)} %bitcast.8, f32[1024,384]{1,0:T(8,128)S(1)} %copy-done.22, f32[1024,384]{1,0:T(8,128)S(1)} %copy-done.24, f32[1,768]{1,0:T(1,128)S(1)} %copy-done.12), custom_call_target="tpu_custom_call" | custom-call | flops 6000000000 | bytes 6000000 | tf_op jit(solution)/shard_map/far_attention/pallas_call | solution.py:417
  65.6 19.5 %all_to_all.15.sums_ref = f32[32,8,256]{2,1,0:T(8,128)S(1)} all-to-all(f32[32,8,256]{2,1,0:T(8,128)S(1)} %get-tuple-element.38), channel_id=1, replica_groups=mesh['x'=4,'z_hi'=2,'y'=4,'slide'=8] {'x','z_hi','y'}, dimensions={0} | all-to-all | bytes 524288 | tf_op jit(solution)/shard_map/all_to_all | solution.py:449
  85.1 0.6 collective-permute-start.2
  87.1 1.3 %pooled.1 = (f32[1,768]{1,0:T(1,128)}, f32[8,8,256]{2,1,0:T(8,128)}) custom-call(s32[1]{0:T(128)S(6)} %copy.16.slide_code_ref, s32[1]{0:T(128)S(6)} %copy.17.report_code_ref, f32[32,8,256]{2,1,0:T(8,128)S(1)} %all_to_all.15.sums_ref, bf16[768,768]{1,0:T(8,128)(2,1)S(1)} %copy-done.1, bf16[768,768]{1,0:T(8,128)(2,1)S(1)} %copy-done, bf16[1,768]{1,0:T(2,128)(2,1)S(1)} %copy-done.6), custom_call_target="tpu_custom_call" | custom-call | tf_op jit(solution)/shard_map/pooled/pallas_call | solution.py:461
  88.3 8.8 %all-to-all-start.2 = ((f32[8,8,256]{2,1,0:T(8,128)}), f32[8,8,256]{2,1,0:T(8,128)S(1)}, u32[]{:S(2)}, u32[]{:S(2)}) async-start(f32[8,8,256]{2,1,0:T(8,128)} %get-tuple-element.41), calls=%async_computation.2 | async-start | bytes 131072 | tf_op jit(solution)/shard_map/all_to_all | solution.py:471
  97.2 3.0 %fusion = bf16[1,512,768]{2,1,0:T(8,128)(2,1)} fusion(bf16[768,768]{1,0:T(8,128)(2,1)S(1)} %copy-done.1, bf16[512,768]{1,0:T(8,128)(2,1)} %get-tuple-element.42, bf16[512,384]{1,0:T(8,128)(2,1)S(1)} %copy-done.14, bf16[512,384]{1,0:T(8,128)(2,1)} %collective-permute-done.2, pred[]{:T(512)S(6)} %eq.5), kind=kOutput, calls=%fused_computation.1 | convolution fusion | flops 608698368 | bytes 3538945 | tf_op jit(solution)/shard_map/dot_general | solution.py:457
  100.2 2.0 %all-to-all-done.2.all_ref = f32[8,8,256]{2,1,0:T(8,128)S(1)} async-done(((f32[8,8,256]{2,1,0:T(8,128)}), f32[8,8,256]{2,1,0:T(8,128)S(1)}, u32[]{:S(2)}, u32[]{:S(2)}) %all-to-all-start.2) | async-done | bytes 65568 | tf_op jit(solution)/shard_map/all_to_all | solution.py:471
  102.2 1.0 contrast.1
  (42 shorter events, 0.1 us)
Async XLA Ops:
  0.6 7.8 %copy-start.2 = (bf16[768,768]{1,0:T(8,128)(2,1)S(1)}, bf16[768,768]{1,0:T(8,128)(2,1)}, u32[]{:S(2)}) copy-start(bf16[768,768]{1,0:T(8,128)(2,1)} %wk_ref.1) | copy-start | bytes 3538948
  0.6 7.8 %copy-start.3 = (bf16[768,768]{1,0:T(8,128)(2,1)S(1)}, bf16[768,768]{1,0:T(8,128)(2,1)}, u32[]{:S(2)}) copy-start(bf16[768,768]{1,0:T(8,128)(2,1)} %wv_ref.1) | copy-start | bytes 3538948
  0.7 7.8 %copy-start.7 = (s32[16]{0:T(128)S(1)}, s32[16]{0:T(128)}, u32[]{:S(2)}) copy-start(s32[16]{0:T(128)} %offset_ref.1) | copy-start | bytes 196
  6.3 26.8 %collective-permute-start = (bf16[512,768]{1,0:T(8,128)(2,1)}, bf16[512,768]{1,0:T(8,128)(2,1)}, u32[]{:S(2)}, u32[]{:S(2)}) collective-permute-start(bf16[512,768]{1,0:T(8,128)(2,1)} %get-tuple-element.27.x_ref), channel_id=1, source_target_pairs={{0,8},{8,0},{16,24},{24,16},{1,9},{9,1},{17,25},{25,17},{2,10},{10... | collective-permute-start | bytes 2359304 | tf_op jit(solution)/shard_map/ppermute | solution.py:28
  8.5 1.2 %copy-start.4 = (bf16[512,768]{1,0:T(8,128)(2,1)S(1)}, bf16[512,768]{1,0:T(8,128)(2,1)}, u32[]{:S(2)}) copy-start(bf16[512,768]{1,0:T(8,128)(2,1)} %get-tuple-element.27.x_ref) | copy-start | bytes 2359300
  9.6 10.1 %copy-start.5 = (bf16[512,768]{1,0:T(8,128)(2,1)S(1)}, bf16[512,768]{1,0:T(8,128)(2,1)}, u32[]{:S(2)}) copy-start(bf16[512,768]{1,0:T(8,128)(2,1)} %get-tuple-element.27.x_ref) | copy-start | bytes 2359300
  9.6 10.1 %copy-start.8 = (bf16[768,768]{1,0:T(8,128)(2,1)S(1)}, bf16[768,768]{1,0:T(8,128)(2,1)}, u32[]{:S(2)}) copy-start(bf16[768,768]{1,0:T(8,128)(2,1)} %wq_ref.3) | copy-start | bytes 3538948
  12.7 11.0 %copy-start.10 = (bf16[512,384]{1,0:T(8,128)(2,1)}, bf16[512,384]{1,0:T(8,128)(2,1)S(1)}, u32[]{:S(2)}) copy-start(bf16[512,384]{1,0:T(8,128)(2,1)S(1)} %get-tuple-element.29.v_ref) | copy-start | bytes 1179652
  12.7 12.7 %collective-permute-start.1 = (bf16[2,16,768]{2,1,0:T(8,128)(2,1)S(1)}, bf16[2,16,768]{2,1,0:T(8,128)(2,1)S(1)}, u32[]{:S(2)}, u32[]{:S(2)}) collective-permute-start(bf16[2,16,768]{2,1,0:T(8,128)(2,1)S(1)} %get-tuple-element.34.own_ref), channel_id=1, source_target_pairs={{0,32},{32,0},{1,33},{33,1},{2,34},{34,2},{3,35},{35,3},{4,36},{36... | collective-permute-start | bytes 147464 | tf_op jit(solution)/shard_map/ppermute | solution.py:28
  23.7 0.9 copy-start.17
  24.6 0.8 copy-start.19
  25.4 1.2 %copy-start.15 = (f32[512,384]{1,0:T(8,128)}, f32[512,384]{1,0:T(8,128)S(1)}, u32[]{:S(2)}) copy-start(f32[512,384]{1,0:T(8,128)S(1)} %get-tuple-element.31.own_mixed_ref) | copy-start | bytes 2359300
  26.5 27.9 %all-to-all-start = ((bf16[16,32,768]{2,1,0:T(8,128)(2,1)}), bf16[16,32,768]{2,1,0:T(8,128)(2,1)S(1)}, u32[]{:S(2)}, u32[]{:S(2)}) async-start(bf16[16,32,768]{2,1,0:T(8,128)(2,1)} %bitcast.2), calls=%async_computation | async-start | bytes 1572864 | tf_op jit(solution)/shard_map/all_to_all | solution.py:365
  33.0 1.3 %copy-start.9 = (bf16[768,768]{1,0:T(8,128)(2,1)S(1)}, bf16[768,768]{1,0:T(8,128)(2,1)}, u32[]{:S(2)}) copy-start(bf16[768,768]{1,0:T(8,128)(2,1)} %wq_ref.3) | copy-start | bytes 3538948
  34.3 1.0 copy-start.11
  35.3 1.1 %copy-start.16 = (f32[512,384]{1,0:T(8,128)S(1)}, f32[512,384]{1,0:T(8,128)}, u32[]{:S(2)}) copy-start(f32[512,384]{1,0:T(8,128)} %copy-done.15) | copy-start | bytes 2359300
  36.4 1.1 %copy-start.18 = (f32[512,384]{1,0:T(8,128)S(1)}, f32[512,384]{1,0:T(8,128)}, u32[]{:S(2)}) copy-start(f32[512,384]{1,0:T(8,128)} %copy-done.17) | copy-start | bytes 2359300
  37.6 1.0 copy-start.20
  38.6 15.9 %copy-start.12 = (f32[1,768]{1,0:T(1,128)S(1)}, f32[1,768]{1,0:T(1,128)}, u32[]{:S(2)}) copy-start(f32[1,768]{1,0:T(1,128)} %get-tuple-element.37.embedded_sum_ref) | copy-start | bytes 9220
  51.2 1.2 %copy-start.21 = (f32[1024,384]{1,0:T(8,128)}, f32[1024,384]{1,0:T(8,128)S(1)}, u32[]{:S(2)}) copy-start(f32[1024,384]{1,0:T(8,128)S(1)} %get-tuple-element.35.near_ref) | copy-start | bytes 4718596
  52.4 1.1 %copy-start.23 = (f32[1024,384]{1,0:T(8,128)}, f32[1024,384]{1,0:T(8,128)S(1)}, u32[]{:S(2)}) copy-start(f32[1024,384]{1,0:T(8,128)S(1)} %get-tuple-element.36.near_lse_ref) | copy-start | bytes 4718596
  53.6 0.9 copy-start.25
  54.5 1.4 %copy-start.22 = (f32[1024,384]{1,0:T(8,128)S(1)}, f32[1024,384]{1,0:T(8,128)}, u32[]{:S(2)}) copy-start(f32[1024,384]{1,0:T(8,128)} %copy-done.21) | copy-start | bytes 4718596
  55.9 1.4 %copy-start.24 = (f32[1024,384]{1,0:T(8,128)S(1)}, f32[1024,384]{1,0:T(8,128)}, u32[]{:S(2)}) copy-start(f32[1024,384]{1,0:T(8,128)} %copy-done.23) | copy-start | bytes 4718596
  57.3 1.1 %copy-start.26 = (bf16[1024,384]{1,0:T(8,128)(2,1)S(1)}, bf16[1024,384]{1,0:T(8,128)(2,1)}, u32[]{:S(2)}) copy-start(bf16[1024,384]{1,0:T(8,128)(2,1)} %copy-done.25) | copy-start | bytes 2359300
  58.4 28.6 %copy-start = (bf16[768,768]{1,0:T(8,128)(2,1)S(1)}, bf16[768,768]{1,0:T(8,128)(2,1)}, u32[]{:S(2)}) copy-start(bf16[768,768]{1,0:T(8,128)(2,1)} %w_head_ref.1) | copy-start | bytes 3538948
  58.4 28.6 %copy-start.1 = (bf16[768,768]{1,0:T(8,128)(2,1)S(1)}, bf16[768,768]{1,0:T(8,128)(2,1)}, u32[]{:S(2)}) copy-start(bf16[768,768]{1,0:T(8,128)(2,1)} %w_out_ref.1) | copy-start | bytes 3538948
  58.4 28.6 %copy-start.6 = (bf16[1,768]{1,0:T(2,128)(2,1)S(1)}, bf16[1,768]{1,0:T(2,128)(2,1)}, u32[]{:S(2)}) copy-start(bf16[1,768]{1,0:T(2,128)(2,1)} %report_ref.1) | copy-start | bytes 4612
  65.6 19.5 %copy-start.13 = (bf16[512,384]{1,0:T(8,128)(2,1)}, bf16[512,384]{1,0:T(8,128)(2,1)S(1)}, u32[]{:S(2)}) copy-start(bf16[512,384]{1,0:T(8,128)(2,1)S(1)} %get-tuple-element.44) | copy-start | bytes 1179652
  85.1 12.0 %copy-start.14 = (bf16[512,384]{1,0:T(8,128)(2,1)S(1)}, bf16[512,384]{1,0:T(8,128)(2,1)}, u32[]{:S(2)}) copy-start(bf16[512,384]{1,0:T(8,128)(2,1)} %copy-done.13) | copy-start | bytes 1179652
  85.1 12.0 %collective-permute-start.2 = (bf16[512,384]{1,0:T(8,128)(2,1)S(1)}, bf16[512,384]{1,0:T(8,128)(2,1)}, u32[]{:S(2)}, u32[]{:S(2)}) collective-permute-start(bf16[512,384]{1,0:T(8,128)(2,1)S(1)} %get-tuple-element.43), channel_id=1, source_target_pairs={{0,8},{8,0},{16,24},{24,16},{1,9},{9,1},{17,25},{25,17},{2,10},{10... | collective-permute-start | bytes 1179656 | tf_op jit(solution)/shard_map/ppermute | solution.py:28
  88.3 13.9 %all-to-all-start.2 = ((f32[8,8,256]{2,1,0:T(8,128)}), f32[8,8,256]{2,1,0:T(8,128)S(1)}, u32[]{:S(2)}, u32[]{:S(2)}) async-start(f32[8,8,256]{2,1,0:T(8,128)} %get-tuple-element.41), calls=%async_computation.2 | async-start | bytes 131072 | tf_op jit(solution)/shard_map/all_to_all | solution.py:471

commit v4 on v3

--- a/solution.py
+++ b/solution.py
@@ -15,10 +15,9 @@
 NORM_EPS = 1e-05
 NT = (((1,), (1,)), ((), ()))
 NN = (((1,), (0,)), ((), ()))
-ATTEND_VMEM = 32 << 20
 SMALL_VMEM = 16 << 20
-EMBED_VMEM = 58 << 20
-EMBED_STEPS = 3
+LARGE_VMEM = 58 << 20
+EMBED_STEPS = 6
 SEQ_AXES = ("x", "z_hi", "y")
 F32 = jnp.float32
 BF16 = jnp.bfloat16
@@ -66,7 +65,16 @@
     return two + (one - two) * share
 
 
-def embed_kernel(x_hbm, w_hbm, gain_ref, embedded_ref, normed_ref, sum_ref, x_scr, w_scr, sems):
+def started(sources, targets, sems, first=0):
+    copies = []
+    for place, (source, target) in enumerate(zip(sources, targets)):
+        copies.append(pltpu.make_async_copy(source, target, sems.at[first + place]))
+        copies[-1].start()
+    return copies
+
+
+def embed_kernel(x_hbm, w_hbm, gain_ref, embedded_hbm, normed_hbm, sum_ref, x_scr, w_scr,
+                 embedded_scr, normed_scr, sems, out_sems):
     depth = x_scr.shape[2]
     halves = 2
     part_rows, part_depth = x_scr.shape[1] // halves, depth // halves
@@ -100,31 +108,30 @@
         product = jnp.dot(x_scr[step], w_scr[step], preferred_element_type=F32)
         total = product if total is None else total + product
     embedded = total.astype(BF16)
-    embedded_ref[...] = embedded
+    embedded_scr[...] = embedded
+    stores = started((embedded_scr,), (embedded_hbm,), out_sems)
     floats = embedded.astype(F32)
     centred = floats - jnp.mean(floats, axis=1, keepdims=True)
     spread = jnp.mean(centred * centred, axis=1, keepdims=True)
     normed = centred * lax.rsqrt(spread + NORM_EPS) * gain_ref[...][None, :]
-    normed_ref[...] = normed.astype(BF16)
+    normed_scr[...] = normed.astype(BF16)
+    stores += started((normed_scr,), (normed_hbm,), out_sems, 1)
     sum_ref[...] = jnp.sum(floats, axis=0, keepdims=True)
-
-
-def own_rows_kernel(part_ref, offset_ref, x_ref, wk_hbm, wv_hbm, far_ref, k_ref, v_ref,
-                    w_scr, sems):
-    rows, width = x_ref.shape
+    for store in stores:
+        store.wait()
+
+
+def own_rows_kernel(part_ref, offset_ref, x_hbm, wk_hbm, wv_hbm, far_ref, k_out, v_out,
+                    x_scr, w_scr, half_scr, sems, out_sems):
+    rows, width = x_scr.shape
     half = width // 2
     heads = offset_ref.shape[0]
-    pieces = sems.shape[1]
-    depth = width // pieces
-    copies = []
-    for place, w_hbm in enumerate((wk_hbm, wv_hbm)):
-        for i in range(pieces):
-            span = slice(i * depth, (i + 1) * depth)
-            copy = pltpu.make_async_copy(
-                w_hbm.at[span, :], w_scr.at[place, span, :], sems.at[place, i]
-            )
-            copy.start()
-            copies.append(copy)
+    spans = (pl.ds(0, half), pl.ds(half, half))
+    loads = started(
+        [x_hbm] + [wk_hbm.at[span] for span in spans] + [wv_hbm.at[span] for span in spans],
+        [x_scr] + [w_scr.at[0, span] for span in spans] + [w_scr.at[1, span] for span in spans],
+        sems,
+    )
     lane = lax.broadcasted_iota(jnp.int32, (1, width), 1)
     lane_offset = jnp.zeros((1, width), jnp.int32)
     for head in range(heads):
@@ -132,17 +139,22 @@
     phase = lax.broadcasted_iota(jnp.int32, (RATE, width), 0)
     chosen = jnp.where(phase == lane_offset, 1.0, 0.0)
     upper = part_ref[0] == 1
-    for place, half_ref in enumerate((k_ref, v_ref)):
-        for copy in copies[place * pieces : (place + 1) * pieces]:
-            copy.wait()
-        full = jnp.dot(x_ref[...], w_scr[place], preferred_element_type=F32)
-        half_ref[...] = jnp.where(upper, full[:, half:], full[:, :half]).astype(BF16)
+    loads[0].wait()
+    stores = []
+    for place, half_out in enumerate((k_out, v_out)):
+        loads[1 + 2 * place].wait()
+        loads[2 + 2 * place].wait()
+        full = jnp.dot(x_scr[...], w_scr[place], preferred_element_type=F32)
+        half_scr[place] = jnp.where(upper, full[:, half:], full[:, :half]).astype(BF16)
+        stores += started((half_scr.at[place],), (half_out,), out_sems, place)
         grouped = full.reshape(rows // RATE, RATE, width) * chosen[None]
         picked = jnp.sum(grouped, axis=1).astype(BF16)
         for part in range(2):
             far_ref[part, :, place * half : (place + 1) * half] = picked[
                 :, part * half : (part + 1) * half
             ]
+    for store in stores:
+        store.wait()
 
 
 def payload_kernel(own_ref, other_ref, out_ref):
@@ -150,61 +162,106 @@
         out_ref[:, :, place, :, :] = jnp.broadcast_to(ref[...][None], out_ref.shape[:2] + ref.shape[1:])
 
 
-def own_kernel(part_ref, x_ref, k_ref, v_ref, wq_ref, q_ref, mixed_ref, lse_ref, *, head_width,
-               score_scale):
-    q = jnp.dot(x_ref[...], wq_ref[...], preferred_element_type=F32) * score_scale
-    q_ref[...] = q.astype(BF16)
-    attend(q_ref[...], k_ref[...], v_ref[...], head_width, mixed_ref, lse_ref, slice(None))
-
-
-def near_kernel(part_ref, other_ref, k_ref, v_ref, q_own_ref, own_mixed_ref, own_lse_ref,
-                wq_ref, wk_ref, wv_ref, q_ref, mixed_ref, lse_ref, k_scr, v_scr,
-                *, head_width, score_scale):
-    step = pl.program_id(0)
-    rows = other_ref.shape[0]
-
-    @pl.when(step == 0)
-    def _():
-        other = other_ref[...]
-        for scr, own_half_ref, w_ref in ((k_scr, k_ref, wk_ref), (v_scr, v_ref, wv_ref)):
-            scr[:rows, :] = own_half_ref[...]
-            scr[rows:, :] = jnp.dot(other, w_ref[...], preferred_element_type=F32).astype(BF16)
-        q_ref[:rows, :] = q_own_ref[...]
-        q = jnp.dot(other, wq_ref[...], preferred_element_type=F32) * score_scale
-        q_ref[rows:, :] = q.astype(BF16)
-        attend(q_own_ref[...], k_scr[rows:, :], v_scr[rows:, :], head_width, mixed_ref, lse_ref,
-               slice(None))
-        own_lse, new_lse = own_lse_ref[...], lse_ref[...]
-        mixed_ref[...] = merge_states(own_mixed_ref[...], own_lse, mixed_ref[...], new_lse)
-        gap = jnp.exp(-jnp.abs(own_lse - new_lse))
-        lse_ref[...] = jnp.maximum(own_lse, new_lse) + jnp.log(1.0 + gap)
-
-    @pl.when(step == 1)
-    def _():
-        attend(q_ref[rows:, :], k_scr[...], v_scr[...], head_width, mixed_ref, lse_ref, slice(None))
-
-
-def far_kernel(q_ref, far_ref, near_ref, near_lse_ref, embedded_sum_ref, own_ref, lent_ref,
-               pack_ref, mixed_scr, lse_scr, sum_scr, *, head_width):
-    step = pl.program_id(0)
-    half = q_ref.shape[1]
-    attend(
-        q_ref[...], far_ref[:, :half], far_ref[:, half:], head_width, mixed_scr, lse_scr, slice(None)
-    )
-    attended = merge_states(near_ref[...], near_lse_ref[...], mixed_scr[...], lse_scr[...])
-    summed = jnp.sum(attended, axis=0, keepdims=True)
-
-    @pl.when(step == 0)
-    def _():
-        own_ref[...] = attended.astype(BF16)
-        sum_scr[...] = summed
-
-    @pl.when(step == 1)
-    def _():
-        lent_ref[...] = attended.astype(BF16)
-        pad = jnp.zeros((1, pack_ref.shape[1] * pack_ref.shape[2] - 3 * half), F32)
-        packed = pack_row((embedded_sum_ref[...], sum_scr[...] + summed, pad))
-        pack_ref[...] = jnp.broadcast_to(packed[None], pack_ref.shape)
+def half_columns(w_hbm, part_ref):
+    half = w_hbm.shape[1] // 2
+    return w_hbm.at[:, pl.ds(pl.multiple_of(part_ref[0] * half, half), half)]
+
+
+def own_kernel(part_ref, x_hbm, wq_hbm, k_hbm, v_hbm, q_out, mixed_out, lse_out,
+               x_scr, wq_scr, k_scr, v_scr, q_scr, mixed_scr, lse_scr, in_sems, out_sems,
+               *, head_width, score_scale):
+    loads = started(
+        (x_hbm, half_columns(wq_hbm, part_ref), k_hbm, v_hbm), (x_scr, wq_scr, k_scr, v_scr), in_sems
+    )
+    loads[0].wait()
+    loads[1].wait()
+    q = jnp.dot(x_scr[...], wq_scr[...], preferred_element_type=F32) * score_scale
+    q_scr[...] = q.astype(BF16)
+    stores = started((q_scr,), (q_out,), out_sems)
+    loads[2].wait()
+    loads[3].wait()
+    attend(q_scr[...], k_scr[...], v_scr[...], head_width, mixed_scr, lse_scr, slice(None))
+    stores += started((mixed_scr, lse_scr), (mixed_out, lse_out), out_sems, 1)
+    for store in stores:
+        store.wait()
+
+
+def near_kernel(part_ref, other_hbm, k_hbm, v_hbm, q_hbm, own_mixed_hbm, own_lse_hbm,
+                wq_hbm, wk_hbm, wv_hbm, q_out, mixed_out, lse_out,
+                x_scr, w_scr, k_scr, v_scr, q_scr, own_mixed_scr, own_lse_scr, mixed_scr, lse_scr,
+                in_sems, out_sems, *, head_width, score_scale):
+    rows = x_scr.shape[0]
+    own, other = pl.ds(0, rows), pl.ds(rows, rows)
+    loads = started(
+        (
+            half_columns(wk_hbm, part_ref), other_hbm, half_columns(wv_hbm, part_ref),
+            half_columns(wq_hbm, part_ref), k_hbm, v_hbm, q_hbm, own_mixed_hbm, own_lse_hbm,
+        ),
+        (
+            w_scr.at[0], x_scr, w_scr.at[1],
+            w_scr.at[2], k_scr.at[own], v_scr.at[own], q_scr.at[own], own_mixed_scr, own_lse_scr,
+        ),
+        in_sems,
+    )
+    loads[0].wait()
+    loads[1].wait()
+    k_scr[rows:, :] = jnp.dot(x_scr[...], w_scr[0], preferred_element_type=F32).astype(BF16)
+    loads[2].wait()
+    v_scr[rows:, :] = jnp.dot(x_scr[...], w_scr[1], preferred_element_type=F32).astype(BF16)
+    loads[3].wait()
+    q = jnp.dot(x_scr[...], w_scr[2], preferred_element_type=F32) * score_scale
+    q_scr[rows:, :] = q.astype(BF16)
+    stores = started((q_scr.at[other],), (q_out.at[other],), out_sems)
+    loads[4].wait()
+    loads[5].wait()
+    attend(q_scr[rows:, :], k_scr[...], v_scr[...], head_width, mixed_scr.at[1], lse_scr.at[1],
+           slice(None))
+    stores += started(
+        (mixed_scr.at[1], lse_scr.at[1]), (mixed_out.at[other], lse_out.at[other]), out_sems, 1
+    )
+    loads[6].wait()
+    stores += started((q_scr.at[own],), (q_out.at[own],), out_sems, 3)
+    attend(q_scr[:rows, :], k_scr[rows:, :], v_scr[rows:, :], head_width, mixed_scr.at[0],
+           lse_scr.at[0], slice(None))
+    loads[7].wait()
+    loads[8].wait()
+    own_lse, new_lse = own_lse_scr[...], lse_scr[0]
+    mixed_scr[0] = merge_states(own_mixed_scr[...], own_lse, mixed_scr[0], new_lse)
+    gap = jnp.exp(-jnp.abs(own_lse - new_lse))
+    lse_scr[0] = jnp.maximum(own_lse, new_lse) + jnp.log(1.0 + gap)
+    stores += started(
+        (mixed_scr.at[0], lse_scr.at[0]), (mixed_out.at[own], lse_out.at[own]), out_sems, 4
+    )
+    for store in stores:
+        store.wait()
+
+
+def far_kernel(q_hbm, far_hbm, near_hbm, near_lse_hbm, embedded_sum_ref, own_ref, lent_ref,
+               pack_ref, q_scr, far_scr, near_scr, near_lse_scr, mixed_scr, lse_scr, sems,
+               *, head_width):
+    half = q_scr.shape[1]
+    rows = own_ref.shape[0]
+    loads = started(
+        (far_hbm, q_hbm, near_hbm, near_lse_hbm), (far_scr, q_scr, near_scr, near_lse_scr), sems
+    )
+    loads[0].wait()
+    loads[1].wait()
+    total = jnp.zeros((1, half), F32)
+    for place, out_ref in enumerate((own_ref, lent_ref)):
+        span = slice(place * rows, (place + 1) * rows)
+        attend(q_scr[span, :], far_scr[:, :half], far_scr[:, half:], head_width,
+               mixed_scr.at[place], lse_scr.at[place], slice(None))
+        if place == 0:
+            loads[2].wait()
+            loads[3].wait()
+        attended = merge_states(
+            near_scr[span, :], near_lse_scr[span, :], mixed_scr[place], lse_scr[place]
+        )
+        out_ref[...] = attended.astype(BF16)
+        total += jnp.sum(attended, axis=0, keepdims=True)
+    pad = jnp.zeros((1, pack_ref.shape[1] * pack_ref.shape[2] - 3 * half), F32)
+    packed = pack_row((embedded_sum_ref[...], total, pad))
+    pack_ref[...] = jnp.broadcast_to(packed[None], pack_ref.shape)
 
 
 def pack_row(pieces):
@@ -313,7 +370,7 @@
     score_scale = 1.0 / math.sqrt(head_width)
     part = lax.axis_index("y") % 2
     parts = part.reshape(1)
-    params = pltpu.CompilerParams(vmem_limit_bytes=ATTEND_VMEM)
+    params = pltpu.CompilerParams(vmem_limit_bytes=LARGE_VMEM)
     small = pltpu.CompilerParams(vmem_limit_bytes=SMALL_VMEM)
     smem = pl.BlockSpec(memory_space=pltpu.SMEM)
     vmem = pl.BlockSpec(memory_space=pltpu.VMEM)
@@ -323,6 +380,7 @@
     embedded, normed, embedded_sum = pl.pallas_call(
         embed_kernel,
         in_specs=[anywhere, anywhere, vmem],
+        out_specs=[anywhere, anywhere, vmem],
         out_shape=[
             jax.ShapeDtypeStruct((rows, width), BF16),
             jax.ShapeDtypeStruct((rows, width), BF16),
@@ -331,9 +389,12 @@
         scratch_shapes=[
             pltpu.VMEM((EMBED_STEPS, rows, depth), BF16),
             pltpu.VMEM((EMBED_STEPS, depth, width), BF16),
+            pltpu.VMEM((rows, width), BF16),
+            pltpu.VMEM((rows, width), BF16),
             pltpu.SemaphoreType.DMA((EMBED_STEPS, 4)),
-        ],
-        compiler_params=pltpu.CompilerParams(vmem_limit_bytes=EMBED_VMEM),
+            pltpu.SemaphoreType.DMA((2,)),
+        ],
+        compiler_params=pltpu.CompilerParams(vmem_limit_bytes=LARGE_VMEM),
         name="embed",
     )(tiles.reshape(rows, in_width), w_embed, attn_gain)
     other_normed = swap_with(normed, "y")
@@ -341,17 +402,21 @@
     far_rows = rows // RATE
     far_own, keys_own, values_own = pl.pallas_call(
         own_rows_kernel,
-        in_specs=[smem, smem, vmem, anywhere, anywhere],
+        in_specs=[smem, smem, anywhere, anywhere, anywhere],
+        out_specs=[vmem, anywhere, anywhere],
         out_shape=[
             jax.ShapeDtypeStruct((2, far_rows, width), BF16),
             jax.ShapeDtypeStruct((rows, half), BF16),
             jax.ShapeDtypeStruct((rows, half), BF16),
         ],
         scratch_shapes=[
+            pltpu.VMEM((rows, width), BF16),
             pltpu.VMEM((2, width, width), BF16),
-            pltpu.SemaphoreType.DMA((2, 2)),
-        ],
-        compiler_params=small,
+            pltpu.VMEM((2, rows, half), BF16),
+            pltpu.SemaphoreType.DMA((5,)),
+            pltpu.SemaphoreType.DMA((2,)),
+        ],
+        compiler_params=params,
         name="own_rows",
     )(parts, head_offset, normed, w_key, w_value)
     far_other = swap_with(far_own, "z_hi")
@@ -364,46 +429,50 @@
     )(far_own, far_other).reshape(plane, 2 * far_rows, width)
     far = lax.all_to_all(payload, ("x", "y"), 0, 0, tiled=True).reshape(ranks * far_rows, width)
 
-    weight_spec = pl.BlockSpec((width, half), lambda i, p: (0, p[0]))
-    whole = pl.BlockSpec((rows, width), lambda i, p: (0, 0))
-    whole_half = pl.BlockSpec((rows, half), lambda i, p: (0, 0))
-    row_block = pl.BlockSpec((rows, half), lambda i, p: (i, 0))
+    half_rows = jax.ShapeDtypeStruct((rows, half), BF16)
+    half_state = jax.ShapeDtypeStruct((rows, half), F32)
     queries_own, own_mixed, own_lse = pl.pallas_call(
         functools.partial(own_kernel, head_width=head_width, score_scale=score_scale),
-        grid_spec=pltpu.PrefetchScalarGridSpec(
-            num_scalar_prefetch=1,
-            grid=(1,),
-            in_specs=[whole, whole_half, whole_half, weight_spec],
-            out_specs=[whole_half, whole_half, whole_half],
-        ),
-        out_shape=[
-            jax.ShapeDtypeStruct((rows, half), BF16),
-            jax.ShapeDtypeStruct((rows, half), F32),
-            jax.ShapeDtypeStruct((rows, half), F32),
+        in_specs=[smem] + [anywhere] * 4,
+        out_specs=[anywhere] * 3,
+        out_shape=[half_rows, half_state, half_state],
+        scratch_shapes=[
+            pltpu.VMEM((rows, width), BF16),
+            pltpu.VMEM((width, half), BF16),
+            pltpu.VMEM((rows, half), BF16),
+            pltpu.VMEM((rows, half), BF16),
+            pltpu.VMEM((rows, half), BF16),
+            pltpu.VMEM((rows, half), F32),
+            pltpu.VMEM((rows, half), F32),
+            pltpu.SemaphoreType.DMA((4,)),
+            pltpu.SemaphoreType.DMA((3,)),
         ],
         compiler_params=params,
         cost_estimate=pl.CostEstimate(
             flops=3_000_000_000, bytes_accessed=4_000_000, transcendentals=2_000_000
         ),
         name="own_attention",
-    )(parts, normed, keys_own, values_own, w_query)
-
+    )(parts, normed, w_query, keys_own, values_own)
+
+    both_rows = jax.ShapeDtypeStruct((2 * rows, half), BF16)
+    both_state = jax.ShapeDtypeStruct((2 * rows, half), F32)
     queries, near_mixed, near_lse = pl.pallas_call(
         functools.partial(near_kernel, head_width=head_width, score_scale=score_scale),
-        grid_spec=pltpu.PrefetchScalarGridSpec(
-            num_scalar_prefetch=1,
-            grid=(2,),
-            in_specs=[whole] + [whole_half] * 5 + [weight_spec] * 3,
-            out_specs=[pl.BlockSpec((2 * rows, half), lambda i, p: (0, 0)), row_block, row_block],
-            scratch_shapes=[
-                pltpu.VMEM((2 * rows, half), BF16),
-                pltpu.VMEM((2 * rows, half), BF16),
-            ],
-        ),
-        out_shape=[
-            jax.ShapeDtypeStruct((2 * rows, half), BF16),
-            jax.ShapeDtypeStruct((2 * rows, half), F32),
-            jax.ShapeDtypeStruct((2 * rows, half), F32),
+        in_specs=[smem] + [anywhere] * 9,
+        out_specs=[anywhere] * 3,
+        out_shape=[both_rows, both_state, both_state],
+        scratch_shapes=[
+            pltpu.VMEM((rows, width), BF16),
+            pltpu.VMEM((3, width, half), BF16),
+            pltpu.VMEM((2 * rows, half), BF16),
+            pltpu.VMEM((2 * rows, half), BF16),
+            pltpu.VMEM((2 * rows, half), BF16),
+            pltpu.VMEM((rows, half), F32),
+            pltpu.VMEM((rows, half), F32),
+            pltpu.VMEM((2, rows, half), F32),
+            pltpu.VMEM((2, rows, half), F32),
+            pltpu.SemaphoreType.DMA((9,)),
+            pltpu.SemaphoreType.DMA((6,)),
         ],
         compiler_params=params,
         cost_estimate=pl.CostEstimate(
@@ -413,31 +482,19 @@
     )(parts, other_normed, keys_own, values_own, queries_own, own_mixed, own_lse,
       w_query, w_key, w_value)
 
-    row_block = pl.BlockSpec((rows, half), lambda i: (i, 0))
     own_half, lent_half, sums = pl.pallas_call(
         functools.partial(far_kernel, head_width=head_width),
-        grid=(2,),
-        in_specs=[
-            row_block,
-            pl.BlockSpec((ranks * far_rows, width), lambda i: (0, 0)),
-            row_block,
-            row_block,
-            pl.BlockSpec((1, width), lambda i: (0, 0)),
-        ],
-        out_specs=[
-            pl.BlockSpec((rows, half), lambda i: (0, 0)),
-            pl.BlockSpec((rows, half), lambda i: (0, 0)),
-            pl.BlockSpec((ranks,) + PACK, lambda i: (0, 0, 0)),
-        ],
-        out_shape=[
-            jax.ShapeDtypeStruct((rows, half), BF16),
-            jax.ShapeDtypeStruct((rows, half), BF16),
-            jax.ShapeDtypeStruct((ranks,) + PACK, F32),
-        ],
+        in_specs=[anywhere] * 4 + [vmem],
+        out_specs=[vmem] * 3,
+        out_shape=[half_rows, half_rows, jax.ShapeDtypeStruct((ranks,) + PACK, F32)],
         scratch_shapes=[
-            pltpu.VMEM((rows, half), F32),
-            pltpu.VMEM((rows, half), F32),
-            pltpu.VMEM((1, half), F32),
+            pltpu.VMEM((2 * rows, half), BF16),
+            pltpu.VMEM((ranks * far_rows, width), BF16),
+            pltpu.VMEM((2 * rows, half), F32),
+            pltpu.VMEM((2 * rows, half), F32),
+            pltpu.VMEM((2, rows, half), F32),
+            pltpu.VMEM((2, rows, half), F32),
+            pltpu.SemaphoreType.DMA((4,)),
         ],
         compiler_params=params,
         cost_estimate=pl.CostEstimate(

time: 104 us -> 99.8 us (0.960)
  local copies, waits for them, and re-layouts: 15.6 us -> 1.81 us
  Pallas kernels: 35.8 us -> 45.8 us
    unnamed x54 -> x14, local copies, waits for them, and re-layouts: 15.6 us -> 1.81 us
    pallas_call x3, Pallas kernels: 15.8 us -> 22.3 us  [the longest x1 10.5 us: on_device(): pl.pallas_call(functools.partial(far_kernel, head_width=head_width), in_s...]
    pallas_call x1, Pallas kernels: 4 us -> 6.41 us  [on_device(): pl.pallas_call(functools.partial(own_kernel, head_width=head_width, score...]
    pallas_call x1, Pallas kernels: 12.7 us -> 13.9 us  [on_device(): pl.pallas_call(functools.partial(near_kernel, head_width=head_width, scor...]
  transfers between devices with their start and end apart: 5 -> 5, of which waited for: 1 -> 1; matrix products, arithmetic and copies ran while one was open for 3% -> 3% of each run, Pallas kernels for 21% -> 28%
where the time goes in v4:
time: 99.8 us; the launch traced here: 99.3 us
  Pallas kernels  45.8 us (46%)
  starting transfers between devices  25.3 us (25%)
  blocking collectives  19.3 us (19%)
  matrix products  3.02 us (3%)
  between operations  2.07 us (2%)
  waiting for transfers between devices  2.06 us (2%)
  local copies, waits for them, and re-layouts  1.81 us (2%)
    all_to_all x1, blocking collectives, on_device(): sums = lax.all_to_all(sums, SEQ_AXES, 0, 0, tiled=True)  19.3 us
    pallas_call x1, Pallas kernels, on_device(): pl.pallas_call(functools.partial(near_kernel, head_width=head_width, scor...  13.9 us
    pallas_call x1, Pallas kernels, on_device(): pl.pallas_call(functools.partial(far_kernel, head_width=head_width), in_s...  10.5 us
    ppermute x3, starting transfers between devices, swap_with(): lax.ppermute(x, axis, [(i, i ^ 1) for i in range(lax.axis_size(axis))])  9.83 us
    all_to_all x1, starting transfers between devices, on_device(): everyone = lax.all_to_all(packed, 'slide', 0, 0, tiled=True)  8.79 us
    all_to_all x1, starting transfers between devices, on_device(): lax.all_to_all(payload, ('x', 'y'), 0, 0, tiled=True)  6.64 us
    pallas_call x1, Pallas kernels, on_device(): pl.pallas_call(functools.partial(own_kernel, head_width=head_width, score...  6.41 us
    pallas_call x1, Pallas kernels, on_device(): pl.pallas_call(embed_kernel, in_specs=[anywhere, anywhere, vmem], out_spe...  6.22 us
  transfers between devices with their start and end apart: 5, of which 1 were waited for; matrix products, arithmetic and copies ran while one was open for 3% of the time, Pallas kernels for 28%

profile of v4, /device:TPU:1, one launch (start us, length us, event | category | flops | bytes accessed | tf_op | source)
XLA Modules:
  0.0 99.3 jit_solution(10103216175373578005)
XLA Ops:
  0.6 6.2 %embed.1 = (bf16[512,768]{1,0:T(8,128)(2,1)}, bf16[512,768]{1,0:T(8,128)(2,1)}, f32[1,768]{1,0:T(1,128)}) custom-call(bf16[512,1536]{1,0:T(8,128)(2,1)} %bitcast.8, bf16[1536,768]{1,0:T(8,128)(2,1)} %w_hbm.1, f32[768]{0:T(1024)} %gain_ref.1), custom_call_target="tpu_custom_call" | custom-call | tf_op jit(solution)/shard_map/embed/pallas_call | solution.py:380
  6.9 2.2 %collective-permute-start = (bf16[512,768]{1,0:T(8,128)(2,1)}, bf16[512,768]{1,0:T(8,128)(2,1)S(1)}, u32[]{:S(2)}, u32[]{:S(2)}) collective-permute-start(bf16[512,768]{1,0:T(8,128)(2,1)} %get-tuple-element.27.x_hbm), channel_id=1, source_target_pairs={{0,8},{8,0},{16,24},{24,16},{1,9},{9,1},{17,25},{25,17},{2,10},{10... | collective-permute-start | bytes 2359304 | tf_op jit(solution)/shard_map/ppermute | solution.py:27
  9.1 5.5 %own_rows.1 = (bf16[2,16,768]{2,1,0:T(8,128)(2,1)}, bf16[512,384]{1,0:T(8,128)(2,1)}, bf16[512,384]{1,0:T(8,128)(2,1)}) custom-call(s32[1]{0:T(128)} %bitcast.part_ref, s32[16]{0:T(128)} %offset_ref.1, bf16[512,768]{1,0:T(8,128)(2,1)} %get-tuple-element.27.x_hbm, bf16[768,768]{1,0:T(8,128)(2,1)} %wk_hbm.3, bf16[768,768]{1,0:T(8,128)(2,1)} %wv_hbm.3), custom_call_target="tpu_custom_call" | custom-call | tf_op jit(solution)/shard_map/own_rows/pallas_call | solution.py:403
  14.6 7.0 %collective-permute-start.1 = (bf16[2,16,768]{2,1,0:T(8,128)(2,1)}, bf16[2,16,768]{2,1,0:T(8,128)(2,1)S(1)}, u32[]{:S(2)}, u32[]{:S(2)}) collective-permute-start(bf16[2,16,768]{2,1,0:T(8,128)(2,1)} %get-tuple-element.34.own_ref), channel_id=1, source_target_pairs={{0,32},{32,0},{1,33},{33,1},{2,34},{34,2},{3,35},{35,3},{4,36},{36... | collective-permute-start | bytes 147464 | tf_op jit(solution)/shard_map/ppermute | solution.py:27
  21.6 0.0 copy-start.2
  21.6 6.4 %own_attention.1 = (bf16[512,384]{1,0:T(8,128)(2,1)}, f32[512,384]{1,0:T(8,128)}, f32[512,384]{1,0:T(8,128)}) custom-call(s32[1]{0:T(128)} %bitcast.part_ref, bf16[512,768]{1,0:T(8,128)(2,1)} %get-tuple-element.27.x_hbm, bf16[768,768]{1,0:T(8,128)(2,1)} %wq_hbm.3, bf16[512,384]{1,0:T(8,128)(2,1)} %get-tuple-element.28.k_hbm, ...), custom_call_target="tpu_custom_call" | custom-call | flops 3000000000 | bytes 4000000 | tf_op jit(solution)/shard_map/own_attention/pallas_call | solution.py:434
  28.1 0.0 collective-permute-done.1.other_ref
  28.1 0.0 copy-done.2
  28.1 1.0 payload.1
  29.0 6.6 %all-to-all-start = ((bf16[16,32,768]{2,1,0:T(8,128)(2,1)}), bf16[16,32,768]{2,1,0:T(8,128)(2,1)S(1)}, u32[]{:S(2)}, u32[]{:S(2)}) async-start(bf16[16,32,768]{2,1,0:T(8,128)(2,1)} %bitcast.2), calls=%async_computation | async-start | bytes 1572864 | tf_op jit(solution)/shard_map/all_to_all | solution.py:430
  35.7 0.0 collective-permute-done.other_hbm
  35.7 0.0 copy-start.6
  35.7 0.9 copy-done.6
  36.6 13.9 %near_attention.1 = (bf16[1024,384]{1,0:T(8,128)(2,1)}, f32[1024,384]{1,0:T(8,128)}, f32[1024,384]{1,0:T(8,128)}) custom-call(s32[1]{0:T(128)} %bitcast.part_ref, bf16[512,768]{1,0:T(8,128)(2,1)} %copy-done.6, bf16[512,384]{1,0:T(8,128)(2,1)} %get-tuple-element.28.k_hbm, bf16[512,384]{1,0:T(8,128)(2,1)} %get-tuple-element.29.v_hbm, ...), custom_call_target="tpu_custom_call" | custom-call | flops 8999999488 | bytes 8000000 | tf_op jit(solution)/shard_map/near_attention/pallas_call | solution.py:459
  50.5 0.0 all-to-all-done
  50.5 0.0 copy-start.4
  50.5 0.9 copy-done.4
  51.4 0.0 copy-start
  51.4 10.5 %far_attention.1 = (bf16[512,384]{1,0:T(8,128)(2,1)}, bf16[512,384]{1,0:T(8,128)(2,1)}, f32[32,8,256]{2,1,0:T(8,128)}) custom-call(bf16[1024,384]{1,0:T(8,128)(2,1)} %get-tuple-element.33.q_hbm, bf16[512,768]{1,0:T(8,128)(2,1)} %bitcast.9, f32[1024,384]{1,0:T(8,128)} %get-tuple-element.35.near_hbm, f32[1024,384]{1,0:T(8,128)} %get-tuple-element.36.near_lse_hbm, ...), custom_call_target="tpu_custom_call" | custom-call | flops 6000000000 | bytes 6000000 | tf_op jit(solution)/shard_map/far_attention/pallas_call | solution.py:485
  61.9 0.0 copy-start.5
  61.9 19.3 %all_to_all.15.sums_ref = f32[32,8,256]{2,1,0:T(8,128)S(1)} all-to-all(f32[32,8,256]{2,1,0:T(8,128)} %get-tuple-element.38), channel_id=1, replica_groups=mesh['x'=4,'z_hi'=2,'y'=4,'slide'=8] {'x','z_hi','y'}, dimensions={0} | all-to-all | bytes 524288 | tf_op jit(solution)/shard_map/all_to_all | solution.py:506
  81.3 0.6 collective-permute-start.2
  83.2 0.0 copy-done
  83.2 0.0 copy-done.1
  83.2 0.0 copy-done.3
  83.2 1.3 %pooled.1 = (f32[1,768]{1,0:T(1,128)}, f32[8,8,256]{2,1,0:T(8,128)}) custom-call(s32[1]{0:T(128)S(6)} %copy.16.slide_code_ref, s32[1]{0:T(128)S(6)} %copy.17.report_code_ref, f32[32,8,256]{2,1,0:T(8,128)S(1)} %all_to_all.15.sums_ref, bf16[768,768]{1,0:T(8,128)(2,1)S(1)} %copy-done.1, bf16[768,768]{1,0:T(8,128)(2,1)S(1)} %copy-done, bf16[1,768]{1,0:T(2,128)(2,1)S(1)} %copy-done.3), custom_call_target="tpu_custom_call" | custom-call | tf_op jit(solution)/shard_map/pooled/pallas_call | solution.py:518
  84.5 8.8 %all-to-all-start.2 = ((f32[8,8,256]{2,1,0:T(8,128)}), f32[8,8,256]{2,1,0:T(8,128)S(1)}, u32[]{:S(2)}, u32[]{:S(2)}) async-start(f32[8,8,256]{2,1,0:T(8,128)} %get-tuple-element.41), calls=%async_computation.2 | async-start | bytes 131072 | tf_op jit(solution)/shard_map/all_to_all | solution.py:528
  93.3 0.0 collective-permute-done.2
  93.3 0.0 copy-done.5
  93.3 3.0 %fusion = bf16[1,512,768]{2,1,0:T(8,128)(2,1)} fusion(bf16[768,768]{1,0:T(8,128)(2,1)S(1)} %copy-done.1, bf16[512,768]{1,0:T(8,128)(2,1)S(1)} %copy-done.5, bf16[512,384]{1,0:T(8,128)(2,1)} %get-tuple-element.44, bf16[512,384]{1,0:T(8,128)(2,1)} %collective-permute-done.2, pred[]{:T(512)S(6)} %eq.5), kind=kOutput, calls=%fused_computation.1 | convolution fusion | flops 608698368 | bytes 3538945 | tf_op jit(solution)/shard_map/dot_general | solution.py:514
  96.3 2.0 %all-to-all-done.2.all_ref = f32[8,8,256]{2,1,0:T(8,128)S(1)} async-done(((f32[8,8,256]{2,1,0:T(8,128)}), f32[8,8,256]{2,1,0:T(8,128)S(1)}, u32[]{:S(2)}, u32[]{:S(2)}) %all-to-all-start.2) | async-done | bytes 65568 | tf_op jit(solution)/shard_map/all_to_all | solution.py:528
  98.4 1.0 contrast.1
  (2 shorter events, 0.0 us)
Async XLA Ops:
  6.9 28.8 %collective-permute-start = (bf16[512,768]{1,0:T(8,128)(2,1)}, bf16[512,768]{1,0:T(8,128)(2,1)S(1)}, u32[]{:S(2)}, u32[]{:S(2)}) collective-permute-start(bf16[512,768]{1,0:T(8,128)(2,1)} %get-tuple-element.27.x_hbm), channel_id=1, source_target_pairs={{0,8},{8,0},{16,24},{24,16},{1,9},{9,1},{17,25},{25,17},{2,10},{10... | collective-permute-start | bytes 2359304 | tf_op jit(solution)/shard_map/ppermute | solution.py:27
  14.6 13.4 %collective-permute-start.1 = (bf16[2,16,768]{2,1,0:T(8,128)(2,1)}, bf16[2,16,768]{2,1,0:T(8,128)(2,1)S(1)}, u32[]{:S(2)}, u32[]{:S(2)}) collective-permute-start(bf16[2,16,768]{2,1,0:T(8,128)(2,1)} %get-tuple-element.34.own_ref), channel_id=1, source_target_pairs={{0,32},{32,0},{1,33},{33,1},{2,34},{34,2},{3,35},{35,3},{4,36},{36... | collective-permute-start | bytes 147464 | tf_op jit(solution)/shard_map/ppermute | solution.py:27
  21.6 6.4 %copy-start.2 = (bf16[2,16,768]{2,1,0:T(8,128)(2,1)S(1)}, bf16[2,16,768]{2,1,0:T(8,128)(2,1)}, u32[]{:S(2)}) copy-start(bf16[2,16,768]{2,1,0:T(8,128)(2,1)} %get-tuple-element.34.own_ref) | copy-start | bytes 147460
  29.0 21.5 %all-to-all-start = ((bf16[16,32,768]{2,1,0:T(8,128)(2,1)}), bf16[16,32,768]{2,1,0:T(8,128)(2,1)S(1)}, u32[]{:S(2)}, u32[]{:S(2)}) async-start(bf16[16,32,768]{2,1,0:T(8,128)(2,1)} %bitcast.2), calls=%async_computation | async-start | bytes 1572864 | tf_op jit(solution)/shard_map/all_to_all | solution.py:430
  35.7 0.9 copy-start.6
  50.5 0.9 copy-start.4
  51.4 31.8 %copy-start = (bf16[768,768]{1,0:T(8,128)(2,1)S(1)}, bf16[768,768]{1,0:T(8,128)(2,1)}, u32[]{:S(2)}) copy-start(bf16[768,768]{1,0:T(8,128)(2,1)} %w_head_ref.1) | copy-start | bytes 3538948
  51.4 31.8 %copy-start.1 = (bf16[768,768]{1,0:T(8,128)(2,1)S(1)}, bf16[768,768]{1,0:T(8,128)(2,1)}, u32[]{:S(2)}) copy-start(bf16[768,768]{1,0:T(8,128)(2,1)} %w_out_ref.1) | copy-start | bytes 3538948
  51.4 31.8 %copy-start.3 = (bf16[1,768]{1,0:T(2,128)(2,1)S(1)}, bf16[1,768]{1,0:T(2,128)(2,1)}, u32[]{:S(2)}) copy-start(bf16[1,768]{1,0:T(2,128)(2,1)} %report_ref.1) | copy-start | bytes 4612
  61.9 31.4 %copy-start.5 = (bf16[512,768]{1,0:T(8,128)(2,1)S(1)}, bf16[512,768]{1,0:T(8,128)(2,1)}, u32[]{:S(2)}) copy-start(bf16[512,768]{1,0:T(8,128)(2,1)} %get-tuple-element.42) | copy-start | bytes 2359300
  81.3 12.0 %collective-permute-start.2 = (bf16[512,384]{1,0:T(8,128)(2,1)}, bf16[512,384]{1,0:T(8,128)(2,1)}, u32[]{:S(2)}, u32[]{:S(2)}) collective-permute-start(bf16[512,384]{1,0:T(8,128)(2,1)} %get-tuple-element.43), channel_id=1, source_target_pairs={{0,8},{8,0},{16,24},{24,16},{1,9},{9,1},{17,25},{25,17},{2,10},{10... | collective-permute-start | bytes 1179656 | tf_op jit(solution)/shard_map/ppermute | solution.py:27
  84.5 13.9 %all-to-all-start.2 = ((f32[8,8,256]{2,1,0:T(8,128)}), f32[8,8,256]{2,1,0:T(8,128)S(1)}, u32[]{:S(2)}, u32[]{:S(2)}) async-start(f32[8,8,256]{2,1,0:T(8,128)} %get-tuple-element.41), calls=%async_computation.2 | async-start | bytes 131072 | tf_op jit(solution)/shard_map/all_to_all | solution.py:528

commit v5 on v4

--- a/solution.py
+++ b/solution.py
@@ -17,7 +17,8 @@
 NN = (((1,), (0,)), ((), ()))
 SMALL_VMEM = 16 << 20
 LARGE_VMEM = 58 << 20
-EMBED_STEPS = 6
+EMBED_STEPS = 2
+EMBED_VMEM = 59 << 20
 SEQ_AXES = ("x", "z_hi", "y")
 F32 = jnp.float32
 BF16 = jnp.bfloat16
@@ -73,65 +74,51 @@
     return copies
 
 
-def embed_kernel(x_hbm, w_hbm, gain_ref, embedded_hbm, normed_hbm, sum_ref, x_scr, w_scr,
-                 embedded_scr, normed_scr, sems, out_sems):
-    depth = x_scr.shape[2]
-    halves = 2
-    part_rows, part_depth = x_scr.shape[1] // halves, depth // halves
-    copies = []
-    for step in range(EMBED_STEPS):
-        group = []
-        for i in range(halves):
-            rows = slice(i * part_rows, (i + 1) * part_rows)
-            group.append(
-                pltpu.make_async_copy(
-                    x_hbm.at[rows, step * depth : (step + 1) * depth],
-                    x_scr.at[step, rows, :],
-                    sems.at[step, i],
+def embed_kernel(x_hbm, w_hbm, gain_ref, embedded_hbm, normed_ref, sum_ref, x_scr, w_scr,
+                 embedded_scr, x_sems, w_sems, out_sems):
+    rows = x_scr.shape[0] // EMBED_STEPS
+    spans = [pl.ds(step * rows, rows) for step in range(EMBED_STEPS)]
+    pieces = w_sems.shape[0]
+    depth = w_scr.shape[0] // pieces
+    parts = [pl.ds(i * depth, depth) for i in range(pieces)]
+    x_loads = started([x_hbm.at[spans[0]]], [x_scr.at[spans[0]]], x_sems)
+    w_loads = started([w_hbm.at[p] for p in parts], [w_scr.at[p] for p in parts], w_sems)
+    x_loads += started(
+        [x_hbm.at[span] for span in spans[1:]], [x_scr.at[span] for span in spans[1:]], x_sems, 1
+    )
+    stores = []
+    summed = jnp.zeros(sum_ref.shape, F32)
+    for step, span in enumerate(spans):
+        x_loads[step].wait()
+        if step == 0:
+            total = None
+            for piece, load in enumerate(w_loads):
+                load.wait()
+                columns = slice(piece * depth, (piece + 1) * depth)
+                product = jnp.dot(
+                    x_scr[span, columns], w_scr[parts[piece], :], preferred_element_type=F32
                 )
-            )
-            first = step * depth + i * part_depth
-            group.append(
-                pltpu.make_async_copy(
-                    w_hbm.at[first : first + part_depth, :],
-                    w_scr.at[step, i * part_depth : (i + 1) * part_depth, :],
-                    sems.at[step, halves + i],
-                )
-            )
-        for copy in group:
-            copy.start()
-        copies.append(group)
-    total = None
-    for step, group in enumerate(copies):
-        for copy in group:
-            copy.wait()
-        product = jnp.dot(x_scr[step], w_scr[step], preferred_element_type=F32)
-        total = product if total is None else total + product
-    embedded = total.astype(BF16)
-    embedded_scr[...] = embedded
-    stores = started((embedded_scr,), (embedded_hbm,), out_sems)
-    floats = embedded.astype(F32)
-    centred = floats - jnp.mean(floats, axis=1, keepdims=True)
-    spread = jnp.mean(centred * centred, axis=1, keepdims=True)
-    normed = centred * lax.rsqrt(spread + NORM_EPS) * gain_ref[...][None, :]
-    normed_scr[...] = normed.astype(BF16)
-    stores += started((normed_scr,), (normed_hbm,), out_sems, 1)
-    sum_ref[...] = jnp.sum(floats, axis=0, keepdims=True)
+                total = product if total is None else total + product
+        else:
+            total = jnp.dot(x_scr[span, :], w_scr[...], preferred_element_type=F32)
+        embedded = total.astype(BF16)
+        embedded_scr[span, :] = embedded
+        stores += started([embedded_scr.at[span]], [embedded_hbm.at[span]], out_sems, step)
+        floats = embedded.astype(F32)
+        centred = floats - jnp.mean(floats, axis=1, keepdims=True)
+        spread = jnp.mean(centred * centred, axis=1, keepdims=True)
+        normed = centred * lax.rsqrt(spread + NORM_EPS) * gain_ref[...][None, :]
+        normed_ref[span, :] = normed.astype(BF16)
+        summed += jnp.sum(floats, axis=0, keepdims=True)
+    sum_ref[...] = summed
     for store in stores:
         store.wait()
 
 
-def own_rows_kernel(part_ref, offset_ref, x_hbm, wk_hbm, wv_hbm, far_ref, k_out, v_out,
-                    x_scr, w_scr, half_scr, sems, out_sems):
-    rows, width = x_scr.shape
+def own_rows_kernel(part_ref, offset_ref, x_ref, wk_ref, wv_ref, far_ref, k_ref, v_ref):
+    rows, width = x_ref.shape
     half = width // 2
     heads = offset_ref.shape[0]
-    spans = (pl.ds(0, half), pl.ds(half, half))
-    loads = started(
-        [x_hbm] + [wk_hbm.at[span] for span in spans] + [wv_hbm.at[span] for span in spans],
-        [x_scr] + [w_scr.at[0, span] for span in spans] + [w_scr.at[1, span] for span in spans],
-        sems,
-    )
     lane = lax.broadcasted_iota(jnp.int32, (1, width), 1)
     lane_offset = jnp.zeros((1, width), jnp.int32)
     for head in range(heads):
@@ -139,22 +126,15 @@
     phase = lax.broadcasted_iota(jnp.int32, (RATE, width), 0)
     chosen = jnp.where(phase == lane_offset, 1.0, 0.0)
     upper = part_ref[0] == 1
-    loads[0].wait()
-    stores = []
-    for place, half_out in enumerate((k_out, v_out)):
-        loads[1 + 2 * place].wait()
-        loads[2 + 2 * place].wait()
-        full = jnp.dot(x_scr[...], w_scr[place], preferred_element_type=F32)
-        half_scr[place] = jnp.where(upper, full[:, half:], full[:, :half]).astype(BF16)
-        stores += started((half_scr.at[place],), (half_out,), out_sems, place)
+    for place, (w_ref, half_ref) in enumerate(((wk_ref, k_ref), (wv_ref, v_ref))):
+        full = jnp.dot(x_ref[...], w_ref[...], preferred_element_type=F32)
+        half_ref[...] = jnp.where(upper, full[:, half:], full[:, :half]).astype(BF16)
         grouped = full.reshape(rows // RATE, RATE, width) * chosen[None]
         picked = jnp.sum(grouped, axis=1).astype(BF16)
         for part in range(2):
             far_ref[part, :, place * half : (place + 1) * half] = picked[
                 :, part * half : (part + 1) * half
             ]
-    for store in stores:
-        store.wait()
 
 
 def payload_kernel(own_ref, other_ref, out_ref):
@@ -167,20 +147,15 @@
     return w_hbm.at[:, pl.ds(pl.multiple_of(part_ref[0] * half, half), half)]
 
 
-def own_kernel(part_ref, x_hbm, wq_hbm, k_hbm, v_hbm, q_out, mixed_out, lse_out,
-               x_scr, wq_scr, k_scr, v_scr, q_scr, mixed_scr, lse_scr, in_sems, out_sems,
-               *, head_width, score_scale):
-    loads = started(
-        (x_hbm, half_columns(wq_hbm, part_ref), k_hbm, v_hbm), (x_scr, wq_scr, k_scr, v_scr), in_sems
-    )
-    loads[0].wait()
-    loads[1].wait()
-    q = jnp.dot(x_scr[...], wq_scr[...], preferred_element_type=F32) * score_scale
+def own_kernel(part_ref, x_ref, wq_ref, k_ref, v_ref, q_out, mixed_out, lse_out,
+               q_scr, mixed_scr, lse_scr, out_sems, *, head_width, score_scale):
+    half = wq_ref.shape[1] // 2
+    upper = part_ref[0] == 1
+    wq = jnp.where(upper, wq_ref[:, half:], wq_ref[:, :half])
+    q = jnp.dot(x_ref[...], wq, preferred_element_type=F32) * score_scale
     q_scr[...] = q.astype(BF16)
     stores = started((q_scr,), (q_out,), out_sems)
-    loads[2].wait()
-    loads[3].wait()
-    attend(q_scr[...], k_scr[...], v_scr[...], head_width, mixed_scr, lse_scr, slice(None))
+    attend(q_scr[...], k_ref[...], v_ref[...], head_width, mixed_scr, lse_scr, slice(None))
     stores += started((mixed_scr, lse_scr), (mixed_out, lse_out), out_sems, 1)
     for store in stores:
         store.wait()
@@ -283,12 +258,11 @@
     return row * lax.rsqrt(jnp.sum(row * row, axis=1, keepdims=True) + 1e-06)
 
 
-def pooled_kernel(slide_code_ref, report_code_ref, sums_ref, w_out_ref, w_head_ref, report_ref,
+def pooled_kernel(codes_ref, sums_ref, w_out_ref, w_head_ref, report_ref,
                   unit_ref, pack_ref, *, length):
     peers = sums_ref.shape[0]
     width = w_out_ref.shape[0]
     half = width // 2
-    lanes = PACK[1]
     even = sums_ref[0]
     odd = sums_ref[1]
     for peer in range(2, peers, 2):
@@ -306,13 +280,7 @@
     pooled = (embedded_sum + exact_row_times(attended_sum, w_out_ref[...])) * (1.0 / length)
     unit = unit_row(exact_row_times(pooled, w_head_ref[...]))
     unit_ref[...] = unit
-    lane = lax.broadcasted_iota(jnp.int32, (1, 2 * lanes), 1)
-    codes = jnp.where(
-        lane == 0,
-        slide_code_ref[0].astype(F32),
-        jnp.where(lane == 1, report_code_ref[0].astype(F32), 0.0),
-    )
-    packed = pack_row((unit, unit_row(report_ref[...].astype(F32)), codes))
+    packed = pack_row((unit, unit_row(report_ref[...].astype(F32)), codes_ref[...]))
     pack_ref[...] = jnp.broadcast_to(packed[None], pack_ref.shape)
 
 
@@ -376,25 +344,25 @@
     vmem = pl.BlockSpec(memory_space=pltpu.VMEM)
     anywhere = pl.BlockSpec(memory_space=pl.ANY)
 
-    depth = in_width // EMBED_STEPS
+    pieces = 3
     embedded, normed, embedded_sum = pl.pallas_call(
         embed_kernel,
         in_specs=[anywhere, anywhere, vmem],
-        out_specs=[anywhere, anywhere, vmem],
+        out_specs=[anywhere, vmem, vmem],
         out_shape=[
             jax.ShapeDtypeStruct((rows, width), BF16),
-            jax.ShapeDtypeStruct((rows, width), BF16),
+            pltpu.VMEM((rows, width), BF16),
             jax.ShapeDtypeStruct((1, width), F32),
         ],
         scratch_shapes=[
-            pltpu.VMEM((EMBED_STEPS, rows, depth), BF16),
-            pltpu.VMEM((EMBED_STEPS, depth, width), BF16),
+            pltpu.VMEM((rows, in_width), BF16),
+            pltpu.VMEM((in_width, width), BF16),
             pltpu.VMEM((rows, width), BF16),
-            pltpu.VMEM((rows, width), BF16),
-            pltpu.SemaphoreType.DMA((EMBED_STEPS, 4)),
-            pltpu.SemaphoreType.DMA((2,)),
-        ],
-        compiler_params=pltpu.CompilerParams(vmem_limit_bytes=LARGE_VMEM),
+            pltpu.SemaphoreType.DMA((EMBED_STEPS,)),
+            pltpu.SemaphoreType.DMA((pieces,)),
+            pltpu.SemaphoreType.DMA((EMBED_STEPS,)),
+        ],
+        compiler_params=pltpu.CompilerParams(vmem_limit_bytes=EMBED_VMEM),
         name="embed",
     )(tiles.reshape(rows, in_width), w_embed, attn_gain)
     other_normed = swap_with(normed, "y")
@@ -402,21 +370,14 @@
     far_rows = rows // RATE
     far_own, keys_own, values_own = pl.pallas_call(
         own_rows_kernel,
-        in_specs=[smem, smem, anywhere, anywhere, anywhere],
-        out_specs=[vmem, anywhere, anywhere],
+        in_specs=[smem, smem, vmem, vmem, vmem],
+        out_specs=[vmem, vmem, vmem],
         out_shape=[
             jax.ShapeDtypeStruct((2, far_rows, width), BF16),
             jax.ShapeDtypeStruct((rows, half), BF16),
             jax.ShapeDtypeStruct((rows, half), BF16),
         ],
-        scratch_shapes=[
-            pltpu.VMEM((rows, width), BF16),
-            pltpu.VMEM((2, width, width), BF16),
-            pltpu.VMEM((2, rows, half), BF16),
-            pltpu.SemaphoreType.DMA((5,)),
-            pltpu.SemaphoreType.DMA((2,)),
-        ],
-        compiler_params=params,
+        compiler_params=small,
         name="own_rows",
     )(parts, head_offset, normed, w_key, w_value)
     far_other = swap_with(far_own, "z_hi")
@@ -430,24 +391,22 @@
     far = lax.all_to_all(payload, ("x", "y"), 0, 0, tiled=True).reshape(ranks * far_rows, width)
 
     half_rows = jax.ShapeDtypeStruct((rows, half), BF16)
-    half_state = jax.ShapeDtypeStruct((rows, half), F32)
     queries_own, own_mixed, own_lse = pl.pallas_call(
         functools.partial(own_kernel, head_width=head_width, score_scale=score_scale),
-        in_specs=[smem] + [anywhere] * 4,
+        in_specs=[smem] + [vmem] * 4,
         out_specs=[anywhere] * 3,
-        out_shape=[half_rows, half_state, half_state],
+        out_shape=[
+            pltpu.HBM((rows, half), BF16),
+            pltpu.HBM((rows, half), F32),
+            pltpu.HBM((rows, half), F32),
+        ],
         scratch_shapes=[
-            pltpu.VMEM((rows, width), BF16),
-            pltpu.VMEM((width, half), BF16),
-            pltpu.VMEM((rows, half), BF16),
-            pltpu.VMEM((rows, half), BF16),
             pltpu.VMEM((rows, half), BF16),
             pltpu.VMEM((rows, half), F32),
             pltpu.VMEM((rows, half), F32),
-            pltpu.SemaphoreType.DMA((4,)),
             pltpu.SemaphoreType.DMA((3,)),
         ],
-        compiler_params=params,
+        compiler_params=pltpu.CompilerParams(vmem_limit_bytes=32 << 20),
         cost_estimate=pl.CostEstimate(
             flops=3_000_000_000, bytes_accessed=4_000_000, transcendentals=2_000_000
         ),
@@ -514,17 +473,20 @@
     encoded = embedded.astype(F32) + jnp.dot(joined, w_out, preferred_element_type=F32)
     encoded = encoded.astype(BF16).reshape(1, rows, width)
 
+    lane = jnp.arange(2 * PACK[1], dtype=jnp.int32)[None, :]
+    codes = jnp.where(lane == 0, slide_code[:, None], jnp.where(lane == 1, report_code[:, None], 0))
+    codes = codes.astype(F32)
     slides = lax.axis_size("slide")
     slide_unit_vectors, packed = pl.pallas_call(
         functools.partial(pooled_kernel, length=rows * ranks),
-        in_specs=[smem, smem, vmem, vmem, vmem, vmem],
+        in_specs=[vmem] * 5,
         out_shape=[
             jax.ShapeDtypeStruct((1, width), F32),
             jax.ShapeDtypeStruct((slides,) + PACK, F32),
         ],
         compiler_params=small,
         name="pooled",
-    )(slide_code, report_code, sums, w_out, w_head, report_emb)
+    )(codes, sums, w_out, w_head, report_emb)
     everyone = lax.all_to_all(packed, "slide", 0, 0, tiled=True)
     everyone, encoded = lax.optimization_barrier((everyone, encoded))
     logits, loss = pl.pallas_call(

time: 99.8 us -> 95 us (0.952)
  Pallas kernels: 45.8 us -> 40.6 us
  blocking collectives: 19.3 us -> 21.5 us
    pallas_call x1, Pallas kernels: 5.55 us -> 2 us  [on_device(): pl.pallas_call(own_rows_kernel, in_specs=[smem, smem, vmem, vmem, vmem],...]
    all_to_all x1, blocking collectives: 19.3 us -> 21.5 us  [on_device(): sums = lax.all_to_all(sums, SEQ_AXES, 0, 0, tiled=True)]
    pallas_call x1, Pallas kernels: 6.41 us -> 4.9 us  [on_device(): pl.pallas_call(functools.partial(own_kernel, head_width=head_width, score...]
  transfers between devices with their start and end apart: 5 -> 5, of which waited for: 1 -> 1; matrix products, arithmetic and copies ran while one was open for 3% -> 3% of each run, Pallas kernels for 28% -> 24%
where the time goes in v5:
time: 95 us; the launch traced here: 94.6 us
  Pallas kernels  40.6 us (43%)
  starting transfers between devices  24.4 us (26%)
  blocking collectives  21.5 us (23%)
  matrix products  3.02 us (3%)
  between operations  2.12 us (2%)
  waiting for transfers between devices  2.06 us (2%)
    all_to_all x1, blocking collectives, on_device(): sums = lax.all_to_all(sums, SEQ_AXES, 0, 0, tiled=True)  21.5 us
    pallas_call x1, Pallas kernels, on_device(): pl.pallas_call(functools.partial(near_kernel, head_width=head_width, scor...  13.9 us
    pallas_call x1, Pallas kernels, on_device(): pl.pallas_call(functools.partial(far_kernel, head_width=head_width), in_s...  10.5 us
    ppermute x3, starting transfers between devices, swap_with(): lax.ppermute(x, axis, [(i, i ^ 1) for i in range(lax.axis_size(axis))])  9.88 us
    all_to_all x1, starting transfers between devices, on_device(): everyone = lax.all_to_all(packed, 'slide', 0, 0, tiled=True)  7.84 us
    all_to_all x1, starting transfers between devices, on_device(): lax.all_to_all(payload, ('x', 'y'), 0, 0, tiled=True)  6.64 us
    pallas_call x1, Pallas kernels, on_device(): pl.pallas_call(embed_kernel, in_specs=[anywhere, anywhere, vmem], out_spe...  6.02 us
    pallas_call x1, Pallas kernels, on_device(): pl.pallas_call(functools.partial(own_kernel, head_width=head_width, score...  4.9 us
  transfers between devices with their start and end apart: 5, of which 1 were waited for; matrix products, arithmetic and copies ran while one was open for 3% of the time, Pallas kernels for 24%

profile of v5, /device:TPU:1, one launch (start us, length us, event | category | flops | bytes accessed | tf_op | source)
XLA Modules:
  0.0 94.6 jit_solution(3503530676364444324)
XLA Ops:
  0.6 0.0 copy-start
  0.6 0.0 copy-start.1
  0.7 0.0 copy-start.5
  0.7 6.0 %embed.1 = (bf16[512,768]{1,0:T(8,128)(2,1)}, bf16[512,768]{1,0:T(8,128)(2,1)S(1)}, f32[1,768]{1,0:T(1,128)}) custom-call(bf16[512,1536]{1,0:T(8,128)(2,1)} %bitcast.12, bf16[1536,768]{1,0:T(8,128)(2,1)} %w_hbm.1, f32[768]{0:T(1024)} %gain_ref.1), custom_call_target="tpu_custom_call" | custom-call | tf_op jit(solution)/shard_map/embed/pallas_call | solution.py:348
  6.7 2.2 %collective-permute-start = (bf16[512,768]{1,0:T(8,128)(2,1)S(1)}, bf16[512,768]{1,0:T(8,128)(2,1)}, u32[]{:S(2)}, u32[]{:S(2)}) collective-permute-start(bf16[512,768]{1,0:T(8,128)(2,1)S(1)} %get-tuple-element.27.x_ref), channel_id=1, source_target_pairs={{0,8},{8,0},{16,24},{24,16},{1,9},{9,1},{17,25},{25,17},{2,10},{10... | collective-permute-start | bytes 2359304 | tf_op jit(solution)/shard_map/ppermute | solution.py:28
  8.9 0.0 copy-done
  8.9 0.0 copy-done.1
  8.9 0.0 copy-done.5
  8.9 2.0 %own_rows.1 = (bf16[2,16,768]{2,1,0:T(8,128)(2,1)S(1)}, bf16[512,384]{1,0:T(8,128)(2,1)S(1)}, bf16[512,384]{1,0:T(8,128)(2,1)S(1)}) custom-call(s32[1]{0:T(128)} %bitcast.2.part_ref, s32[16]{0:T(128)S(1)} %copy-done.5, bf16[512,768]{1,0:T(8,128)(2,1)S(1)} %get-tuple-element.27.x_ref, bf16[768,768]{1,0:T(8,128)(2,1)S(1)} %copy-done, ...), custom_call_target="tpu_custom_call" | custom-call | tf_op jit(solution)/shard_map/own_rows/pallas_call | solution.py:371
  10.9 0.0 copy-start.7
  10.9 0.0 copy-start.8
  10.9 7.0 %collective-permute-start.1 = (bf16[2,16,768]{2,1,0:T(8,128)(2,1)S(1)}, bf16[2,16,768]{2,1,0:T(8,128)(2,1)S(1)}, u32[]{:S(2)}, u32[]{:S(2)}) collective-permute-start(bf16[2,16,768]{2,1,0:T(8,128)(2,1)S(1)} %get-tuple-element.34.own_ref), channel_id=1, source_target_pairs={{0,32},{32,0},{1,33},{33,1},{2,34},{34,2},{3,35},{35,3},{4,36},{36... | collective-permute-start | bytes 147464 | tf_op jit(solution)/shard_map/ppermute | solution.py:28
  17.9 0.0 copy-done.6
  17.9 4.9 %own_attention.1 = (bf16[512,384]{1,0:T(8,128)(2,1)}, f32[512,384]{1,0:T(8,128)}, f32[512,384]{1,0:T(8,128)}) custom-call(s32[1]{0:T(128)} %bitcast.2.part_ref, bf16[512,768]{1,0:T(8,128)(2,1)S(1)} %get-tuple-element.27.x_ref, bf16[768,768]{1,0:T(8,128)(2,1)S(1)} %copy-done.6, bf16[512,384]{1,0:T(8,128)(2,1)S(1)} %get-tuple-element.28.k_ref.k_hbm, ...), custom_call_target="tpu_custom_call" | custom-call | flops 3000000000 | bytes 4000000 | tf_op jit(solution)/shard_map/own_attention/pallas_call | solution.py:394
  22.9 0.0 copy-done.7
  22.9 0.0 collective-permute-done.1.other_ref
  22.9 1.0 %payload.1 = bf16[8,2,2,16,768]{4,3,2,1,0:T(8,128)(2,1)} custom-call(bf16[2,16,768]{2,1,0:T(8,128)(2,1)S(1)} %get-tuple-element.34.own_ref, bf16[2,16,768]{2,1,0:T(8,128)(2,1)S(1)} %collective-permute-done.1.other_ref), custom_call_target="tpu_custom_call" | custom-call | tf_op jit(solution)/shard_map/payload/pallas_call | solution.py:384
  23.8 6.6 %all-to-all-start = ((bf16[16,32,768]{2,1,0:T(8,128)(2,1)}), bf16[16,32,768]{2,1,0:T(8,128)(2,1)S(1)}, u32[]{:S(2)}, u32[]{:S(2)}) async-start(bf16[16,32,768]{2,1,0:T(8,128)(2,1)} %bitcast.4), calls=%async_computation | async-start | bytes 1572864 | tf_op jit(solution)/shard_map/all_to_all | solution.py:391
  30.5 0.0 collective-permute-done.other_hbm
  30.5 13.9 %near_attention.1 = (bf16[1024,384]{1,0:T(8,128)(2,1)}, f32[1024,384]{1,0:T(8,128)}, f32[1024,384]{1,0:T(8,128)}) custom-call(s32[1]{0:T(128)} %bitcast.2.part_ref, bf16[512,768]{1,0:T(8,128)(2,1)} %collective-permute-done.other_hbm, bf16[512,384]{1,0:T(8,128)(2,1)} %copy-done.7, bf16[512,384]{1,0:T(8,128)(2,1)} %copy-done.8, ...), custom_call_target="tpu_custom_call" | custom-call | flops 8999999488 | bytes 8000000 | tf_op jit(solution)/shard_map/near_attention/pallas_call | solution.py:418
  44.4 0.0 all-to-all-done
  44.5 0.9 copy-done.9
  45.3 10.5 %far_attention.1 = (bf16[512,384]{1,0:T(8,128)(2,1)}, bf16[512,384]{1,0:T(8,128)(2,1)}, f32[32,8,256]{2,1,0:T(8,128)}) custom-call(bf16[1024,384]{1,0:T(8,128)(2,1)} %get-tuple-element.33.q_hbm, bf16[512,768]{1,0:T(8,128)(2,1)} %bitcast.13, f32[1024,384]{1,0:T(8,128)} %get-tuple-element.35.near_hbm, f32[1024,384]{1,0:T(8,128)} %get-tuple-element.36.near_lse_hbm, ...), custom_call_target="tpu_custom_call" | custom-call | flops 6000000000 | bytes 6000000 | tf_op jit(solution)/shard_map/far_attention/pallas_call | solution.py:444
  55.9 0.0 copy-start.10
  55.9 21.5 %all_to_all.15.sums_ref = f32[32,8,256]{2,1,0:T(8,128)S(1)} all-to-all(f32[32,8,256]{2,1,0:T(8,128)} %get-tuple-element.38), channel_id=1, replica_groups=mesh['x'=4,'z_hi'=2,'y'=4,'slide'=8] {'x','z_hi','y'}, dimensions={0} | all-to-all | bytes 524288 | tf_op jit(solution)/shard_map/all_to_all | solution.py:465
  77.4 0.7 collective-permute-start.2
  79.4 1.3 %pooled.1 = (f32[1,768]{1,0:T(1,128)}, f32[8,8,256]{2,1,0:T(8,128)}) custom-call(f32[1,512]{1,0:T(1,128)S(1)} %fusion.7.codes_ref, f32[32,8,256]{2,1,0:T(8,128)S(1)} %all_to_all.15.sums_ref, bf16[768,768]{1,0:T(8,128)(2,1)S(1)} %copy-done.3, bf16[768,768]{1,0:T(8,128)(2,1)S(1)} %copy-done.2, bf16[1,768]{1,0:T(2,128)(2,1)S(1)} %copy-done.4), custom_call_target="tpu_custom_call" | custom-call | tf_op jit(solution)/shard_map/pooled/pallas_call | solution.py:480
  80.7 7.8 %all-to-all-start.2 = ((f32[8,8,256]{2,1,0:T(8,128)}), f32[8,8,256]{2,1,0:T(8,128)S(1)}, u32[]{:S(2)}, u32[]{:S(2)}) async-start(f32[8,8,256]{2,1,0:T(8,128)} %get-tuple-element.41), calls=%async_computation.2 | async-start | bytes 131072 | tf_op jit(solution)/shard_map/all_to_all | solution.py:490
  88.5 0.0 collective-permute-done.2
  88.5 3.0 %fusion = bf16[1,512,768]{2,1,0:T(8,128)(2,1)} fusion(bf16[768,768]{1,0:T(8,128)(2,1)S(1)} %copy-done.3, bf16[512,768]{1,0:T(8,128)(2,1)S(1)} %copy-done.10, bf16[512,384]{1,0:T(8,128)(2,1)} %get-tuple-element.44, bf16[512,384]{1,0:T(8,128)(2,1)} %collective-permute-done.2, pred[]{:T(512)S(6)} %eq.37), kind=kOutput, calls=%fused_computation.1 | convolution fusion | flops 608698368 | bytes 3538945 | tf_op jit(solution)/shard_map/dot_general | solution.py:473
  91.6 2.0 %all-to-all-done.2.all_ref = f32[8,8,256]{2,1,0:T(8,128)S(1)} async-done(((f32[8,8,256]{2,1,0:T(8,128)}), f32[8,8,256]{2,1,0:T(8,128)S(1)}, u32[]{:S(2)}, u32[]{:S(2)}) %all-to-all-start.2) | async-done | bytes 65568 | tf_op jit(solution)/shard_map/all_to_all | solution.py:490
  93.6 1.0 %contrast.1 = (f32[8,8]{1,0:T(8,128)}, f32[1,1]{1,0:T(1,128)}) custom-call(f32[8,8,256]{2,1,0:T(8,128)S(1)} %all-to-all-done.2.all_ref), custom_call_target="tpu_custom_call" | custom-call | tf_op jit(solution)/shard_map/contrast/pallas_call | solution.py:492
  (11 shorter events, 0.0 us)
Async XLA Ops:
  0.6 8.3 %copy-start = (bf16[768,768]{1,0:T(8,128)(2,1)S(1)}, bf16[768,768]{1,0:T(8,128)(2,1)}, u32[]{:S(2)}) copy-start(bf16[768,768]{1,0:T(8,128)(2,1)} %wk_hbm.1) | copy-start | bytes 3538948
  0.6 8.3 %copy-start.1 = (bf16[768,768]{1,0:T(8,128)(2,1)S(1)}, bf16[768,768]{1,0:T(8,128)(2,1)}, u32[]{:S(2)}) copy-start(bf16[768,768]{1,0:T(8,128)(2,1)} %wv_hbm.1) | copy-start | bytes 3538948
  0.7 8.3 %copy-start.5 = (s32[16]{0:T(128)S(1)}, s32[16]{0:T(128)}, u32[]{:S(2)}) copy-start(s32[16]{0:T(128)} %offset_ref.1) | copy-start | bytes 196
  6.7 23.8 %collective-permute-start = (bf16[512,768]{1,0:T(8,128)(2,1)S(1)}, bf16[512,768]{1,0:T(8,128)(2,1)}, u32[]{:S(2)}, u32[]{:S(2)}) collective-permute-start(bf16[512,768]{1,0:T(8,128)(2,1)S(1)} %get-tuple-element.27.x_ref), channel_id=1, source_target_pairs={{0,8},{8,0},{16,24},{24,16},{1,9},{9,1},{17,25},{25,17},{2,10},{10... | collective-permute-start | bytes 2359304 | tf_op jit(solution)/shard_map/ppermute | solution.py:28
  8.9 9.0 %copy-start.6 = (bf16[768,768]{1,0:T(8,128)(2,1)S(1)}, bf16[768,768]{1,0:T(8,128)(2,1)}, u32[]{:S(2)}) copy-start(bf16[768,768]{1,0:T(8,128)(2,1)} %wq_hbm.1) | copy-start | bytes 3538948
  10.9 11.9 %copy-start.7 = (bf16[512,384]{1,0:T(8,128)(2,1)}, bf16[512,384]{1,0:T(8,128)(2,1)S(1)}, u32[]{:S(2)}) copy-start(bf16[512,384]{1,0:T(8,128)(2,1)S(1)} %get-tuple-element.28.k_ref.k_hbm) | copy-start | bytes 1179652
  10.9 11.9 %copy-start.8 = (bf16[512,384]{1,0:T(8,128)(2,1)}, bf16[512,384]{1,0:T(8,128)(2,1)S(1)}, u32[]{:S(2)}) copy-start(bf16[512,384]{1,0:T(8,128)(2,1)S(1)} %get-tuple-element.29.v_ref.v_hbm) | copy-start | bytes 1179652
  10.9 11.9 %collective-permute-start.1 = (bf16[2,16,768]{2,1,0:T(8,128)(2,1)S(1)}, bf16[2,16,768]{2,1,0:T(8,128)(2,1)S(1)}, u32[]{:S(2)}, u32[]{:S(2)}) collective-permute-start(bf16[2,16,768]{2,1,0:T(8,128)(2,1)S(1)} %get-tuple-element.34.own_ref), channel_id=1, source_target_pairs={{0,32},{32,0},{1,33},{33,1},{2,34},{34,2},{3,35},{35,3},{4,36},{36... | collective-permute-start | bytes 147464 | tf_op jit(solution)/shard_map/ppermute | solution.py:28
  23.8 20.6 %all-to-all-start = ((bf16[16,32,768]{2,1,0:T(8,128)(2,1)}), bf16[16,32,768]{2,1,0:T(8,128)(2,1)S(1)}, u32[]{:S(2)}, u32[]{:S(2)}) async-start(bf16[16,32,768]{2,1,0:T(8,128)(2,1)} %bitcast.4), calls=%async_computation | async-start | bytes 1572864 | tf_op jit(solution)/shard_map/all_to_all | solution.py:391
  44.4 0.9 copy-start.9
  45.3 34.0 %copy-start.2 = (bf16[768,768]{1,0:T(8,128)(2,1)S(1)}, bf16[768,768]{1,0:T(8,128)(2,1)}, u32[]{:S(2)}) copy-start(bf16[768,768]{1,0:T(8,128)(2,1)} %w_head_ref.1) | copy-start | bytes 3538948
  45.3 34.0 %copy-start.3 = (bf16[768,768]{1,0:T(8,128)(2,1)S(1)}, bf16[768,768]{1,0:T(8,128)(2,1)}, u32[]{:S(2)}) copy-start(bf16[768,768]{1,0:T(8,128)(2,1)} %w_out_ref.1) | copy-start | bytes 3538948
  45.3 34.1 %copy-start.4 = (bf16[1,768]{1,0:T(2,128)(2,1)S(1)}, bf16[1,768]{1,0:T(2,128)(2,1)}, u32[]{:S(2)}) copy-start(bf16[1,768]{1,0:T(2,128)(2,1)} %report_ref.1) | copy-start | bytes 4612
  55.9 32.7 %copy-start.10 = (bf16[512,768]{1,0:T(8,128)(2,1)S(1)}, bf16[512,768]{1,0:T(8,128)(2,1)}, u32[]{:S(2)}) copy-start(bf16[512,768]{1,0:T(8,128)(2,1)} %get-tuple-element.42) | copy-start | bytes 2359300
  77.4 11.2 %collective-permute-start.2 = (bf16[512,384]{1,0:T(8,128)(2,1)}, bf16[512,384]{1,0:T(8,128)(2,1)}, u32[]{:S(2)}, u32[]{:S(2)}) collective-permute-start(bf16[512,384]{1,0:T(8,128)(2,1)} %get-tuple-element.43), channel_id=1, source_target_pairs={{0,8},{8,0},{16,24},{24,16},{1,9},{9,1},{17,25},{25,17},{2,10},{10... | collective-permute-start | bytes 1179656 | tf_op jit(solution)/shard_map/ppermute | solution.py:28
  80.7 12.9 %all-to-all-start.2 = ((f32[8,8,256]{2,1,0:T(8,128)}), f32[8,8,256]{2,1,0:T(8,128)S(1)}, u32[]{:S(2)}, u32[]{:S(2)}) async-start(f32[8,8,256]{2,1,0:T(8,128)} %get-tuple-element.41), calls=%async_computation.2 | async-start | bytes 131072 | tf_op jit(solution)/shard_map/all_to_all | solution.py:490

commit v6 on v5

--- a/solution.py
+++ b/solution.py
@@ -40,8 +40,10 @@
     return (lane >= offset) & (lane < offset + width)
 
 
-def attend(queries, keys, values, head_width, mixed_ref, lse_ref, rows):
-    for head in range(queries.shape[1] // head_width):
+def attend(queries, keys, values, head_width, mixed_ref, lse_ref, finish):
+    width = queries.shape[1]
+    finished = 0
+    for head in range(width // head_width):
         first, last, _ = head_window(head, head_width)
         mine = in_head_lanes(head, head_width)
         masked = jnp.where(mine, queries[:, first:last], jnp.zeros((), queries.dtype))
@@ -55,10 +57,13 @@
         mixed = mixed * (1.0 / total)
         lse = jnp.broadcast_to(peak + jnp.log(total), mixed.shape)
         if head > 0:
-            mixed = jnp.where(mine, mixed, mixed_ref[rows, first:last])
-            lse = jnp.where(mine, lse, lse_ref[rows, first:last])
-        mixed_ref[rows, first:last] = mixed
-        lse_ref[rows, first:last] = lse
+            mixed = jnp.where(mine, mixed, mixed_ref[:, first:last])
+            lse = jnp.where(mine, lse, lse_ref[:, first:last])
+        mixed_ref[:, first:last] = mixed
+        lse_ref[:, first:last] = lse
+        while (finished + 1) * LANES <= (head + 1) * head_width:
+            finish(finished, slice(finished * LANES, (finished + 1) * LANES))
+            finished += 1
 
 
 def merge_states(one, one_lse, two, two_lse):
@@ -155,8 +160,18 @@
     q = jnp.dot(x_ref[...], wq, preferred_element_type=F32) * score_scale
     q_scr[...] = q.astype(BF16)
     stores = started((q_scr,), (q_out,), out_sems)
-    attend(q_scr[...], k_ref[...], v_ref[...], head_width, mixed_scr, lse_scr, slice(None))
-    stores += started((mixed_scr, lse_scr), (mixed_out, lse_out), out_sems, 1)
+
+    def finish(tile, lanes):
+        stores.extend(
+            started(
+                (mixed_scr.at[:, lanes], lse_scr.at[:, lanes]),
+                (mixed_out.at[:, lanes], lse_out.at[:, lanes]),
+                out_sems,
+                1 + 2 * tile,
+            )
+        )
+
+    attend(q_scr[...], k_ref[...], v_ref[...], head_width, mixed_scr, lse_scr, finish)
     for store in stores:
         store.wait()
 
@@ -189,54 +204,86 @@
     stores = started((q_scr.at[other],), (q_out.at[other],), out_sems)
     loads[4].wait()
     loads[5].wait()
+
+    def store_tile(place, span, first, lanes):
+        stores.extend(
+            started(
+                (mixed_scr.at[place, :, lanes], lse_scr.at[place, :, lanes]),
+                (mixed_out.at[span, lanes], lse_out.at[span, lanes]),
+                out_sems,
+                first,
+            )
+        )
+
+    tiles = mixed_scr.shape[2] // LANES
     attend(q_scr[rows:, :], k_scr[...], v_scr[...], head_width, mixed_scr.at[1], lse_scr.at[1],
-           slice(None))
-    stores += started(
-        (mixed_scr.at[1], lse_scr.at[1]), (mixed_out.at[other], lse_out.at[other]), out_sems, 1
-    )
+           lambda tile, lanes: store_tile(1, other, 2 + 2 * tile, lanes))
     loads[6].wait()
-    stores += started((q_scr.at[own],), (q_out.at[own],), out_sems, 3)
+    stores += started((q_scr.at[own],), (q_out.at[own],), out_sems, 1)
+
+    def finish_own(tile, lanes):
+        if tile == 0:
+            loads[7].wait()
+            loads[8].wait()
+        own_lse, new_lse = own_lse_scr[:, lanes], lse_scr[0, :, lanes]
+        mixed_scr[0, :, lanes] = merge_states(
+            own_mixed_scr[:, lanes], own_lse, mixed_scr[0, :, lanes], new_lse
+        )
+        gap = jnp.exp(-jnp.abs(own_lse - new_lse))
+        lse_scr[0, :, lanes] = jnp.maximum(own_lse, new_lse) + jnp.log(1.0 + gap)
+        store_tile(0, own, 2 + 2 * tiles + 2 * tile, lanes)
+
     attend(q_scr[:rows, :], k_scr[rows:, :], v_scr[rows:, :], head_width, mixed_scr.at[0],
-           lse_scr.at[0], slice(None))
-    loads[7].wait()
-    loads[8].wait()
-    own_lse, new_lse = own_lse_scr[...], lse_scr[0]
-    mixed_scr[0] = merge_states(own_mixed_scr[...], own_lse, mixed_scr[0], new_lse)
-    gap = jnp.exp(-jnp.abs(own_lse - new_lse))
-    lse_scr[0] = jnp.maximum(own_lse, new_lse) + jnp.log(1.0 + gap)
-    stores += started(
-        (mixed_scr.at[0], lse_scr.at[0]), (mixed_out.at[own], lse_out.at[own]), out_sems, 4
-    )
+           lse_scr.at[0], finish_own)
     for store in stores:
         store.wait()
 
 
-def far_kernel(q_hbm, far_hbm, near_hbm, near_lse_hbm, embedded_sum_ref, own_ref, lent_ref,
-               pack_ref, q_scr, far_scr, near_scr, near_lse_scr, mixed_scr, lse_scr, sems,
-               *, head_width):
+def far_kernel(q_hbm, far_hbm, near_hbm, near_lse_hbm, embedded_sum_ref, own_out, lent_out,
+               pack_ref, q_scr, far_scr, near_scr, near_lse_scr, mixed_scr, lse_scr, out_scr,
+               in_sems, out_sems, *, head_width):
     half = q_scr.shape[1]
-    rows = own_ref.shape[0]
-    loads = started(
-        (far_hbm, q_hbm, near_hbm, near_lse_hbm), (far_scr, q_scr, near_scr, near_lse_scr), sems
-    )
+    rows = out_scr.shape[1]
+    spans = (pl.ds(0, rows), pl.ds(rows, rows))
+    sources, targets = [far_hbm], [far_scr]
+    for refs in ((q_hbm, q_scr), (near_hbm, near_scr), (near_lse_hbm, near_lse_scr)):
+        for span in spans:
+            sources.append(refs[0].at[span])
+            targets.append(refs[1].at[span])
+    loads = started(sources, targets, in_sems)
     loads[0].wait()
-    loads[1].wait()
-    total = jnp.zeros((1, half), F32)
-    for place, out_ref in enumerate((own_ref, lent_ref)):
+    stores = []
+    sums = []
+    for place, out in enumerate((own_out, lent_out)):
+        loads[1 + place].wait()
         span = slice(place * rows, (place + 1) * rows)
+
+        def finish(tile, lanes):
+            if tile == 0:
+                loads[3 + place].wait()
+                loads[5 + place].wait()
+            attended = merge_states(
+                near_scr[span, lanes], near_lse_scr[span, lanes],
+                mixed_scr[place, :, lanes], lse_scr[place, :, lanes],
+            )
+            out_scr[place, :, lanes] = attended.astype(BF16)
+            sums.append(jnp.sum(attended, axis=0, keepdims=True))
+            stores.extend(
+                started(
+                    (out_scr.at[place, :, lanes],), (out.at[:, lanes],), out_sems,
+                    place * (half // LANES) + tile,
+                )
+            )
+
         attend(q_scr[span, :], far_scr[:, :half], far_scr[:, half:], head_width,
-               mixed_scr.at[place], lse_scr.at[place], slice(None))
-        if place == 0:
-            loads[2].wait()
-            loads[3].wait()
-        attended = merge_states(
-            near_scr[span, :], near_lse_scr[span, :], mixed_scr[place], lse_scr[place]
-        )
-        out_ref[...] = attended.astype(BF16)
-        total += jnp.sum(attended, axis=0, keepdims=True)
+               mixed_scr.at[place], lse_scr.at[place], finish)
+    tiles = half // LANES
+    total = jnp.concatenate([sums[t] + sums[tiles + t] for t in range(tiles)], axis=1)
     pad = jnp.zeros((1, pack_ref.shape[1] * pack_ref.shape[2] - 3 * half), F32)
     packed = pack_row((embedded_sum_ref[...], total, pad))
     pack_ref[...] = jnp.broadcast_to(packed[None], pack_ref.shape)
+    for store in stores:
+        store.wait()
 
 
 def pack_row(pieces):
@@ -280,7 +327,7 @@
     pooled = (embedded_sum + exact_row_times(attended_sum, w_out_ref[...])) * (1.0 / length)
     unit = unit_row(exact_row_times(pooled, w_head_ref[...]))
     unit_ref[...] = unit
-    packed = pack_row((unit, unit_row(report_ref[...].astype(F32)), codes_ref[...]))
+    packed = pack_row((unit, unit_row(report_ref[...].astype(F32)), codes_ref[...][None, :]))
     pack_ref[...] = jnp.broadcast_to(packed[None], pack_ref.shape)
 
 
@@ -390,6 +437,7 @@
     )(far_own, far_other).reshape(plane, 2 * far_rows, width)
     far = lax.all_to_all(payload, ("x", "y"), 0, 0, tiled=True).reshape(ranks * far_rows, width)
 
+    lane_tiles = half // LANES
     half_rows = jax.ShapeDtypeStruct((rows, half), BF16)
     queries_own, own_mixed, own_lse = pl.pallas_call(
         functools.partial(own_kernel, head_width=head_width, score_scale=score_scale),
@@ -404,7 +452,7 @@
             pltpu.VMEM((rows, half), BF16),
             pltpu.VMEM((rows, half), F32),
             pltpu.VMEM((rows, half), F32),
-            pltpu.SemaphoreType.DMA((3,)),
+            pltpu.SemaphoreType.DMA((1 + 2 * lane_tiles,)),
         ],
         compiler_params=pltpu.CompilerParams(vmem_limit_bytes=32 << 20),
         cost_estimate=pl.CostEstimate(
@@ -431,7 +479,7 @@
             pltpu.VMEM((2, rows, half), F32),
             pltpu.VMEM((2, rows, half), F32),
             pltpu.SemaphoreType.DMA((9,)),
-            pltpu.SemaphoreType.DMA((6,)),
+            pltpu.SemaphoreType.DMA((2 + 4 * lane_tiles,)),
         ],
         compiler_params=params,
         cost_estimate=pl.CostEstimate(
@@ -444,7 +492,7 @@
     own_half, lent_half, sums = pl.pallas_call(
         functools.partial(far_kernel, head_width=head_width),
         in_specs=[anywhere] * 4 + [vmem],
-        out_specs=[vmem] * 3,
+        out_specs=[anywhere, anywhere, vmem],
         out_shape=[half_rows, half_rows, jax.ShapeDtypeStruct((ranks,) + PACK, F32)],
         scratch_shapes=[
             pltpu.VMEM((2 * rows, half), BF16),
@@ -453,7 +501,9 @@
             pltpu.VMEM((2 * rows, half), F32),
             pltpu.VMEM((2, rows, half), F32),
             pltpu.VMEM((2, rows, half), F32),
-            pltpu.SemaphoreType.DMA((4,)),
+            pltpu.VMEM((2, rows, half), BF16),
+            pltpu.SemaphoreType.DMA((7,)),
+            pltpu.SemaphoreType.DMA((2 * lane_tiles,)),
         ],
         compiler_params=params,
         cost_estimate=pl.CostEstimate(
@@ -463,19 +513,16 @@
     )(queries, far, near_mixed, near_lse, embedded_sum)
 
     sums = lax.all_to_all(sums, SEQ_AXES, 0, 0, tiled=True)
-    sums, lent_half = lax.optimization_barrier((sums, lent_half))
+    lane = jnp.arange(2 * PACK[1], dtype=jnp.int32)
+    codes = jnp.where(lane == 0, slide_code, jnp.where(lane == 1, report_code, 0)).astype(F32)
+    w_mine = lax.dynamic_slice_in_dim(w_out, part * half, half, axis=0)
+    w_theirs = lax.dynamic_slice_in_dim(w_out, (1 - part) * half, half, axis=0)
+    encoded = embedded.astype(F32) + jnp.dot(own_half, w_mine, preferred_element_type=F32)
+    sums, lent_half, encoded, codes = lax.optimization_barrier((sums, lent_half, encoded, codes))
     other_half = swap_with(lent_half, "y")
-    joined = jnp.where(
-        part == 1,
-        jnp.concatenate((other_half, own_half), axis=1),
-        jnp.concatenate((own_half, other_half), axis=1),
-    )
-    encoded = embedded.astype(F32) + jnp.dot(joined, w_out, preferred_element_type=F32)
+    encoded = encoded + jnp.dot(other_half, w_theirs, preferred_element_type=F32)
     encoded = encoded.astype(BF16).reshape(1, rows, width)
 
-    lane = jnp.arange(2 * PACK[1], dtype=jnp.int32)[None, :]
-    codes = jnp.where(lane == 0, slide_code[:, None], jnp.where(lane == 1, report_code[:, None], 0))
-    codes = codes.astype(F32)
     slides = lax.axis_size("slide")
     slide_unit_vectors, packed = pl.pallas_call(
         functools.partial(pooled_kernel, length=rows * ranks),

time: 95 us -> 94.9 us (level)
  blocking collectives: 21.5 us -> 0 us
  starting transfers between devices: 24.4 us -> 33.8 us
  waiting for transfers between devices: 2.06 us -> 10.1 us
  matrix products: 3.02 us -> 5.71 us
  Pallas kernels: 40.6 us -> 41.7 us
    all_to_all x1 -> x0, blocking collectives: 21.5 us -> none  [on_device(): sums = lax.all_to_all(sums, SEQ_AXES, 0, 0, tiled=True)]
    all_to_all x0 -> x1, starting transfers between devices: none -> 9.48 us  [on_device(): sums = lax.all_to_all(sums, SEQ_AXES, 0, 0, tiled=True)]
    all_to_all x0 -> x1, waiting for transfers between devices: none -> 7.87 us  [on_device(): sums = lax.all_to_all(sums, SEQ_AXES, 0, 0, tiled=True)]
    dot_general x1 -> x2, matrix products: 3.02 us -> 5.71 us  [the longest x1 2.86 us: on_device(): jnp.dot(other_half, w_theirs, preferred_element_type=F32)]
    pallas_call x1, Pallas kernels: 10.5 us -> 11.5 us  [on_device(): pl.pallas_call(functools.partial(far_kernel, head_width=head_width), in_s...]
  transfers between devices with their start and end apart: 5 -> 6, of which waited for: 1 -> 2; matrix products, arithmetic and copies ran while one was open for 3% -> 6% of each run, Pallas kernels for 24% -> 25%
where the time goes in v6:
time: 94.9 us; the launch traced here: 94.4 us
  Pallas kernels  41.7 us (44%)
  starting transfers between devices  33.8 us (36%)
  waiting for transfers between devices  10.1 us (11%)
  matrix products  5.71 us (6%)
  between operations  2.13 us (2%)
    pallas_call x1, Pallas kernels, on_device(): pl.pallas_call(functools.partial(near_kernel, head_width=head_width, scor...  14.3 us
    pallas_call x1, Pallas kernels, on_device(): pl.pallas_call(functools.partial(far_kernel, head_width=head_width), in_s...  11.5 us
    ppermute x3, starting transfers between devices, swap_with(): lax.ppermute(x, axis, [(i, i ^ 1) for i in range(lax.axis_size(axis))])  9.88 us
    all_to_all x1, starting transfers between devices, on_device(): sums = lax.all_to_all(sums, SEQ_AXES, 0, 0, tiled=True)  9.48 us
    all_to_all x1, waiting for transfers between devices, on_device(): sums = lax.all_to_all(sums, SEQ_AXES, 0, 0, tiled=True)  7.87 us
    all_to_all x1, starting transfers between devices, on_device(): everyone = lax.all_to_all(packed, 'slide', 0, 0, tiled=True)  7.84 us
    all_to_all x1, starting transfers between devices, on_device(): lax.all_to_all(payload, ('x', 'y'), 0, 0, tiled=True)  6.64 us
    pallas_call x1, Pallas kernels, on_device(): pl.pallas_call(embed_kernel, in_specs=[anywhere, anywhere, vmem], out_spe...  6.02 us
  transfers between devices with their start and end apart: 6, of which 2 were waited for; matrix products, arithmetic and copies ran while one was open for 6% of the time, Pallas kernels for 25%

profile of v6, /device:TPU:1, one launch (start us, length us, event | category | flops | bytes accessed | tf_op | source)
XLA Modules:
  0.0 94.4 jit_solution(16401473221747809456)
XLA Ops:
  0.6 0.0 copy-start.1
  0.6 0.0 copy-start.2
  0.7 0.0 copy-start.5
  0.7 6.0 %embed.1 = (bf16[512,768]{1,0:T(8,128)(2,1)}, bf16[512,768]{1,0:T(8,128)(2,1)S(1)}, f32[1,768]{1,0:T(1,128)}) custom-call(bf16[512,1536]{1,0:T(8,128)(2,1)} %bitcast.13, bf16[1536,768]{1,0:T(8,128)(2,1)} %w_hbm.1, f32[768]{0:T(1024)} %gain_ref.1), custom_call_target="tpu_custom_call" | custom-call | tf_op jit(solution)/shard_map/embed/pallas_call | solution.py:395
  6.7 2.2 %collective-permute-start = (bf16[512,768]{1,0:T(8,128)(2,1)S(1)}, bf16[512,768]{1,0:T(8,128)(2,1)}, u32[]{:S(2)}, u32[]{:S(2)}) collective-permute-start(bf16[512,768]{1,0:T(8,128)(2,1)S(1)} %get-tuple-element.29.x_ref), channel_id=1, source_target_pairs={{0,8},{8,0},{16,24},{24,16},{1,9},{9,1},{17,25},{25,17},{2,10},{10... | collective-permute-start | bytes 2359304 | tf_op jit(solution)/shard_map/ppermute | solution.py:28
  8.9 0.0 copy-done.1
  8.9 0.0 copy-done.2
  8.9 0.0 copy-done.5
  8.9 2.0 %own_rows.1 = (bf16[2,16,768]{2,1,0:T(8,128)(2,1)S(1)}, bf16[512,384]{1,0:T(8,128)(2,1)S(1)}, bf16[512,384]{1,0:T(8,128)(2,1)S(1)}) custom-call(s32[1]{0:T(128)} %bitcast.part_ref, s32[16]{0:T(128)S(1)} %copy-done.5, bf16[512,768]{1,0:T(8,128)(2,1)S(1)} %get-tuple-element.29.x_ref, bf16[768,768]{1,0:T(8,128)(2,1)S(1)} %copy-done.1, ...), custom_call_target="tpu_custom_call" | custom-call | tf_op jit(solution)/shard_map/own_rows/pallas_call | solution.py:418
  10.9 7.0 %collective-permute-start.1 = (bf16[2,16,768]{2,1,0:T(8,128)(2,1)S(1)}, bf16[2,16,768]{2,1,0:T(8,128)(2,1)S(1)}, u32[]{:S(2)}, u32[]{:S(2)}) collective-permute-start(bf16[2,16,768]{2,1,0:T(8,128)(2,1)S(1)} %get-tuple-element.36.own_ref), channel_id=1, source_target_pairs={{0,32},{32,0},{1,33},{33,1},{2,34},{34,2},{3,35},{35,3},{4,36},{36... | collective-permute-start | bytes 147464 | tf_op jit(solution)/shard_map/ppermute | solution.py:28
  17.9 4.7 %own_attention.1 = (bf16[512,384]{1,0:T(8,128)(2,1)}, f32[512,384]{1,0:T(8,128)}, f32[512,384]{1,0:T(8,128)}) custom-call(s32[1]{0:T(128)} %bitcast.part_ref, bf16[512,768]{1,0:T(8,128)(2,1)S(1)} %get-tuple-element.29.x_ref, bf16[768,768]{1,0:T(8,128)(2,1)S(1)} %copy-done.6, bf16[512,384]{1,0:T(8,128)(2,1)S(1)} %get-tuple-element.30.k_ref.k_hbm, ...), custom_call_target="tpu_custom_call" | custom-call | flops 3000000000 | bytes 4000000 | tf_op jit(solution)/shard_map/own_attention/pallas_call | solution.py:442
  22.7 0.0 collective-permute-done.1.other_ref
  22.7 1.0 %payload.1 = bf16[8,2,2,16,768]{4,3,2,1,0:T(8,128)(2,1)} custom-call(bf16[2,16,768]{2,1,0:T(8,128)(2,1)S(1)} %get-tuple-element.36.own_ref, bf16[2,16,768]{2,1,0:T(8,128)(2,1)S(1)} %collective-permute-done.1.other_ref), custom_call_target="tpu_custom_call" | custom-call | tf_op jit(solution)/shard_map/payload/pallas_call | solution.py:431
  23.7 6.6 %all-to-all-start = ((bf16[16,32,768]{2,1,0:T(8,128)(2,1)}), bf16[16,32,768]{2,1,0:T(8,128)(2,1)S(1)}, u32[]{:S(2)}, u32[]{:S(2)}) async-start(bf16[16,32,768]{2,1,0:T(8,128)(2,1)} %bitcast.2), calls=%async_computation | async-start | bytes 1572864 | tf_op jit(solution)/shard_map/all_to_all | solution.py:438
  30.3 0.0 collective-permute-done.other_hbm
  30.3 14.3 %near_attention.1 = (bf16[1024,384]{1,0:T(8,128)(2,1)}, f32[1024,384]{1,0:T(8,128)}, f32[1024,384]{1,0:T(8,128)}) custom-call(s32[1]{0:T(128)} %bitcast.part_ref, bf16[512,768]{1,0:T(8,128)(2,1)} %collective-permute-done.other_hbm, bf16[512,384]{1,0:T(8,128)(2,1)} %copy-done.7, bf16[512,384]{1,0:T(8,128)(2,1)} %copy-done.8, ...), custom_call_target="tpu_custom_call" | custom-call | flops 8999999488 | bytes 8000000 | tf_op jit(solution)/shard_map/near_attention/pallas_call | solution.py:466
  44.6 0.0 all-to-all-done
  44.6 0.0 copy-start.9
  44.6 0.9 copy-done.9
  45.5 11.5 %far_attention.1 = (bf16[512,384]{1,0:T(8,128)(2,1)}, bf16[512,384]{1,0:T(8,128)(2,1)}, f32[32,8,256]{2,1,0:T(8,128)}) custom-call(bf16[1024,384]{1,0:T(8,128)(2,1)} %get-tuple-element.35.q_hbm, bf16[512,768]{1,0:T(8,128)(2,1)} %bitcast.14, f32[1024,384]{1,0:T(8,128)} %get-tuple-element.37.near_hbm, f32[1024,384]{1,0:T(8,128)} %get-tuple-element.38.near_lse_hbm, ...), custom_call_target="tpu_custom_call" | custom-call | flops 6000000000 | bytes 6000000 | tf_op jit(solution)/shard_map/far_attention/pallas_call | solution.py:492
  57.0 9.5 %all-to-all-start.1 = ((f32[32,8,256]{2,1,0:T(8,128)}), f32[32,8,256]{2,1,0:T(8,128)S(1)}, u32[]{:S(2)}, u32[]{:S(2)}) async-start(f32[32,8,256]{2,1,0:T(8,128)} %get-tuple-element.40), calls=%async_computation.1 | async-start | bytes 524288 | tf_op jit(solution)/shard_map/all_to_all | solution.py:515
  67.8 0.0 copy-start.3
  67.8 0.0 copy-start.4
  67.9 2.8 %convert_add_fusion = f32[512,768]{1,0:T(8,128)} fusion(bf16[512,768]{1,0:T(8,128)(2,1)S(1)} %copy-done.10, bf16[512,384]{1,0:T(8,128)(2,1)} %get-tuple-element.43, bf16[768,768]{1,0:T(8,128)(2,1)S(1)} %copy-done, s32[]{:T(128)S(6)} %select_n.22), kind=kOutput, calls=%fused_computation.1 | convolution fusion | flops 302776320 | bytes 3342340 | tf_op jit(solution)/shard_map/dot_general | solution.py:520
  70.7 7.9 %all-to-all-done.1.sums_ref = f32[32,8,256]{2,1,0:T(8,128)S(1)} async-done(((f32[32,8,256]{2,1,0:T(8,128)}), f32[32,8,256]{2,1,0:T(8,128)S(1)}, u32[]{:S(2)}, u32[]{:S(2)}) %all-to-all-start.1) | async-done | bytes 262176 | tf_op jit(solution)/shard_map/all_to_all | solution.py:515
  78.6 0.7 collective-permute-start.2
  79.3 1.3 %pooled.1 = (f32[1,768]{1,0:T(1,128)}, f32[8,8,256]{2,1,0:T(8,128)}) custom-call(f32[512]{0:T(512)S(1)} %select_convert_fusion.codes_ref, f32[32,8,256]{2,1,0:T(8,128)S(1)} %all-to-all-done.1.sums_ref, bf16[768,768]{1,0:T(8,128)(2,1)S(1)} %copy-done, bf16[768,768]{1,0:T(8,128)(2,1)S(1)} %copy-done.3, bf16[1,768]{1,0:T(2,128)(2,1)S(1)} %copy-done.4), custom_call_target="tpu_custom_call" | custom-call | tf_op jit(solution)/shard_map/pooled/pallas_call | solution.py:527
  80.6 7.8 %all-to-all-start.2 = ((f32[8,8,256]{2,1,0:T(8,128)}), f32[8,8,256]{2,1,0:T(8,128)S(1)}, u32[]{:S(2)}, u32[]{:S(2)}) async-start(f32[8,8,256]{2,1,0:T(8,128)} %get-tuple-element.46), calls=%async_computation.2 | async-start | bytes 131072 | tf_op jit(solution)/shard_map/all_to_all | solution.py:537
  88.4 0.0 collective-permute-done.2
  88.4 2.9 %fusion = bf16[1,512,768]{2,1,0:T(8,128)(2,1)} fusion(f32[512,768]{1,0:T(8,128)} %convert_add_fusion, bf16[512,384]{1,0:T(8,128)(2,1)S(1)} %collective-permute-done.2, bf16[768,768]{1,0:T(8,128)(2,1)S(1)} %copy-done, s32[]{:T(128)S(6)} %select_n.25), kind=kOutput, calls=%fused_computation.2 | convolution fusion | flops 302776320 | bytes 3342340 | tf_op jit(solution)/shard_map/dot_general | solution.py:523
  91.3 2.2 %all-to-all-done.2.all_ref = f32[8,8,256]{2,1,0:T(8,128)S(1)} async-done(((f32[8,8,256]{2,1,0:T(8,128)}), f32[8,8,256]{2,1,0:T(8,128)S(1)}, u32[]{:S(2)}, u32[]{:S(2)}) %all-to-all-start.2) | async-done | bytes 65568 | tf_op jit(solution)/shard_map/all_to_all | solution.py:537
  93.5 1.0 %contrast.1 = (f32[8,8]{1,0:T(8,128)}, f32[1,1]{1,0:T(1,128)}) custom-call(f32[8,8,256]{2,1,0:T(8,128)S(1)} %all-to-all-done.2.all_ref), custom_call_target="tpu_custom_call" | custom-call | tf_op jit(solution)/shard_map/contrast/pallas_call | solution.py:539
  (13 shorter events, 0.0 us)
Async XLA Ops:
  0.6 8.3 %copy-start.1 = (bf16[768,768]{1,0:T(8,128)(2,1)S(1)}, bf16[768,768]{1,0:T(8,128)(2,1)}, u32[]{:S(2)}) copy-start(bf16[768,768]{1,0:T(8,128)(2,1)} %wk_hbm.1) | copy-start | bytes 3538948
  0.6 8.3 %copy-start.2 = (bf16[768,768]{1,0:T(8,128)(2,1)S(1)}, bf16[768,768]{1,0:T(8,128)(2,1)}, u32[]{:S(2)}) copy-start(bf16[768,768]{1,0:T(8,128)(2,1)} %wv_hbm.1) | copy-start | bytes 3538948
  0.7 8.3 %copy-start.5 = (s32[16]{0:T(128)S(1)}, s32[16]{0:T(128)}, u32[]{:S(2)}) copy-start(s32[16]{0:T(128)} %offset_ref.1) | copy-start | bytes 196
  6.7 23.6 %collective-permute-start = (bf16[512,768]{1,0:T(8,128)(2,1)S(1)}, bf16[512,768]{1,0:T(8,128)(2,1)}, u32[]{:S(2)}, u32[]{:S(2)}) collective-permute-start(bf16[512,768]{1,0:T(8,128)(2,1)S(1)} %get-tuple-element.29.x_ref), channel_id=1, source_target_pairs={{0,8},{8,0},{16,24},{24,16},{1,9},{9,1},{17,25},{25,17},{2,10},{10... | collective-permute-start | bytes 2359304 | tf_op jit(solution)/shard_map/ppermute | solution.py:28
  8.9 9.0 %copy-start.6 = (bf16[768,768]{1,0:T(8,128)(2,1)S(1)}, bf16[768,768]{1,0:T(8,128)(2,1)}, u32[]{:S(2)}) copy-start(bf16[768,768]{1,0:T(8,128)(2,1)} %wq_hbm.1) | copy-start | bytes 3538948
  10.9 11.8 %copy-start.7 = (bf16[512,384]{1,0:T(8,128)(2,1)}, bf16[512,384]{1,0:T(8,128)(2,1)S(1)}, u32[]{:S(2)}) copy-start(bf16[512,384]{1,0:T(8,128)(2,1)S(1)} %get-tuple-element.30.k_ref.k_hbm) | copy-start | bytes 1179652
  10.9 11.8 %copy-start.8 = (bf16[512,384]{1,0:T(8,128)(2,1)}, bf16[512,384]{1,0:T(8,128)(2,1)S(1)}, u32[]{:S(2)}) copy-start(bf16[512,384]{1,0:T(8,128)(2,1)S(1)} %get-tuple-element.31.v_ref.v_hbm) | copy-start | bytes 1179652
  10.9 11.8 %collective-permute-start.1 = (bf16[2,16,768]{2,1,0:T(8,128)(2,1)S(1)}, bf16[2,16,768]{2,1,0:T(8,128)(2,1)S(1)}, u32[]{:S(2)}, u32[]{:S(2)}) collective-permute-start(bf16[2,16,768]{2,1,0:T(8,128)(2,1)S(1)} %get-tuple-element.36.own_ref), channel_id=1, source_target_pairs={{0,32},{32,0},{1,33},{33,1},{2,34},{34,2},{3,35},{35,3},{4,36},{36... | collective-permute-start | bytes 147464 | tf_op jit(solution)/shard_map/ppermute | solution.py:28
  23.7 20.9 %all-to-all-start = ((bf16[16,32,768]{2,1,0:T(8,128)(2,1)}), bf16[16,32,768]{2,1,0:T(8,128)(2,1)S(1)}, u32[]{:S(2)}, u32[]{:S(2)}) async-start(bf16[16,32,768]{2,1,0:T(8,128)(2,1)} %bitcast.2), calls=%async_computation | async-start | bytes 1572864 | tf_op jit(solution)/shard_map/all_to_all | solution.py:438
  44.6 0.9 copy-start.9
  45.5 22.3 %copy-start = (bf16[768,768]{1,0:T(8,128)(2,1)S(1)}, bf16[768,768]{1,0:T(8,128)(2,1)}, u32[]{:S(2)}) copy-start(bf16[768,768]{1,0:T(8,128)(2,1)} %w_out_ref.1) | copy-start | bytes 3538948
  45.5 22.3 %copy-start.10 = (bf16[512,768]{1,0:T(8,128)(2,1)S(1)}, bf16[512,768]{1,0:T(8,128)(2,1)}, u32[]{:S(2)}) copy-start(bf16[512,768]{1,0:T(8,128)(2,1)} %get-tuple-element.42) | copy-start | bytes 2359300
  57.0 21.6 %all-to-all-start.1 = ((f32[32,8,256]{2,1,0:T(8,128)}), f32[32,8,256]{2,1,0:T(8,128)S(1)}, u32[]{:S(2)}, u32[]{:S(2)}) async-start(f32[32,8,256]{2,1,0:T(8,128)} %get-tuple-element.40), calls=%async_computation.1 | async-start | bytes 524288 | tf_op jit(solution)/shard_map/all_to_all | solution.py:515
  67.8 11.4 %copy-start.3 = (bf16[768,768]{1,0:T(8,128)(2,1)S(1)}, bf16[768,768]{1,0:T(8,128)(2,1)}, u32[]{:S(2)}) copy-start(bf16[768,768]{1,0:T(8,128)(2,1)} %w_head_ref.1) | copy-start | bytes 3538948
  67.8 11.4 %copy-start.4 = (bf16[1,768]{1,0:T(2,128)(2,1)S(1)}, bf16[1,768]{1,0:T(2,128)(2,1)}, u32[]{:S(2)}) copy-start(bf16[1,768]{1,0:T(2,128)(2,1)} %report_ref.1) | copy-start | bytes 4612
  78.6 9.8 %collective-permute-start.2 = (bf16[512,384]{1,0:T(8,128)(2,1)}, bf16[512,384]{1,0:T(8,128)(2,1)S(1)}, u32[]{:S(2)}, u32[]{:S(2)}) collective-permute-start(bf16[512,384]{1,0:T(8,128)(2,1)} %get-tuple-element.48), channel_id=1, source_target_pairs={{0,8},{8,0},{16,24},{24,16},{1,9},{9,1},{17,25},{25,17},{2,10},{10... | collective-permute-start | bytes 1179656 | tf_op jit(solution)/shard_map/ppermute | solution.py:28
  80.6 12.9 %all-to-all-start.2 = ((f32[8,8,256]{2,1,0:T(8,128)}), f32[8,8,256]{2,1,0:T(8,128)S(1)}, u32[]{:S(2)}, u32[]{:S(2)}) async-start(f32[8,8,256]{2,1,0:T(8,128)} %get-tuple-element.46), calls=%async_computation.2 | async-start | bytes 131072 | tf_op jit(solution)/shard_map/all_to_all | solution.py:537

commit v7 on v6

--- a/solution.py
+++ b/solution.py
@@ -17,7 +17,7 @@
 NN = (((1,), (0,)), ((), ()))
 SMALL_VMEM = 16 << 20
 LARGE_VMEM = 58 << 20
-EMBED_STEPS = 2
+EMBED_PIECES = 3
 EMBED_VMEM = 59 << 20
 SEQ_AXES = ("x", "z_hi", "y")
 F32 = jnp.float32
@@ -40,7 +40,7 @@
     return (lane >= offset) & (lane < offset + width)
 
 
-def attend(queries, keys, values, head_width, mixed_ref, lse_ref, finish):
+def attend(queries, keys, values, head_width, mixed_ref, lse_ref, finish=None):
     width = queries.shape[1]
     finished = 0
     for head in range(width // head_width):
@@ -61,7 +61,7 @@
             lse = jnp.where(mine, lse, lse_ref[:, first:last])
         mixed_ref[:, first:last] = mixed
         lse_ref[:, first:last] = lse
-        while (finished + 1) * LANES <= (head + 1) * head_width:
+        while finish is not None and (finished + 1) * LANES <= (head + 1) * head_width:
             finish(finished, slice(finished * LANES, (finished + 1) * LANES))
             finished += 1
 
@@ -81,41 +81,30 @@
 
 def embed_kernel(x_hbm, w_hbm, gain_ref, embedded_hbm, normed_ref, sum_ref, x_scr, w_scr,
                  embedded_scr, x_sems, w_sems, out_sems):
-    rows = x_scr.shape[0] // EMBED_STEPS
-    spans = [pl.ds(step * rows, rows) for step in range(EMBED_STEPS)]
+    rows = x_scr.shape[0] // x_sems.shape[0]
+    spans = [pl.ds(i * rows, rows) for i in range(x_sems.shape[0])]
     pieces = w_sems.shape[0]
     depth = w_scr.shape[0] // pieces
     parts = [pl.ds(i * depth, depth) for i in range(pieces)]
-    x_loads = started([x_hbm.at[spans[0]]], [x_scr.at[spans[0]]], x_sems)
+    x_loads = started([x_hbm.at[span] for span in spans], [x_scr.at[span] for span in spans], x_sems)
     w_loads = started([w_hbm.at[p] for p in parts], [w_scr.at[p] for p in parts], w_sems)
-    x_loads += started(
-        [x_hbm.at[span] for span in spans[1:]], [x_scr.at[span] for span in spans[1:]], x_sems, 1
-    )
-    stores = []
-    summed = jnp.zeros(sum_ref.shape, F32)
-    for step, span in enumerate(spans):
-        x_loads[step].wait()
-        if step == 0:
-            total = None
-            for piece, load in enumerate(w_loads):
-                load.wait()
-                columns = slice(piece * depth, (piece + 1) * depth)
-                product = jnp.dot(
-                    x_scr[span, columns], w_scr[parts[piece], :], preferred_element_type=F32
-                )
-                total = product if total is None else total + product
-        else:
-            total = jnp.dot(x_scr[span, :], w_scr[...], preferred_element_type=F32)
-        embedded = total.astype(BF16)
-        embedded_scr[span, :] = embedded
-        stores += started([embedded_scr.at[span]], [embedded_hbm.at[span]], out_sems, step)
-        floats = embedded.astype(F32)
-        centred = floats - jnp.mean(floats, axis=1, keepdims=True)
-        spread = jnp.mean(centred * centred, axis=1, keepdims=True)
-        normed = centred * lax.rsqrt(spread + NORM_EPS) * gain_ref[...][None, :]
-        normed_ref[span, :] = normed.astype(BF16)
-        summed += jnp.sum(floats, axis=0, keepdims=True)
-    sum_ref[...] = summed
+    for load in x_loads:
+        load.wait()
+    total = None
+    for piece, load in enumerate(w_loads):
+        load.wait()
+        columns = slice(piece * depth, (piece + 1) * depth)
+        product = jnp.dot(x_scr[:, columns], w_scr[columns, :], preferred_element_type=F32)
+        total = product if total is None else total + product
+    embedded = total.astype(BF16)
+    embedded_scr[...] = embedded
+    stores = started([embedded_scr], [embedded_hbm], out_sems)
+    floats = embedded.astype(F32)
+    centred = floats - jnp.mean(floats, axis=1, keepdims=True)
+    spread = jnp.mean(centred * centred, axis=1, keepdims=True)
+    normed = centred * lax.rsqrt(spread + NORM_EPS) * gain_ref[...][None, :]
+    normed_ref[...] = normed.astype(BF16)
+    sum_ref[...] = jnp.sum(floats, axis=0, keepdims=True)
     for store in stores:
         store.wait()
 
@@ -205,36 +194,29 @@
     loads[4].wait()
     loads[5].wait()
 
-    def store_tile(place, span, first, lanes):
+    def store_block(place, span, first):
         stores.extend(
             started(
-                (mixed_scr.at[place, :, lanes], lse_scr.at[place, :, lanes]),
-                (mixed_out.at[span, lanes], lse_out.at[span, lanes]),
+                (mixed_scr.at[place], lse_scr.at[place]),
+                (mixed_out.at[span], lse_out.at[span]),
                 out_sems,
                 first,
             )
         )
 
-    tiles = mixed_scr.shape[2] // LANES
-    attend(q_scr[rows:, :], k_scr[...], v_scr[...], head_width, mixed_scr.at[1], lse_scr.at[1],
-           lambda tile, lanes: store_tile(1, other, 2 + 2 * tile, lanes))
+    attend(q_scr[rows:, :], k_scr[...], v_scr[...], head_width, mixed_scr.at[1], lse_scr.at[1])
+    store_block(1, other, 2)
     loads[6].wait()
     stores += started((q_scr.at[own],), (q_out.at[own],), out_sems, 1)
-
-    def finish_own(tile, lanes):
-        if tile == 0:
-            loads[7].wait()
-            loads[8].wait()
-        own_lse, new_lse = own_lse_scr[:, lanes], lse_scr[0, :, lanes]
-        mixed_scr[0, :, lanes] = merge_states(
-            own_mixed_scr[:, lanes], own_lse, mixed_scr[0, :, lanes], new_lse
-        )
-        gap = jnp.exp(-jnp.abs(own_lse - new_lse))
-        lse_scr[0, :, lanes] = jnp.maximum(own_lse, new_lse) + jnp.log(1.0 + gap)
-        store_tile(0, own, 2 + 2 * tiles + 2 * tile, lanes)
-
     attend(q_scr[:rows, :], k_scr[rows:, :], v_scr[rows:, :], head_width, mixed_scr.at[0],
-           lse_scr.at[0], finish_own)
+           lse_scr.at[0])
+    loads[7].wait()
+    loads[8].wait()
+    own_lse, new_lse = own_lse_scr[...], lse_scr[0]
+    mixed_scr[0] = merge_states(own_mixed_scr[...], own_lse, mixed_scr[0], new_lse)
+    gap = jnp.exp(-jnp.abs(own_lse - new_lse))
+    lse_scr[0] = jnp.maximum(own_lse, new_lse) + jnp.log(1.0 + gap)
+    store_block(0, own, 4)
     for store in stores:
         store.wait()
 
@@ -257,28 +239,17 @@
     for place, out in enumerate((own_out, lent_out)):
         loads[1 + place].wait()
         span = slice(place * rows, (place + 1) * rows)
-
-        def finish(tile, lanes):
-            if tile == 0:
-                loads[3 + place].wait()
-                loads[5 + place].wait()
-            attended = merge_states(
-                near_scr[span, lanes], near_lse_scr[span, lanes],
-                mixed_scr[place, :, lanes], lse_scr[place, :, lanes],
-            )
-            out_scr[place, :, lanes] = attended.astype(BF16)
-            sums.append(jnp.sum(attended, axis=0, keepdims=True))
-            stores.extend(
-                started(
-                    (out_scr.at[place, :, lanes],), (out.at[:, lanes],), out_sems,
-                    place * (half // LANES) + tile,
-                )
-            )
-
         attend(q_scr[span, :], far_scr[:, :half], far_scr[:, half:], head_width,
-               mixed_scr.at[place], lse_scr.at[place], finish)
-    tiles = half // LANES
-    total = jnp.concatenate([sums[t] + sums[tiles + t] for t in range(tiles)], axis=1)
+               mixed_scr.at[place], lse_scr.at[place])
+        loads[3 + place].wait()
+        loads[5 + place].wait()
+        attended = merge_states(
+            near_scr[span, :], near_lse_scr[span, :], mixed_scr[place], lse_scr[place]
+        )
+        out_scr[place] = attended.astype(BF16)
+        stores += started((out_scr.at[place],), (out,), out_sems, place)
+        sums.append(jnp.sum(attended, axis=0, keepdims=True))
+    total = sums[0] + sums[1]
     pad = jnp.zeros((1, pack_ref.shape[1] * pack_ref.shape[2] - 3 * half), F32)
     packed = pack_row((embedded_sum_ref[...], total, pad))
     pack_ref[...] = jnp.broadcast_to(packed[None], pack_ref.shape)
@@ -391,7 +362,6 @@
     vmem = pl.BlockSpec(memory_space=pltpu.VMEM)
     anywhere = pl.BlockSpec(memory_space=pl.ANY)
 
-    pieces = 3
     embedded, normed, embedded_sum = pl.pallas_call(
         embed_kernel,
         in_specs=[anywhere, anywhere, vmem],
@@ -405,9 +375,9 @@
             pltpu.VMEM((rows, in_width), BF16),
             pltpu.VMEM((in_width, width), BF16),
             pltpu.VMEM((rows, width), BF16),
-            pltpu.SemaphoreType.DMA((EMBED_STEPS,)),
-            pltpu.SemaphoreType.DMA((pieces,)),
-            pltpu.SemaphoreType.DMA((EMBED_STEPS,)),
+            pltpu.SemaphoreType.DMA((2,)),
+            pltpu.SemaphoreType.DMA((EMBED_PIECES,)),
+            pltpu.SemaphoreType.DMA((1,)),
         ],
         compiler_params=pltpu.CompilerParams(vmem_limit_bytes=EMBED_VMEM),
         name="embed",
@@ -479,7 +449,7 @@
             pltpu.VMEM((2, rows, half), F32),
             pltpu.VMEM((2, rows, half), F32),
             pltpu.SemaphoreType.DMA((9,)),
-            pltpu.SemaphoreType.DMA((2 + 4 * lane_tiles,)),
+            pltpu.SemaphoreType.DMA((6,)),
         ],
         compiler_params=params,
         cost_estimate=pl.CostEstimate(
@@ -503,7 +473,7 @@
             pltpu.VMEM((2, rows, half), F32),
             pltpu.VMEM((2, rows, half), BF16),
             pltpu.SemaphoreType.DMA((7,)),
-            pltpu.SemaphoreType.DMA((2 * lane_tiles,)),
+            pltpu.SemaphoreType.DMA((2,)),
         ],
         compiler_params=params,
         cost_estimate=pl.CostEstimate(

time: 94.9 us -> 93.9 us (0.989)
  transfers between devices with their start and end apart: 6 -> 6, of which waited for: 2 -> 2; matrix products, arithmetic and copies ran while one was open for 6% -> 6% of each run, Pallas kernels for 25% -> 24%
where the time goes in v7:
time: 93.9 us; the launch traced here: 93.5 us
  Pallas kernels  40.8 us (43%)
  starting transfers between devices  33.8 us (36%)
  waiting for transfers between devices  10.1 us (11%)
  matrix products  5.71 us (6%)
  between operations  2.13 us (2%)
    pallas_call x1, Pallas kernels, on_device(): pl.pallas_call(functools.partial(near_kernel, head_width=head_width, scor...  13.9 us
    pallas_call x1, Pallas kernels, on_device(): pl.pallas_call(functools.partial(far_kernel, head_width=head_width), in_s...  10.9 us
    ppermute x3, starting transfers between devices, swap_with(): lax.ppermute(x, axis, [(i, i ^ 1) for i in range(lax.axis_size(axis))])  9.88 us
    all_to_all x1, starting transfers between devices, on_device(): sums = lax.all_to_all(sums, SEQ_AXES, 0, 0, tiled=True)  9.47 us
    all_to_all x1, waiting for transfers between devices, on_device(): sums = lax.all_to_all(sums, SEQ_AXES, 0, 0, tiled=True)  7.87 us
    all_to_all x1, starting transfers between devices, on_device(): everyone = lax.all_to_all(packed, 'slide', 0, 0, tiled=True)  7.84 us
    all_to_all x1, starting transfers between devices, on_device(): lax.all_to_all(payload, ('x', 'y'), 0, 0, tiled=True)  6.64 us
    pallas_call x1, Pallas kernels, on_device(): pl.pallas_call(embed_kernel, in_specs=[anywhere, anywhere, vmem], out_spe...  6.02 us
  transfers between devices with their start and end apart: 6, of which 2 were waited for; matrix products, arithmetic and copies ran while one was open for 6% of the time, Pallas kernels for 24%

profile of v7, /device:TPU:1, one launch (start us, length us, event | category | flops | bytes accessed | tf_op | source)
XLA Modules:
  0.0 93.5 jit_solution(4013788868587852944)
XLA Ops:
  0.6 0.0 copy-start.1
  0.6 0.0 copy-start.2
  0.7 0.0 copy-start.5
  0.7 6.0 %embed.1 = (bf16[512,768]{1,0:T(8,128)(2,1)}, bf16[512,768]{1,0:T(8,128)(2,1)S(1)}, f32[1,768]{1,0:T(1,128)}) custom-call(bf16[512,1536]{1,0:T(8,128)(2,1)} %bitcast.13, bf16[1536,768]{1,0:T(8,128)(2,1)} %w_hbm.1, f32[768]{0:T(1024)} %gain_ref.1), custom_call_target="tpu_custom_call" | custom-call | tf_op jit(solution)/shard_map/embed/pallas_call | solution.py:365
  6.7 2.2 %collective-permute-start = (bf16[512,768]{1,0:T(8,128)(2,1)S(1)}, bf16[512,768]{1,0:T(8,128)(2,1)}, u32[]{:S(2)}, u32[]{:S(2)}) collective-permute-start(bf16[512,768]{1,0:T(8,128)(2,1)S(1)} %get-tuple-element.29.x_ref), channel_id=1, source_target_pairs={{0,8},{8,0},{16,24},{24,16},{1,9},{9,1},{17,25},{25,17},{2,10},{10... | collective-permute-start | bytes 2359304 | tf_op jit(solution)/shard_map/ppermute | solution.py:28
  8.9 0.0 copy-done.1
  8.9 2.0 %own_rows.1 = (bf16[2,16,768]{2,1,0:T(8,128)(2,1)S(1)}, bf16[512,384]{1,0:T(8,128)(2,1)S(1)}, bf16[512,384]{1,0:T(8,128)(2,1)S(1)}) custom-call(s32[1]{0:T(128)} %bitcast.part_ref, s32[16]{0:T(128)S(1)} %copy-done.5, bf16[512,768]{1,0:T(8,128)(2,1)S(1)} %get-tuple-element.29.x_ref, bf16[768,768]{1,0:T(8,128)(2,1)S(1)} %copy-done.1, ...), custom_call_target="tpu_custom_call" | custom-call | tf_op jit(solution)/shard_map/own_rows/pallas_call | solution.py:388
  10.9 7.0 %collective-permute-start.1 = (bf16[2,16,768]{2,1,0:T(8,128)(2,1)S(1)}, bf16[2,16,768]{2,1,0:T(8,128)(2,1)S(1)}, u32[]{:S(2)}, u32[]{:S(2)}) collective-permute-start(bf16[2,16,768]{2,1,0:T(8,128)(2,1)S(1)} %get-tuple-element.36.own_ref), channel_id=1, source_target_pairs={{0,32},{32,0},{1,33},{33,1},{2,34},{34,2},{3,35},{35,3},{4,36},{36... | collective-permute-start | bytes 147464 | tf_op jit(solution)/shard_map/ppermute | solution.py:28
  17.9 0.0 copy-done.6
  17.9 4.7 %own_attention.1 = (bf16[512,384]{1,0:T(8,128)(2,1)}, f32[512,384]{1,0:T(8,128)}, f32[512,384]{1,0:T(8,128)}) custom-call(s32[1]{0:T(128)} %bitcast.part_ref, bf16[512,768]{1,0:T(8,128)(2,1)S(1)} %get-tuple-element.29.x_ref, bf16[768,768]{1,0:T(8,128)(2,1)S(1)} %copy-done.6, bf16[512,384]{1,0:T(8,128)(2,1)S(1)} %get-tuple-element.30.k_ref.k_hbm, ...), custom_call_target="tpu_custom_call" | custom-call | flops 3000000000 | bytes 4000000 | tf_op jit(solution)/shard_map/own_attention/pallas_call | solution.py:412
  22.7 0.0 collective-permute-done.1.other_ref
  22.7 1.0 %payload.1 = bf16[8,2,2,16,768]{4,3,2,1,0:T(8,128)(2,1)} custom-call(bf16[2,16,768]{2,1,0:T(8,128)(2,1)S(1)} %get-tuple-element.36.own_ref, bf16[2,16,768]{2,1,0:T(8,128)(2,1)S(1)} %collective-permute-done.1.other_ref), custom_call_target="tpu_custom_call" | custom-call | tf_op jit(solution)/shard_map/payload/pallas_call | solution.py:401
  23.7 6.6 %all-to-all-start = ((bf16[16,32,768]{2,1,0:T(8,128)(2,1)}), bf16[16,32,768]{2,1,0:T(8,128)(2,1)S(1)}, u32[]{:S(2)}, u32[]{:S(2)}) async-start(bf16[16,32,768]{2,1,0:T(8,128)(2,1)} %bitcast.2), calls=%async_computation | async-start | bytes 1572864 | tf_op jit(solution)/shard_map/all_to_all | solution.py:408
  30.3 0.0 collective-permute-done.other_hbm
  30.3 13.9 %near_attention.1 = (bf16[1024,384]{1,0:T(8,128)(2,1)}, f32[1024,384]{1,0:T(8,128)}, f32[1024,384]{1,0:T(8,128)}) custom-call(s32[1]{0:T(128)} %bitcast.part_ref, bf16[512,768]{1,0:T(8,128)(2,1)} %collective-permute-done.other_hbm, bf16[512,384]{1,0:T(8,128)(2,1)} %copy-done.7, bf16[512,384]{1,0:T(8,128)(2,1)} %copy-done.8, ...), custom_call_target="tpu_custom_call" | custom-call | flops 8999999488 | bytes 8000000 | tf_op jit(solution)/shard_map/near_attention/pallas_call | solution.py:436
  44.2 0.0 all-to-all-done
  44.3 0.9 copy-done.9
  45.1 10.9 %far_attention.1 = (bf16[512,384]{1,0:T(8,128)(2,1)}, bf16[512,384]{1,0:T(8,128)(2,1)}, f32[32,8,256]{2,1,0:T(8,128)}) custom-call(bf16[1024,384]{1,0:T(8,128)(2,1)} %get-tuple-element.35.q_hbm, bf16[512,768]{1,0:T(8,128)(2,1)} %bitcast.14, f32[1024,384]{1,0:T(8,128)} %get-tuple-element.37.near_hbm, f32[1024,384]{1,0:T(8,128)} %get-tuple-element.38.near_lse_hbm, ...), custom_call_target="tpu_custom_call" | custom-call | flops 6000000000 | bytes 6000000 | tf_op jit(solution)/shard_map/far_attention/pallas_call | solution.py:462
  56.1 9.5 %all-to-all-start.1 = ((f32[32,8,256]{2,1,0:T(8,128)}), f32[32,8,256]{2,1,0:T(8,128)S(1)}, u32[]{:S(2)}, u32[]{:S(2)}) async-start(f32[32,8,256]{2,1,0:T(8,128)} %get-tuple-element.40), calls=%async_computation.1 | async-start | bytes 524288 | tf_op jit(solution)/shard_map/all_to_all | solution.py:485
  66.9 0.0 copy-done
  66.9 0.0 copy-done.10
  66.9 0.0 copy-start.3
  66.9 0.0 copy-start.4
  66.9 2.8 %convert_add_fusion = f32[512,768]{1,0:T(8,128)} fusion(bf16[512,768]{1,0:T(8,128)(2,1)S(1)} %copy-done.10, bf16[512,384]{1,0:T(8,128)(2,1)} %get-tuple-element.43, bf16[768,768]{1,0:T(8,128)(2,1)S(1)} %copy-done, s32[]{:T(128)S(6)} %select_n.22), kind=kOutput, calls=%fused_computation.1 | convolution fusion | flops 302776320 | bytes 3342340 | tf_op jit(solution)/shard_map/dot_general | solution.py:490
  69.8 7.9 %all-to-all-done.1.sums_ref = f32[32,8,256]{2,1,0:T(8,128)S(1)} async-done(((f32[32,8,256]{2,1,0:T(8,128)}), f32[32,8,256]{2,1,0:T(8,128)S(1)}, u32[]{:S(2)}, u32[]{:S(2)}) %all-to-all-start.1) | async-done | bytes 262176 | tf_op jit(solution)/shard_map/all_to_all | solution.py:485
  77.6 0.7 collective-permute-start.2
  78.3 1.3 %pooled.1 = (f32[1,768]{1,0:T(1,128)}, f32[8,8,256]{2,1,0:T(8,128)}) custom-call(f32[512]{0:T(512)S(1)} %select_convert_fusion.codes_ref, f32[32,8,256]{2,1,0:T(8,128)S(1)} %all-to-all-done.1.sums_ref, bf16[768,768]{1,0:T(8,128)(2,1)S(1)} %copy-done, bf16[768,768]{1,0:T(8,128)(2,1)S(1)} %copy-done.3, bf16[1,768]{1,0:T(2,128)(2,1)S(1)} %copy-done.4), custom_call_target="tpu_custom_call" | custom-call | tf_op jit(solution)/shard_map/pooled/pallas_call | solution.py:497
  79.6 7.8 %all-to-all-start.2 = ((f32[8,8,256]{2,1,0:T(8,128)}), f32[8,8,256]{2,1,0:T(8,128)S(1)}, u32[]{:S(2)}, u32[]{:S(2)}) async-start(f32[8,8,256]{2,1,0:T(8,128)} %get-tuple-element.46), calls=%async_computation.2 | async-start | bytes 131072 | tf_op jit(solution)/shard_map/all_to_all | solution.py:507
  87.5 0.0 collective-permute-done.2
  87.5 2.9 %fusion = bf16[1,512,768]{2,1,0:T(8,128)(2,1)} fusion(f32[512,768]{1,0:T(8,128)} %convert_add_fusion, bf16[512,384]{1,0:T(8,128)(2,1)S(1)} %collective-permute-done.2, bf16[768,768]{1,0:T(8,128)(2,1)S(1)} %copy-done, s32[]{:T(128)S(6)} %select_n.25), kind=kOutput, calls=%fused_computation.2 | convolution fusion | flops 302776320 | bytes 3342340 | tf_op jit(solution)/shard_map/dot_general | solution.py:493
  90.3 2.2 %all-to-all-done.2.all_ref = f32[8,8,256]{2,1,0:T(8,128)S(1)} async-done(((f32[8,8,256]{2,1,0:T(8,128)}), f32[8,8,256]{2,1,0:T(8,128)S(1)}, u32[]{:S(2)}, u32[]{:S(2)}) %all-to-all-start.2) | async-done | bytes 65568 | tf_op jit(solution)/shard_map/all_to_all | solution.py:507
  92.5 1.0 %contrast.1 = (f32[8,8]{1,0:T(8,128)}, f32[1,1]{1,0:T(1,128)}) custom-call(f32[8,8,256]{2,1,0:T(8,128)S(1)} %all-to-all-done.2.all_ref), custom_call_target="tpu_custom_call" | custom-call | tf_op jit(solution)/shard_map/contrast/pallas_call | solution.py:509
  (13 shorter events, 0.0 us)
Async XLA Ops:
  0.6 8.3 %copy-start.1 = (bf16[768,768]{1,0:T(8,128)(2,1)S(1)}, bf16[768,768]{1,0:T(8,128)(2,1)}, u32[]{:S(2)}) copy-start(bf16[768,768]{1,0:T(8,128)(2,1)} %wk_hbm.1) | copy-start | bytes 3538948
  0.6 8.3 %copy-start.2 = (bf16[768,768]{1,0:T(8,128)(2,1)S(1)}, bf16[768,768]{1,0:T(8,128)(2,1)}, u32[]{:S(2)}) copy-start(bf16[768,768]{1,0:T(8,128)(2,1)} %wv_hbm.1) | copy-start | bytes 3538948
  0.7 8.3 %copy-start.5 = (s32[16]{0:T(128)S(1)}, s32[16]{0:T(128)}, u32[]{:S(2)}) copy-start(s32[16]{0:T(128)} %offset_ref.1) | copy-start | bytes 196
  6.7 23.6 %collective-permute-start = (bf16[512,768]{1,0:T(8,128)(2,1)S(1)}, bf16[512,768]{1,0:T(8,128)(2,1)}, u32[]{:S(2)}, u32[]{:S(2)}) collective-permute-start(bf16[512,768]{1,0:T(8,128)(2,1)S(1)} %get-tuple-element.29.x_ref), channel_id=1, source_target_pairs={{0,8},{8,0},{16,24},{24,16},{1,9},{9,1},{17,25},{25,17},{2,10},{10... | collective-permute-start | bytes 2359304 | tf_op jit(solution)/shard_map/ppermute | solution.py:28
  8.9 9.0 %copy-start.6 = (bf16[768,768]{1,0:T(8,128)(2,1)S(1)}, bf16[768,768]{1,0:T(8,128)(2,1)}, u32[]{:S(2)}) copy-start(bf16[768,768]{1,0:T(8,128)(2,1)} %wq_hbm.1) | copy-start | bytes 3538948
  10.9 11.8 %copy-start.7 = (bf16[512,384]{1,0:T(8,128)(2,1)}, bf16[512,384]{1,0:T(8,128)(2,1)S(1)}, u32[]{:S(2)}) copy-start(bf16[512,384]{1,0:T(8,128)(2,1)S(1)} %get-tuple-element.30.k_ref.k_hbm) | copy-start | bytes 1179652
  10.9 11.8 %copy-start.8 = (bf16[512,384]{1,0:T(8,128)(2,1)}, bf16[512,384]{1,0:T(8,128)(2,1)S(1)}, u32[]{:S(2)}) copy-start(bf16[512,384]{1,0:T(8,128)(2,1)S(1)} %get-tuple-element.31.v_ref.v_hbm) | copy-start | bytes 1179652
  10.9 11.8 %collective-permute-start.1 = (bf16[2,16,768]{2,1,0:T(8,128)(2,1)S(1)}, bf16[2,16,768]{2,1,0:T(8,128)(2,1)S(1)}, u32[]{:S(2)}, u32[]{:S(2)}) collective-permute-start(bf16[2,16,768]{2,1,0:T(8,128)(2,1)S(1)} %get-tuple-element.36.own_ref), channel_id=1, source_target_pairs={{0,32},{32,0},{1,33},{33,1},{2,34},{34,2},{3,35},{35,3},{4,36},{36... | collective-permute-start | bytes 147464 | tf_op jit(solution)/shard_map/ppermute | solution.py:28
  23.7 20.6 %all-to-all-start = ((bf16[16,32,768]{2,1,0:T(8,128)(2,1)}), bf16[16,32,768]{2,1,0:T(8,128)(2,1)S(1)}, u32[]{:S(2)}, u32[]{:S(2)}) async-start(bf16[16,32,768]{2,1,0:T(8,128)(2,1)} %bitcast.2), calls=%async_computation | async-start | bytes 1572864 | tf_op jit(solution)/shard_map/all_to_all | solution.py:408
  44.2 0.9 copy-start.9
  45.1 21.8 %copy-start = (bf16[768,768]{1,0:T(8,128)(2,1)S(1)}, bf16[768,768]{1,0:T(8,128)(2,1)}, u32[]{:S(2)}) copy-start(bf16[768,768]{1,0:T(8,128)(2,1)} %w_out_ref.1) | copy-start | bytes 3538948
  45.1 21.8 %copy-start.10 = (bf16[512,768]{1,0:T(8,128)(2,1)S(1)}, bf16[512,768]{1,0:T(8,128)(2,1)}, u32[]{:S(2)}) copy-start(bf16[512,768]{1,0:T(8,128)(2,1)} %get-tuple-element.42) | copy-start | bytes 2359300
  56.1 21.6 %all-to-all-start.1 = ((f32[32,8,256]{2,1,0:T(8,128)}), f32[32,8,256]{2,1,0:T(8,128)S(1)}, u32[]{:S(2)}, u32[]{:S(2)}) async-start(f32[32,8,256]{2,1,0:T(8,128)} %get-tuple-element.40), calls=%async_computation.1 | async-start | bytes 524288 | tf_op jit(solution)/shard_map/all_to_all | solution.py:485
  66.9 11.4 %copy-start.3 = (bf16[768,768]{1,0:T(8,128)(2,1)S(1)}, bf16[768,768]{1,0:T(8,128)(2,1)}, u32[]{:S(2)}) copy-start(bf16[768,768]{1,0:T(8,128)(2,1)} %w_head_ref.1) | copy-start | bytes 3538948
  66.9 11.4 %copy-start.4 = (bf16[1,768]{1,0:T(2,128)(2,1)S(1)}, bf16[1,768]{1,0:T(2,128)(2,1)}, u32[]{:S(2)}) copy-start(bf16[1,768]{1,0:T(2,128)(2,1)} %report_ref.1) | copy-start | bytes 4612
  77.6 9.8 %collective-permute-start.2 = (bf16[512,384]{1,0:T(8,128)(2,1)}, bf16[512,384]{1,0:T(8,128)(2,1)S(1)}, u32[]{:S(2)}, u32[]{:S(2)}) collective-permute-start(bf16[512,384]{1,0:T(8,128)(2,1)} %get-tuple-element.48), channel_id=1, source_target_pairs={{0,8},{8,0},{16,24},{24,16},{1,9},{9,1},{17,25},{25,17},{2,10},{10... | collective-permute-start | bytes 1179656 | tf_op jit(solution)/shard_map/ppermute | solution.py:28
  79.6 12.9 %all-to-all-start.2 = ((f32[8,8,256]{2,1,0:T(8,128)}), f32[8,8,256]{2,1,0:T(8,128)S(1)}, u32[]{:S(2)}, u32[]{:S(2)}) async-start(f32[8,8,256]{2,1,0:T(8,128)} %get-tuple-element.46), calls=%async_computation.2 | async-start | bytes 131072 | tf_op jit(solution)/shard_map/all_to_all | solution.py:507

commit v8 on v7

--- a/solution.py
+++ b/solution.py
@@ -80,23 +80,26 @@
 
 
 def embed_kernel(x_hbm, w_hbm, gain_ref, embedded_hbm, normed_ref, sum_ref, x_scr, w_scr,
-                 embedded_scr, x_sems, w_sems, out_sems):
+                 embedded_scr, acc_scr, x_sems, w_sems, out_sems):
     rows = x_scr.shape[0] // x_sems.shape[0]
     spans = [pl.ds(i * rows, rows) for i in range(x_sems.shape[0])]
     pieces = w_sems.shape[0]
     depth = w_scr.shape[0] // pieces
     parts = [pl.ds(i * depth, depth) for i in range(pieces)]
     x_loads = started([x_hbm.at[span] for span in spans], [x_scr.at[span] for span in spans], x_sems)
-    w_loads = started([w_hbm.at[p] for p in parts], [w_scr.at[p] for p in parts], w_sems)
+    started([w_hbm.at[p] for p in parts], [w_scr.at[p] for p in parts], w_sems)
     for load in x_loads:
         load.wait()
-    total = None
-    for piece, load in enumerate(w_loads):
-        load.wait()
-        columns = slice(piece * depth, (piece + 1) * depth)
-        product = jnp.dot(x_scr[:, columns], w_scr[columns, :], preferred_element_type=F32)
-        total = product if total is None else total + product
-    embedded = total.astype(BF16)
+    acc_scr[...] = jnp.zeros_like(acc_scr)
+
+    def add_piece(piece, carry):
+        span = pl.ds(pl.multiple_of(piece * depth, depth), depth)
+        pltpu.make_async_copy(w_hbm.at[span], w_scr.at[span], w_sems.at[piece]).wait()
+        acc_scr[...] += jnp.dot(x_scr[:, span], w_scr[span, :], preferred_element_type=F32)
+        return carry
+
+    lax.fori_loop(0, pieces, add_piece, 0)
+    embedded = acc_scr[...].astype(BF16)
     embedded_scr[...] = embedded
     stores = started([embedded_scr], [embedded_hbm], out_sems)
     floats = embedded.astype(F32)
@@ -221,40 +224,47 @@
         store.wait()
 
 
-def far_kernel(q_hbm, far_hbm, near_hbm, near_lse_hbm, embedded_sum_ref, own_out, lent_out,
-               pack_ref, q_scr, far_scr, near_scr, near_lse_scr, mixed_scr, lse_scr, out_scr,
-               in_sems, out_sems, *, head_width):
+def far_kernel(q_hbm, far_hbm, near_hbm, near_lse_hbm, embedded_sum_ref, own_ref,
+               lent_ref, pack_ref, q_scr, far_scr, near_scr, near_lse_scr, mixed_scr, lse_scr, sum_scr,
+               in_sems, *, head_width):
     half = q_scr.shape[1]
-    rows = out_scr.shape[1]
-    spans = (pl.ds(0, rows), pl.ds(rows, rows))
-    sources, targets = [far_hbm], [far_scr]
-    for refs in ((q_hbm, q_scr), (near_hbm, near_scr), (near_lse_hbm, near_lse_scr)):
-        for span in spans:
-            sources.append(refs[0].at[span])
-            targets.append(refs[1].at[span])
-    loads = started(sources, targets, in_sems)
+    rows = mixed_scr.shape[0]
+    loads = started(
+        (far_hbm, q_hbm, near_hbm, near_lse_hbm), (far_scr, q_scr, near_scr, near_lse_scr), in_sems
+    )
     loads[0].wait()
-    stores = []
-    sums = []
-    for place, out in enumerate((own_out, lent_out)):
-        loads[1 + place].wait()
-        span = slice(place * rows, (place + 1) * rows)
-        attend(q_scr[span, :], far_scr[:, :half], far_scr[:, half:], head_width,
-               mixed_scr.at[place], lse_scr.at[place])
-        loads[3 + place].wait()
-        loads[5 + place].wait()
+    loads[1].wait()
+    sum_scr[...] = jnp.zeros_like(sum_scr)
+
+    def block(place, carry):
+        span = pl.ds(pl.multiple_of(place * rows, rows), rows)
+        attend(q_scr[span, :], far_scr[:, :half], far_scr[:, half:], head_width, mixed_scr, lse_scr)
+
+        @pl.when(place == 0)
+        def _():
+            loads[2].wait()
+            loads[3].wait()
+
         attended = merge_states(
-            near_scr[span, :], near_lse_scr[span, :], mixed_scr[place], lse_scr[place]
+            near_scr[span, :], near_lse_scr[span, :], mixed_scr[...], lse_scr[...]
         )
-        out_scr[place] = attended.astype(BF16)
-        stores += started((out_scr.at[place],), (out,), out_sems, place)
-        sums.append(jnp.sum(attended, axis=0, keepdims=True))
-    total = sums[0] + sums[1]
+        rounded = attended.astype(BF16)
+
+        @pl.when(place == 0)
+        def _():
+            own_ref[...] = rounded
+
+        @pl.when(place == 1)
+        def _():
+            lent_ref[...] = rounded
+
+        sum_scr[...] += jnp.sum(attended, axis=0, keepdims=True)
+        return carry
+
+    lax.fori_loop(0, q_scr.shape[0] // rows, block, 0)
     pad = jnp.zeros((1, pack_ref.shape[1] * pack_ref.shape[2] - 3 * half), F32)
-    packed = pack_row((embedded_sum_ref[...], total, pad))
+    packed = pack_row((embedded_sum_ref[...], sum_scr[...], pad))
     pack_ref[...] = jnp.broadcast_to(packed[None], pack_ref.shape)
-    for store in stores:
-        store.wait()
 
 
 def pack_row(pieces):
@@ -375,6 +385,7 @@
             pltpu.VMEM((rows, in_width), BF16),
             pltpu.VMEM((in_width, width), BF16),
             pltpu.VMEM((rows, width), BF16),
+            pltpu.VMEM((rows, width), F32),
             pltpu.SemaphoreType.DMA((2,)),
             pltpu.SemaphoreType.DMA((EMBED_PIECES,)),
             pltpu.SemaphoreType.DMA((1,)),
@@ -462,18 +473,17 @@
     own_half, lent_half, sums = pl.pallas_call(
         functools.partial(far_kernel, head_width=head_width),
         in_specs=[anywhere] * 4 + [vmem],
-        out_specs=[anywhere, anywhere, vmem],
+        out_specs=[vmem, vmem, vmem],
         out_shape=[half_rows, half_rows, jax.ShapeDtypeStruct((ranks,) + PACK, F32)],
         scratch_shapes=[
             pltpu.VMEM((2 * rows, half), BF16),
             pltpu.VMEM((ranks * far_rows, width), BF16),
             pltpu.VMEM((2 * rows, half), F32),
             pltpu.VMEM((2 * rows, half), F32),
-            pltpu.VMEM((2, rows, half), F32),
-            pltpu.VMEM((2, rows, half), F32),
-            pltpu.VMEM((2, rows, half), BF16),
-            pltpu.SemaphoreType.DMA((7,)),
-            pltpu.SemaphoreType.DMA((2,)),
+            pltpu.VMEM((rows, half), F32),
+            pltpu.VMEM((rows, half), F32),
+            pltpu.VMEM((1, half), F32),
+            pltpu.SemaphoreType.DMA((4,)),
         ],
         compiler_params=params,
         cost_estimate=pl.CostEstimate(

time: 93.9 us -> 93.9 us (level)
  transfers between devices with their start and end apart: 6 -> 6, of which waited for: 2 -> 2; matrix products, arithmetic and copies ran while one was open for 6% -> 6% of each run, Pallas kernels for 24% -> 25%
where the time goes in v8:
time: 93.9 us; the launch traced here: 93.4 us
  Pallas kernels  40.7 us (43%)
  starting transfers between devices  33.8 us (36%)
  waiting for transfers between devices  10.1 us (11%)
  matrix products  5.71 us (6%)
  between operations  2.13 us (2%)
    pallas_call x1, Pallas kernels, on_device(): pl.pallas_call(functools.partial(near_kernel, head_width=head_width, scor...  13.9 us
    pallas_call x1, Pallas kernels, on_device(): pl.pallas_call(functools.partial(far_kernel, head_width=head_width), in_s...  10.7 us
    ppermute x3, starting transfers between devices, swap_with(): lax.ppermute(x, axis, [(i, i ^ 1) for i in range(lax.axis_size(axis))])  9.89 us
    all_to_all x1, starting transfers between devices, on_device(): sums = lax.all_to_all(sums, SEQ_AXES, 0, 0, tiled=True)  9.65 us
    all_to_all x1, waiting for transfers between devices, on_device(): sums = lax.all_to_all(sums, SEQ_AXES, 0, 0, tiled=True)  7.87 us
    all_to_all x1, starting transfers between devices, on_device(): everyone = lax.all_to_all(packed, 'slide', 0, 0, tiled=True)  7.84 us
    all_to_all x1, starting transfers between devices, on_device(): lax.all_to_all(payload, ('x', 'y'), 0, 0, tiled=True)  6.47 us
    pallas_call x1, Pallas kernels, on_device(): pl.pallas_call(embed_kernel, in_specs=[anywhere, anywhere, vmem], out_spe...  6.22 us
  transfers between devices with their start and end apart: 6, of which 2 were waited for; matrix products, arithmetic and copies ran while one was open for 6% of the time, Pallas kernels for 25%

profile of v8, /device:TPU:1, one launch (start us, length us, event | category | flops | bytes accessed | tf_op | source)
XLA Modules:
  0.0 93.4 jit_solution(18315103906905677466)
XLA Ops:
  0.6 0.0 copy-start.1
  0.6 0.0 copy-start.2
  0.7 0.0 copy-start.5
  0.7 6.2 %embed.1 = (bf16[512,768]{1,0:T(8,128)(2,1)}, bf16[512,768]{1,0:T(8,128)(2,1)S(1)}, f32[1,768]{1,0:T(1,128)}) custom-call(bf16[512,1536]{1,0:T(8,128)(2,1)} %bitcast.13, bf16[1536,768]{1,0:T(8,128)(2,1)} %w_hbm.1, f32[768]{0:T(1024)} %gain_ref.1), custom_call_target="tpu_custom_call" | custom-call | tf_op jit(solution)/shard_map/embed/pallas_call | solution.py:375
  6.9 2.2 %collective-permute-start = (bf16[512,768]{1,0:T(8,128)(2,1)S(1)}, bf16[512,768]{1,0:T(8,128)(2,1)}, u32[]{:S(2)}, u32[]{:S(2)}) collective-permute-start(bf16[512,768]{1,0:T(8,128)(2,1)S(1)} %get-tuple-element.29.x_ref), channel_id=1, source_target_pairs={{0,8},{8,0},{16,24},{24,16},{1,9},{9,1},{17,25},{25,17},{2,10},{10... | collective-permute-start | bytes 2359304 | tf_op jit(solution)/shard_map/ppermute | solution.py:28
  9.1 0.0 copy-done.1
  9.1 0.0 copy-done.2
  9.1 0.0 copy-done.5
  9.1 2.0 %own_rows.1 = (bf16[2,16,768]{2,1,0:T(8,128)(2,1)S(1)}, bf16[512,384]{1,0:T(8,128)(2,1)S(1)}, bf16[512,384]{1,0:T(8,128)(2,1)S(1)}) custom-call(s32[1]{0:T(128)} %bitcast.part_ref, s32[16]{0:T(128)S(1)} %copy-done.5, bf16[512,768]{1,0:T(8,128)(2,1)S(1)} %get-tuple-element.29.x_ref, bf16[768,768]{1,0:T(8,128)(2,1)S(1)} %copy-done.1, ...), custom_call_target="tpu_custom_call" | custom-call | tf_op jit(solution)/shard_map/own_rows/pallas_call | solution.py:399
  11.1 7.0 %collective-permute-start.1 = (bf16[2,16,768]{2,1,0:T(8,128)(2,1)S(1)}, bf16[2,16,768]{2,1,0:T(8,128)(2,1)S(1)}, u32[]{:S(2)}, u32[]{:S(2)}) collective-permute-start(bf16[2,16,768]{2,1,0:T(8,128)(2,1)S(1)} %get-tuple-element.36.own_ref), channel_id=1, source_target_pairs={{0,32},{32,0},{1,33},{33,1},{2,34},{34,2},{3,35},{35,3},{4,36},{36... | collective-permute-start | bytes 147464 | tf_op jit(solution)/shard_map/ppermute | solution.py:28
  18.1 4.7 %own_attention.1 = (bf16[512,384]{1,0:T(8,128)(2,1)}, f32[512,384]{1,0:T(8,128)}, f32[512,384]{1,0:T(8,128)}) custom-call(s32[1]{0:T(128)} %bitcast.part_ref, bf16[512,768]{1,0:T(8,128)(2,1)S(1)} %get-tuple-element.29.x_ref, bf16[768,768]{1,0:T(8,128)(2,1)S(1)} %copy-done.6, bf16[512,384]{1,0:T(8,128)(2,1)S(1)} %get-tuple-element.30.k_ref.k_hbm, ...), custom_call_target="tpu_custom_call" | custom-call | flops 3000000000 | bytes 4000000 | tf_op jit(solution)/shard_map/own_attention/pallas_call | solution.py:423
  22.9 0.0 collective-permute-done.1.other_ref
  22.9 1.0 %payload.1 = bf16[8,2,2,16,768]{4,3,2,1,0:T(8,128)(2,1)} custom-call(bf16[2,16,768]{2,1,0:T(8,128)(2,1)S(1)} %get-tuple-element.36.own_ref, bf16[2,16,768]{2,1,0:T(8,128)(2,1)S(1)} %collective-permute-done.1.other_ref), custom_call_target="tpu_custom_call" | custom-call | tf_op jit(solution)/shard_map/payload/pallas_call | solution.py:412
  23.9 6.5 %all-to-all-start = ((bf16[16,32,768]{2,1,0:T(8,128)(2,1)}), bf16[16,32,768]{2,1,0:T(8,128)(2,1)S(1)}, u32[]{:S(2)}, u32[]{:S(2)}) async-start(bf16[16,32,768]{2,1,0:T(8,128)(2,1)} %bitcast.2), calls=%async_computation | async-start | bytes 1572864 | tf_op jit(solution)/shard_map/all_to_all | solution.py:419
  30.3 0.0 collective-permute-done.other_hbm
  30.3 13.9 %near_attention.1 = (bf16[1024,384]{1,0:T(8,128)(2,1)}, f32[1024,384]{1,0:T(8,128)}, f32[1024,384]{1,0:T(8,128)}) custom-call(s32[1]{0:T(128)} %bitcast.part_ref, bf16[512,768]{1,0:T(8,128)(2,1)} %collective-permute-done.other_hbm, bf16[512,384]{1,0:T(8,128)(2,1)} %copy-done.7, bf16[512,384]{1,0:T(8,128)(2,1)} %copy-done.8, ...), custom_call_target="tpu_custom_call" | custom-call | flops 8999999488 | bytes 8000000 | tf_op jit(solution)/shard_map/near_attention/pallas_call | solution.py:447
  44.3 0.0 all-to-all-done
  44.3 0.0 copy-start.9
  44.3 0.9 copy-done.9
  45.2 10.7 %far_attention.1 = (bf16[512,384]{1,0:T(8,128)(2,1)}, bf16[512,384]{1,0:T(8,128)(2,1)}, f32[32,8,256]{2,1,0:T(8,128)}) custom-call(bf16[1024,384]{1,0:T(8,128)(2,1)} %get-tuple-element.35.q_hbm, bf16[512,768]{1,0:T(8,128)(2,1)} %bitcast.14, f32[1024,384]{1,0:T(8,128)} %get-tuple-element.37.near_hbm, f32[1024,384]{1,0:T(8,128)} %get-tuple-element.38.near_lse_hbm, ...), custom_call_target="tpu_custom_call" | custom-call | flops 6000000000 | bytes 6000000 | tf_op jit(solution)/shard_map/far_attention/pallas_call | solution.py:473
  55.8 9.6 %all-to-all-start.1 = ((f32[32,8,256]{2,1,0:T(8,128)}), f32[32,8,256]{2,1,0:T(8,128)S(1)}, u32[]{:S(2)}, u32[]{:S(2)}) async-start(f32[32,8,256]{2,1,0:T(8,128)} %get-tuple-element.40), calls=%async_computation.1 | async-start | bytes 524288 | tf_op jit(solution)/shard_map/all_to_all | solution.py:495
  66.8 0.0 copy-start.3
  66.8 0.0 copy-start.4
  66.9 2.8 %convert_add_fusion = f32[512,768]{1,0:T(8,128)} fusion(bf16[512,768]{1,0:T(8,128)(2,1)S(1)} %copy-done.10, bf16[512,384]{1,0:T(8,128)(2,1)} %get-tuple-element.43, bf16[768,768]{1,0:T(8,128)(2,1)S(1)} %copy-done, s32[]{:T(128)S(6)} %select_n.22), kind=kOutput, calls=%fused_computation.1 | convolution fusion | flops 302776320 | bytes 3342340 | tf_op jit(solution)/shard_map/dot_general | solution.py:500
  69.7 7.9 %all-to-all-done.1.sums_ref = f32[32,8,256]{2,1,0:T(8,128)S(1)} async-done(((f32[32,8,256]{2,1,0:T(8,128)}), f32[32,8,256]{2,1,0:T(8,128)S(1)}, u32[]{:S(2)}, u32[]{:S(2)}) %all-to-all-start.1) | async-done | bytes 262176 | tf_op jit(solution)/shard_map/all_to_all | solution.py:495
  77.6 0.7 collective-permute-start.2
  78.3 1.3 %pooled.1 = (f32[1,768]{1,0:T(1,128)}, f32[8,8,256]{2,1,0:T(8,128)}) custom-call(f32[512]{0:T(512)S(1)} %select_convert_fusion.codes_ref, f32[32,8,256]{2,1,0:T(8,128)S(1)} %all-to-all-done.1.sums_ref, bf16[768,768]{1,0:T(8,128)(2,1)S(1)} %copy-done, bf16[768,768]{1,0:T(8,128)(2,1)S(1)} %copy-done.3, bf16[1,768]{1,0:T(2,128)(2,1)S(1)} %copy-done.4), custom_call_target="tpu_custom_call" | custom-call | tf_op jit(solution)/shard_map/pooled/pallas_call | solution.py:507
  79.6 7.8 %all-to-all-start.2 = ((f32[8,8,256]{2,1,0:T(8,128)}), f32[8,8,256]{2,1,0:T(8,128)S(1)}, u32[]{:S(2)}, u32[]{:S(2)}) async-start(f32[8,8,256]{2,1,0:T(8,128)} %get-tuple-element.46), calls=%async_computation.2 | async-start | bytes 131072 | tf_op jit(solution)/shard_map/all_to_all | solution.py:517
  87.4 0.0 collective-permute-done.2
  87.4 2.9 %fusion = bf16[1,512,768]{2,1,0:T(8,128)(2,1)} fusion(f32[512,768]{1,0:T(8,128)} %convert_add_fusion, bf16[512,384]{1,0:T(8,128)(2,1)S(1)} %collective-permute-done.2, bf16[768,768]{1,0:T(8,128)(2,1)S(1)} %copy-done, s32[]{:T(128)S(6)} %select_n.25), kind=kOutput, calls=%fused_computation.2 | convolution fusion | flops 302776320 | bytes 3342340 | tf_op jit(solution)/shard_map/dot_general | solution.py:503
  90.3 2.2 %all-to-all-done.2.all_ref = f32[8,8,256]{2,1,0:T(8,128)S(1)} async-done(((f32[8,8,256]{2,1,0:T(8,128)}), f32[8,8,256]{2,1,0:T(8,128)S(1)}, u32[]{:S(2)}, u32[]{:S(2)}) %all-to-all-start.2) | async-done | bytes 65568 | tf_op jit(solution)/shard_map/all_to_all | solution.py:517
  92.5 1.0 %contrast.1 = (f32[8,8]{1,0:T(8,128)}, f32[1,1]{1,0:T(1,128)}) custom-call(f32[8,8,256]{2,1,0:T(8,128)S(1)} %all-to-all-done.2.all_ref), custom_call_target="tpu_custom_call" | custom-call | tf_op jit(solution)/shard_map/contrast/pallas_call | solution.py:519
  (13 shorter events, 0.0 us)
Async XLA Ops:
  0.6 8.5 %copy-start.1 = (bf16[768,768]{1,0:T(8,128)(2,1)S(1)}, bf16[768,768]{1,0:T(8,128)(2,1)}, u32[]{:S(2)}) copy-start(bf16[768,768]{1,0:T(8,128)(2,1)} %wk_hbm.1) | copy-start | bytes 3538948
  0.6 8.5 %copy-start.2 = (bf16[768,768]{1,0:T(8,128)(2,1)S(1)}, bf16[768,768]{1,0:T(8,128)(2,1)}, u32[]{:S(2)}) copy-start(bf16[768,768]{1,0:T(8,128)(2,1)} %wv_hbm.1) | copy-start | bytes 3538948
  0.7 8.5 %copy-start.5 = (s32[16]{0:T(128)S(1)}, s32[16]{0:T(128)}, u32[]{:S(2)}) copy-start(s32[16]{0:T(128)} %offset_ref.1) | copy-start | bytes 196
  6.9 23.4 %collective-permute-start = (bf16[512,768]{1,0:T(8,128)(2,1)S(1)}, bf16[512,768]{1,0:T(8,128)(2,1)}, u32[]{:S(2)}, u32[]{:S(2)}) collective-permute-start(bf16[512,768]{1,0:T(8,128)(2,1)S(1)} %get-tuple-element.29.x_ref), channel_id=1, source_target_pairs={{0,8},{8,0},{16,24},{24,16},{1,9},{9,1},{17,25},{25,17},{2,10},{10... | collective-permute-start | bytes 2359304 | tf_op jit(solution)/shard_map/ppermute | solution.py:28
  9.1 9.0 %copy-start.6 = (bf16[768,768]{1,0:T(8,128)(2,1)S(1)}, bf16[768,768]{1,0:T(8,128)(2,1)}, u32[]{:S(2)}) copy-start(bf16[768,768]{1,0:T(8,128)(2,1)} %wq_hbm.1) | copy-start | bytes 3538948
  11.1 11.8 %copy-start.7 = (bf16[512,384]{1,0:T(8,128)(2,1)}, bf16[512,384]{1,0:T(8,128)(2,1)S(1)}, u32[]{:S(2)}) copy-start(bf16[512,384]{1,0:T(8,128)(2,1)S(1)} %get-tuple-element.30.k_ref.k_hbm) | copy-start | bytes 1179652
  11.1 11.8 %copy-start.8 = (bf16[512,384]{1,0:T(8,128)(2,1)}, bf16[512,384]{1,0:T(8,128)(2,1)S(1)}, u32[]{:S(2)}) copy-start(bf16[512,384]{1,0:T(8,128)(2,1)S(1)} %get-tuple-element.31.v_ref.v_hbm) | copy-start | bytes 1179652
  11.1 11.8 %collective-permute-start.1 = (bf16[2,16,768]{2,1,0:T(8,128)(2,1)S(1)}, bf16[2,16,768]{2,1,0:T(8,128)(2,1)S(1)}, u32[]{:S(2)}, u32[]{:S(2)}) collective-permute-start(bf16[2,16,768]{2,1,0:T(8,128)(2,1)S(1)} %get-tuple-element.36.own_ref), channel_id=1, source_target_pairs={{0,32},{32,0},{1,33},{33,1},{2,34},{34,2},{3,35},{35,3},{4,36},{36... | collective-permute-start | bytes 147464 | tf_op jit(solution)/shard_map/ppermute | solution.py:28
  23.9 20.4 %all-to-all-start = ((bf16[16,32,768]{2,1,0:T(8,128)(2,1)}), bf16[16,32,768]{2,1,0:T(8,128)(2,1)S(1)}, u32[]{:S(2)}, u32[]{:S(2)}) async-start(bf16[16,32,768]{2,1,0:T(8,128)(2,1)} %bitcast.2), calls=%async_computation | async-start | bytes 1572864 | tf_op jit(solution)/shard_map/all_to_all | solution.py:419
  44.3 0.9 copy-start.9
  45.2 21.6 %copy-start = (bf16[768,768]{1,0:T(8,128)(2,1)S(1)}, bf16[768,768]{1,0:T(8,128)(2,1)}, u32[]{:S(2)}) copy-start(bf16[768,768]{1,0:T(8,128)(2,1)} %w_out_ref.1) | copy-start | bytes 3538948
  45.2 21.7 %copy-start.10 = (bf16[512,768]{1,0:T(8,128)(2,1)S(1)}, bf16[512,768]{1,0:T(8,128)(2,1)}, u32[]{:S(2)}) copy-start(bf16[512,768]{1,0:T(8,128)(2,1)} %get-tuple-element.42) | copy-start | bytes 2359300
  55.8 21.7 %all-to-all-start.1 = ((f32[32,8,256]{2,1,0:T(8,128)}), f32[32,8,256]{2,1,0:T(8,128)S(1)}, u32[]{:S(2)}, u32[]{:S(2)}) async-start(f32[32,8,256]{2,1,0:T(8,128)} %get-tuple-element.40), calls=%async_computation.1 | async-start | bytes 524288 | tf_op jit(solution)/shard_map/all_to_all | solution.py:495
  66.8 11.4 %copy-start.3 = (bf16[768,768]{1,0:T(8,128)(2,1)S(1)}, bf16[768,768]{1,0:T(8,128)(2,1)}, u32[]{:S(2)}) copy-start(bf16[768,768]{1,0:T(8,128)(2,1)} %w_head_ref.1) | copy-start | bytes 3538948
  66.8 11.4 %copy-start.4 = (bf16[1,768]{1,0:T(2,128)(2,1)S(1)}, bf16[1,768]{1,0:T(2,128)(2,1)}, u32[]{:S(2)}) copy-start(bf16[1,768]{1,0:T(2,128)(2,1)} %report_ref.1) | copy-start | bytes 4612
  77.6 9.8 %collective-permute-start.2 = (bf16[512,384]{1,0:T(8,128)(2,1)}, bf16[512,384]{1,0:T(8,128)(2,1)S(1)}, u32[]{:S(2)}, u32[]{:S(2)}) collective-permute-start(bf16[512,384]{1,0:T(8,128)(2,1)} %get-tuple-element.48), channel_id=1, source_target_pairs={{0,8},{8,0},{16,24},{24,16},{1,9},{9,1},{17,25},{25,17},{2,10},{10... | collective-permute-start | bytes 1179656 | tf_op jit(solution)/shard_map/ppermute | solution.py:28
  79.6 12.9 %all-to-all-start.2 = ((f32[8,8,256]{2,1,0:T(8,128)}), f32[8,8,256]{2,1,0:T(8,128)S(1)}, u32[]{:S(2)}, u32[]{:S(2)}) async-start(f32[8,8,256]{2,1,0:T(8,128)} %get-tuple-element.46), calls=%async_computation.2 | async-start | bytes 131072 | tf_op jit(solution)/shard_map/all_to_all | solution.py:517

commit v9 on v8

--- a/solution.py
+++ b/solution.py
@@ -80,26 +80,23 @@
 
 
 def embed_kernel(x_hbm, w_hbm, gain_ref, embedded_hbm, normed_ref, sum_ref, x_scr, w_scr,
-                 embedded_scr, acc_scr, x_sems, w_sems, out_sems):
+                 embedded_scr, x_sems, w_sems, out_sems):
     rows = x_scr.shape[0] // x_sems.shape[0]
     spans = [pl.ds(i * rows, rows) for i in range(x_sems.shape[0])]
     pieces = w_sems.shape[0]
     depth = w_scr.shape[0] // pieces
     parts = [pl.ds(i * depth, depth) for i in range(pieces)]
     x_loads = started([x_hbm.at[span] for span in spans], [x_scr.at[span] for span in spans], x_sems)
-    started([w_hbm.at[p] for p in parts], [w_scr.at[p] for p in parts], w_sems)
+    w_loads = started([w_hbm.at[p] for p in parts], [w_scr.at[p] for p in parts], w_sems)
     for load in x_loads:
         load.wait()
-    acc_scr[...] = jnp.zeros_like(acc_scr)
-
-    def add_piece(piece, carry):
-        span = pl.ds(pl.multiple_of(piece * depth, depth), depth)
-        pltpu.make_async_copy(w_hbm.at[span], w_scr.at[span], w_sems.at[piece]).wait()
-        acc_scr[...] += jnp.dot(x_scr[:, span], w_scr[span, :], preferred_element_type=F32)
-        return carry
-
-    lax.fori_loop(0, pieces, add_piece, 0)
-    embedded = acc_scr[...].astype(BF16)
+    total = None
+    for piece, load in enumerate(w_loads):
+        load.wait()
+        columns = slice(piece * depth, (piece + 1) * depth)
+        product = jnp.dot(x_scr[:, columns], w_scr[columns, :], preferred_element_type=F32)
+        total = product if total is None else total + product
+    embedded = total.astype(BF16)
     embedded_scr[...] = embedded
     stores = started([embedded_scr], [embedded_hbm], out_sems)
     floats = embedded.astype(F32)
@@ -145,7 +142,7 @@
 
 
 def own_kernel(part_ref, x_ref, wq_ref, k_ref, v_ref, q_out, mixed_out, lse_out,
-               q_scr, mixed_scr, lse_scr, out_sems, *, head_width, score_scale):
+               q_scr, mixed_scr, lse_scr, rounded_scr, out_sems, *, head_width, score_scale):
     half = wq_ref.shape[1] // 2
     upper = part_ref[0] == 1
     wq = jnp.where(upper, wq_ref[:, half:], wq_ref[:, :half])
@@ -154,9 +151,10 @@
     stores = started((q_scr,), (q_out,), out_sems)
 
     def finish(tile, lanes):
+        rounded_scr[:, lanes] = mixed_scr[:, lanes].astype(BF16)
         stores.extend(
             started(
-                (mixed_scr.at[:, lanes], lse_scr.at[:, lanes]),
+                (rounded_scr.at[:, lanes], lse_scr.at[:, lanes]),
                 (mixed_out.at[:, lanes], lse_out.at[:, lanes]),
                 out_sems,
                 1 + 2 * tile,
@@ -171,7 +169,7 @@
 def near_kernel(part_ref, other_hbm, k_hbm, v_hbm, q_hbm, own_mixed_hbm, own_lse_hbm,
                 wq_hbm, wk_hbm, wv_hbm, q_out, mixed_out, lse_out,
                 x_scr, w_scr, k_scr, v_scr, q_scr, own_mixed_scr, own_lse_scr, mixed_scr, lse_scr,
-                in_sems, out_sems, *, head_width, score_scale):
+                rounded_scr, in_sems, out_sems, *, head_width, score_scale):
     rows = x_scr.shape[0]
     own, other = pl.ds(0, rows), pl.ds(rows, rows)
     loads = started(
@@ -198,9 +196,10 @@
     loads[5].wait()
 
     def store_block(place, span, first):
+        rounded_scr[place] = mixed_scr[place].astype(BF16)
         stores.extend(
             started(
-                (mixed_scr.at[place], lse_scr.at[place]),
+                (rounded_scr.at[place], lse_scr.at[place]),
                 (mixed_out.at[span], lse_out.at[span]),
                 out_sems,
                 first,
@@ -216,7 +215,7 @@
     loads[7].wait()
     loads[8].wait()
     own_lse, new_lse = own_lse_scr[...], lse_scr[0]
-    mixed_scr[0] = merge_states(own_mixed_scr[...], own_lse, mixed_scr[0], new_lse)
+    mixed_scr[0] = merge_states(own_mixed_scr[...].astype(F32), own_lse, mixed_scr[0], new_lse)
     gap = jnp.exp(-jnp.abs(own_lse - new_lse))
     lse_scr[0] = jnp.maximum(own_lse, new_lse) + jnp.log(1.0 + gap)
     store_block(0, own, 4)
@@ -246,7 +245,7 @@
             loads[3].wait()
 
         attended = merge_states(
-            near_scr[span, :], near_lse_scr[span, :], mixed_scr[...], lse_scr[...]
+            near_scr[span, :].astype(F32), near_lse_scr[span, :], mixed_scr[...], lse_scr[...]
         )
         rounded = attended.astype(BF16)
 
@@ -385,7 +384,6 @@
             pltpu.VMEM((rows, in_width), BF16),
             pltpu.VMEM((in_width, width), BF16),
             pltpu.VMEM((rows, width), BF16),
-            pltpu.VMEM((rows, width), F32),
             pltpu.SemaphoreType.DMA((2,)),
             pltpu.SemaphoreType.DMA((EMBED_PIECES,)),
             pltpu.SemaphoreType.DMA((1,)),
@@ -426,13 +424,14 @@
         out_specs=[anywhere] * 3,
         out_shape=[
             pltpu.HBM((rows, half), BF16),
-            pltpu.HBM((rows, half), F32),
+            pltpu.HBM((rows, half), BF16),
             pltpu.HBM((rows, half), F32),
         ],
         scratch_shapes=[
             pltpu.VMEM((rows, half), BF16),
             pltpu.VMEM((rows, half), F32),
             pltpu.VMEM((rows, half), F32),
+            pltpu.VMEM((rows, half), BF16),
             pltpu.SemaphoreType.DMA((1 + 2 * lane_tiles,)),
         ],
         compiler_params=pltpu.CompilerParams(vmem_limit_bytes=32 << 20),
@@ -448,17 +447,18 @@
         functools.partial(near_kernel, head_width=head_width, score_scale=score_scale),
         in_specs=[smem] + [anywhere] * 9,
         out_specs=[anywhere] * 3,
-        out_shape=[both_rows, both_state, both_state],
+        out_shape=[both_rows, both_rows, both_state],
         scratch_shapes=[
             pltpu.VMEM((rows, width), BF16),
             pltpu.VMEM((3, width, half), BF16),
             pltpu.VMEM((2 * rows, half), BF16),
             pltpu.VMEM((2 * rows, half), BF16),
             pltpu.VMEM((2 * rows, half), BF16),
-            pltpu.VMEM((rows, half), F32),
+            pltpu.VMEM((rows, half), BF16),
             pltpu.VMEM((rows, half), F32),
             pltpu.VMEM((2, rows, half), F32),
             pltpu.VMEM((2, rows, half), F32),
+            pltpu.VMEM((2, rows, half), BF16),
             pltpu.SemaphoreType.DMA((9,)),
             pltpu.SemaphoreType.DMA((6,)),
         ],
@@ -478,7 +478,7 @@
         scratch_shapes=[
             pltpu.VMEM((2 * rows, half), BF16),
             pltpu.VMEM((ranks * far_rows, width), BF16),
-            pltpu.VMEM((2 * rows, half), F32),
+            pltpu.VMEM((2 * rows, half), BF16),
             pltpu.VMEM((2 * rows, half), F32),
             pltpu.VMEM((rows, half), F32),
             pltpu.VMEM((rows, half), F32),

time: 93.9 us -> 94.3 us (level)
  no operation moved by 1% of the time
where the time goes in v9:
time: 94.3 us; the launch traced here: 93.8 us
  Pallas kernels  40.9 us (43%)
  starting transfers between devices  34 us (36%)
  waiting for transfers between devices  10.1 us (11%)
  matrix products  5.71 us (6%)
  between operations  2.13 us (2%)
    pallas_call x1, Pallas kernels, on_device(): pl.pallas_call(functools.partial(near_kernel, head_width=head_width, scor...  14.5 us
    pallas_call x1, Pallas kernels, on_device(): pl.pallas_call(functools.partial(far_kernel, head_width=head_width), in_s...  10.7 us
    ppermute x3, starting transfers between devices, swap_with(): lax.ppermute(x, axis, [(i, i ^ 1) for i in range(lax.axis_size(axis))])  9.88 us
    all_to_all x1, starting transfers between devices, on_device(): sums = lax.all_to_all(sums, SEQ_AXES, 0, 0, tiled=True)  9.79 us
    all_to_all x1, waiting for transfers between devices, on_device(): sums = lax.all_to_all(sums, SEQ_AXES, 0, 0, tiled=True)  7.87 us
    all_to_all x1, starting transfers between devices, on_device(): everyone = lax.all_to_all(packed, 'slide', 0, 0, tiled=True)  7.87 us
    all_to_all x1, starting transfers between devices, on_device(): lax.all_to_all(payload, ('x', 'y'), 0, 0, tiled=True)  6.47 us
    pallas_call x1, Pallas kernels, on_device(): pl.pallas_call(embed_kernel, in_specs=[anywhere, anywhere, vmem], out_spe...  6.02 us
  transfers between devices with their start and end apart: 6, of which 2 were waited for; matrix products, arithmetic and copies ran while one was open for 6% of the time, Pallas kernels for 25%

profile of v9, /device:TPU:1, one launch (start us, length us, event | category | flops | bytes accessed | tf_op | source)
XLA Modules:
  0.0 93.8 jit_solution(17451689137538018877)
XLA Ops:
  0.6 0.0 copy-start.1
  0.6 0.0 copy-start.2
  0.7 0.0 copy-start.5
  0.7 6.0 %embed.1 = (bf16[512,768]{1,0:T(8,128)(2,1)}, bf16[512,768]{1,0:T(8,128)(2,1)S(1)}, f32[1,768]{1,0:T(1,128)}) custom-call(bf16[512,1536]{1,0:T(8,128)(2,1)} %bitcast.13, bf16[1536,768]{1,0:T(8,128)(2,1)} %w_hbm.1, f32[768]{0:T(1024)} %gain_ref.1), custom_call_target="tpu_custom_call" | custom-call | tf_op jit(solution)/shard_map/embed/pallas_call | solution.py:374
  6.7 2.2 %collective-permute-start = (bf16[512,768]{1,0:T(8,128)(2,1)S(1)}, bf16[512,768]{1,0:T(8,128)(2,1)}, u32[]{:S(2)}, u32[]{:S(2)}) collective-permute-start(bf16[512,768]{1,0:T(8,128)(2,1)S(1)} %get-tuple-element.29.x_ref), channel_id=1, source_target_pairs={{0,8},{8,0},{16,24},{24,16},{1,9},{9,1},{17,25},{25,17},{2,10},{10... | collective-permute-start | bytes 2359304 | tf_op jit(solution)/shard_map/ppermute | solution.py:28
  8.9 0.0 copy-done.1
  8.9 0.0 copy-done.2
  8.9 2.0 %own_rows.1 = (bf16[2,16,768]{2,1,0:T(8,128)(2,1)S(1)}, bf16[512,384]{1,0:T(8,128)(2,1)S(1)}, bf16[512,384]{1,0:T(8,128)(2,1)S(1)}) custom-call(s32[1]{0:T(128)} %bitcast.part_ref, s32[16]{0:T(128)S(1)} %copy-done.5, bf16[512,768]{1,0:T(8,128)(2,1)S(1)} %get-tuple-element.29.x_ref, bf16[768,768]{1,0:T(8,128)(2,1)S(1)} %copy-done.1, ...), custom_call_target="tpu_custom_call" | custom-call | tf_op jit(solution)/shard_map/own_rows/pallas_call | solution.py:397
  10.9 7.0 %collective-permute-start.1 = (bf16[2,16,768]{2,1,0:T(8,128)(2,1)S(1)}, bf16[2,16,768]{2,1,0:T(8,128)(2,1)S(1)}, u32[]{:S(2)}, u32[]{:S(2)}) collective-permute-start(bf16[2,16,768]{2,1,0:T(8,128)(2,1)S(1)} %get-tuple-element.36.own_ref), channel_id=1, source_target_pairs={{0,32},{32,0},{1,33},{33,1},{2,34},{34,2},{3,35},{35,3},{4,36},{36... | collective-permute-start | bytes 147464 | tf_op jit(solution)/shard_map/ppermute | solution.py:28
  17.9 4.6 %own_attention.1 = (bf16[512,384]{1,0:T(8,128)(2,1)}, bf16[512,384]{1,0:T(8,128)(2,1)}, f32[512,384]{1,0:T(8,128)}) custom-call(s32[1]{0:T(128)} %bitcast.part_ref, bf16[512,768]{1,0:T(8,128)(2,1)S(1)} %get-tuple-element.29.x_ref, bf16[768,768]{1,0:T(8,128)(2,1)S(1)} %copy-done.6, bf16[512,384]{1,0:T(8,128)(2,1)S(1)} %get-tuple-element.30.k_ref.k_hbm, ...), custom_call_target="tpu_custom_call" | custom-call | flops 3000000000 | bytes 4000000 | tf_op jit(solution)/shard_map/own_attention/pallas_call | solution.py:421
  22.5 0.0 collective-permute-done.1.other_ref
  22.5 1.0 %payload.1 = bf16[8,2,2,16,768]{4,3,2,1,0:T(8,128)(2,1)} custom-call(bf16[2,16,768]{2,1,0:T(8,128)(2,1)S(1)} %get-tuple-element.36.own_ref, bf16[2,16,768]{2,1,0:T(8,128)(2,1)S(1)} %collective-permute-done.1.other_ref), custom_call_target="tpu_custom_call" | custom-call | tf_op jit(solution)/shard_map/payload/pallas_call | solution.py:410
  23.5 6.5 %all-to-all-start = ((bf16[16,32,768]{2,1,0:T(8,128)(2,1)}), bf16[16,32,768]{2,1,0:T(8,128)(2,1)S(1)}, u32[]{:S(2)}, u32[]{:S(2)}) async-start(bf16[16,32,768]{2,1,0:T(8,128)(2,1)} %bitcast.2), calls=%async_computation | async-start | bytes 1572864 | tf_op jit(solution)/shard_map/all_to_all | solution.py:417
  30.0 0.0 collective-permute-done.other_hbm
  30.0 14.5 %near_attention.1 = (bf16[1024,384]{1,0:T(8,128)(2,1)}, bf16[1024,384]{1,0:T(8,128)(2,1)}, f32[1024,384]{1,0:T(8,128)}) custom-call(s32[1]{0:T(128)} %bitcast.part_ref, bf16[512,768]{1,0:T(8,128)(2,1)} %collective-permute-done.other_hbm, bf16[512,384]{1,0:T(8,128)(2,1)} %copy-done.7, bf16[512,384]{1,0:T(8,128)(2,1)} %copy-done.8, ...), custom_call_target="tpu_custom_call" | custom-call | flops 8999999488 | bytes 8000000 | tf_op jit(solution)/shard_map/near_attention/pallas_call | solution.py:446
  44.5 0.0 all-to-all-done
  44.5 0.0 copy-start.9
  44.5 0.9 copy-done.9
  45.4 10.7 %far_attention.1 = (bf16[512,384]{1,0:T(8,128)(2,1)}, bf16[512,384]{1,0:T(8,128)(2,1)}, f32[32,8,256]{2,1,0:T(8,128)}) custom-call(bf16[1024,384]{1,0:T(8,128)(2,1)} %get-tuple-element.35.q_hbm, bf16[512,768]{1,0:T(8,128)(2,1)} %bitcast.14, bf16[1024,384]{1,0:T(8,128)(2,1)} %get-tuple-element.37.near_hbm, f32[1024,384]{1,0:T(8,128)} %get-tuple-element.38.near_lse_hbm, ...), custom_call_target="tpu_custom_call" | custom-call | flops 6000000000 | bytes 6000000 | tf_op jit(solution)/shard_map/far_attention/pallas_call | solution.py:473
  56.1 9.8 %all-to-all-start.1 = ((f32[32,8,256]{2,1,0:T(8,128)}), f32[32,8,256]{2,1,0:T(8,128)S(1)}, u32[]{:S(2)}, u32[]{:S(2)}) async-start(f32[32,8,256]{2,1,0:T(8,128)} %get-tuple-element.40), calls=%async_computation.1 | async-start | bytes 524288 | tf_op jit(solution)/shard_map/all_to_all | solution.py:495
  67.2 0.0 copy-start.3
  67.2 0.0 copy-start.4
  67.2 2.8 %convert_add_fusion = f32[512,768]{1,0:T(8,128)} fusion(bf16[512,768]{1,0:T(8,128)(2,1)S(1)} %copy-done.10, bf16[512,384]{1,0:T(8,128)(2,1)} %get-tuple-element.43, bf16[768,768]{1,0:T(8,128)(2,1)S(1)} %copy-done, s32[]{:T(128)S(6)} %select_n.22), kind=kOutput, calls=%fused_computation.1 | convolution fusion | flops 302776320 | bytes 3342340 | tf_op jit(solution)/shard_map/dot_general | solution.py:500
  70.1 7.9 %all-to-all-done.1.sums_ref = f32[32,8,256]{2,1,0:T(8,128)S(1)} async-done(((f32[32,8,256]{2,1,0:T(8,128)}), f32[32,8,256]{2,1,0:T(8,128)S(1)}, u32[]{:S(2)}, u32[]{:S(2)}) %all-to-all-start.1) | async-done | bytes 262176 | tf_op jit(solution)/shard_map/all_to_all | solution.py:495
  77.9 0.7 collective-permute-start.2
  78.6 0.0 copy-done.4
  78.6 1.3 %pooled.1 = (f32[1,768]{1,0:T(1,128)}, f32[8,8,256]{2,1,0:T(8,128)}) custom-call(f32[512]{0:T(512)S(1)} %select_convert_fusion.codes_ref, f32[32,8,256]{2,1,0:T(8,128)S(1)} %all-to-all-done.1.sums_ref, bf16[768,768]{1,0:T(8,128)(2,1)S(1)} %copy-done, bf16[768,768]{1,0:T(8,128)(2,1)S(1)} %copy-done.3, bf16[1,768]{1,0:T(2,128)(2,1)S(1)} %copy-done.4), custom_call_target="tpu_custom_call" | custom-call | tf_op jit(solution)/shard_map/pooled/pallas_call | solution.py:507
  79.9 7.9 %all-to-all-start.2 = ((f32[8,8,256]{2,1,0:T(8,128)}), f32[8,8,256]{2,1,0:T(8,128)S(1)}, u32[]{:S(2)}, u32[]{:S(2)}) async-start(f32[8,8,256]{2,1,0:T(8,128)} %get-tuple-element.46), calls=%async_computation.2 | async-start | bytes 131072 | tf_op jit(solution)/shard_map/all_to_all | solution.py:517
  87.8 0.0 collective-permute-done.2
  87.8 2.9 %fusion = bf16[1,512,768]{2,1,0:T(8,128)(2,1)} fusion(f32[512,768]{1,0:T(8,128)} %convert_add_fusion, bf16[512,384]{1,0:T(8,128)(2,1)S(1)} %collective-permute-done.2, bf16[768,768]{1,0:T(8,128)(2,1)S(1)} %copy-done, s32[]{:T(128)S(6)} %select_n.25), kind=kOutput, calls=%fused_computation.2 | convolution fusion | flops 302776320 | bytes 3342340 | tf_op jit(solution)/shard_map/dot_general | solution.py:503
  90.6 2.2 %all-to-all-done.2.all_ref = f32[8,8,256]{2,1,0:T(8,128)S(1)} async-done(((f32[8,8,256]{2,1,0:T(8,128)}), f32[8,8,256]{2,1,0:T(8,128)S(1)}, u32[]{:S(2)}, u32[]{:S(2)}) %all-to-all-start.2) | async-done | bytes 65568 | tf_op jit(solution)/shard_map/all_to_all | solution.py:517
  92.9 1.0 %contrast.1 = (f32[8,8]{1,0:T(8,128)}, f32[1,1]{1,0:T(1,128)}) custom-call(f32[8,8,256]{2,1,0:T(8,128)S(1)} %all-to-all-done.2.all_ref), custom_call_target="tpu_custom_call" | custom-call | tf_op jit(solution)/shard_map/contrast/pallas_call | solution.py:519
  (13 shorter events, 0.0 us)
Async XLA Ops:
  0.6 8.3 %copy-start.1 = (bf16[768,768]{1,0:T(8,128)(2,1)S(1)}, bf16[768,768]{1,0:T(8,128)(2,1)}, u32[]{:S(2)}) copy-start(bf16[768,768]{1,0:T(8,128)(2,1)} %wk_hbm.1) | copy-start | bytes 3538948
  0.6 8.3 %copy-start.2 = (bf16[768,768]{1,0:T(8,128)(2,1)S(1)}, bf16[768,768]{1,0:T(8,128)(2,1)}, u32[]{:S(2)}) copy-start(bf16[768,768]{1,0:T(8,128)(2,1)} %wv_hbm.1) | copy-start | bytes 3538948
  0.7 8.3 %copy-start.5 = (s32[16]{0:T(128)S(1)}, s32[16]{0:T(128)}, u32[]{:S(2)}) copy-start(s32[16]{0:T(128)} %offset_ref.1) | copy-start | bytes 196
  6.7 23.3 %collective-permute-start = (bf16[512,768]{1,0:T(8,128)(2,1)S(1)}, bf16[512,768]{1,0:T(8,128)(2,1)}, u32[]{:S(2)}, u32[]{:S(2)}) collective-permute-start(bf16[512,768]{1,0:T(8,128)(2,1)S(1)} %get-tuple-element.29.x_ref), channel_id=1, source_target_pairs={{0,8},{8,0},{16,24},{24,16},{1,9},{9,1},{17,25},{25,17},{2,10},{10... | collective-permute-start | bytes 2359304 | tf_op jit(solution)/shard_map/ppermute | solution.py:28
  8.9 9.0 %copy-start.6 = (bf16[768,768]{1,0:T(8,128)(2,1)S(1)}, bf16[768,768]{1,0:T(8,128)(2,1)}, u32[]{:S(2)}) copy-start(bf16[768,768]{1,0:T(8,128)(2,1)} %wq_hbm.1) | copy-start | bytes 3538948
  10.9 11.6 %copy-start.7 = (bf16[512,384]{1,0:T(8,128)(2,1)}, bf16[512,384]{1,0:T(8,128)(2,1)S(1)}, u32[]{:S(2)}) copy-start(bf16[512,384]{1,0:T(8,128)(2,1)S(1)} %get-tuple-element.30.k_ref.k_hbm) | copy-start | bytes 1179652
  10.9 11.6 %copy-start.8 = (bf16[512,384]{1,0:T(8,128)(2,1)}, bf16[512,384]{1,0:T(8,128)(2,1)S(1)}, u32[]{:S(2)}) copy-start(bf16[512,384]{1,0:T(8,128)(2,1)S(1)} %get-tuple-element.31.v_ref.v_hbm) | copy-start | bytes 1179652
  10.9 11.6 %collective-permute-start.1 = (bf16[2,16,768]{2,1,0:T(8,128)(2,1)S(1)}, bf16[2,16,768]{2,1,0:T(8,128)(2,1)S(1)}, u32[]{:S(2)}, u32[]{:S(2)}) collective-permute-start(bf16[2,16,768]{2,1,0:T(8,128)(2,1)S(1)} %get-tuple-element.36.own_ref), channel_id=1, source_target_pairs={{0,32},{32,0},{1,33},{33,1},{2,34},{34,2},{3,35},{35,3},{4,36},{36... | collective-permute-start | bytes 147464 | tf_op jit(solution)/shard_map/ppermute | solution.py:28
  23.5 21.0 %all-to-all-start = ((bf16[16,32,768]{2,1,0:T(8,128)(2,1)}), bf16[16,32,768]{2,1,0:T(8,128)(2,1)S(1)}, u32[]{:S(2)}, u32[]{:S(2)}) async-start(bf16[16,32,768]{2,1,0:T(8,128)(2,1)} %bitcast.2), calls=%async_computation | async-start | bytes 1572864 | tf_op jit(solution)/shard_map/all_to_all | solution.py:417
  44.5 0.9 copy-start.9
  45.4 21.8 %copy-start = (bf16[768,768]{1,0:T(8,128)(2,1)S(1)}, bf16[768,768]{1,0:T(8,128)(2,1)}, u32[]{:S(2)}) copy-start(bf16[768,768]{1,0:T(8,128)(2,1)} %w_out_ref.1) | copy-start | bytes 3538948
  45.4 21.8 %copy-start.10 = (bf16[512,768]{1,0:T(8,128)(2,1)S(1)}, bf16[512,768]{1,0:T(8,128)(2,1)}, u32[]{:S(2)}) copy-start(bf16[512,768]{1,0:T(8,128)(2,1)} %get-tuple-element.42) | copy-start | bytes 2359300
  56.1 21.9 %all-to-all-start.1 = ((f32[32,8,256]{2,1,0:T(8,128)}), f32[32,8,256]{2,1,0:T(8,128)S(1)}, u32[]{:S(2)}, u32[]{:S(2)}) async-start(f32[32,8,256]{2,1,0:T(8,128)} %get-tuple-element.40), calls=%async_computation.1 | async-start | bytes 524288 | tf_op jit(solution)/shard_map/all_to_all | solution.py:495
  67.2 11.4 %copy-start.3 = (bf16[768,768]{1,0:T(8,128)(2,1)S(1)}, bf16[768,768]{1,0:T(8,128)(2,1)}, u32[]{:S(2)}) copy-start(bf16[768,768]{1,0:T(8,128)(2,1)} %w_head_ref.1) | copy-start | bytes 3538948
  67.2 11.4 %copy-start.4 = (bf16[1,768]{1,0:T(2,128)(2,1)S(1)}, bf16[1,768]{1,0:T(2,128)(2,1)}, u32[]{:S(2)}) copy-start(bf16[1,768]{1,0:T(2,128)(2,1)} %report_ref.1) | copy-start | bytes 4612
  77.9 9.8 %collective-permute-start.2 = (bf16[512,384]{1,0:T(8,128)(2,1)}, bf16[512,384]{1,0:T(8,128)(2,1)S(1)}, u32[]{:S(2)}, u32[]{:S(2)}) collective-permute-start(bf16[512,384]{1,0:T(8,128)(2,1)} %get-tuple-element.48), channel_id=1, source_target_pairs={{0,8},{8,0},{16,24},{24,16},{1,9},{9,1},{17,25},{25,17},{2,10},{10... | collective-permute-start | bytes 1179656 | tf_op jit(solution)/shard_map/ppermute | solution.py:28
  79.9 12.9 %all-to-all-start.2 = ((f32[8,8,256]{2,1,0:T(8,128)}), f32[8,8,256]{2,1,0:T(8,128)S(1)}, u32[]{:S(2)}, u32[]{:S(2)}) async-start(f32[8,8,256]{2,1,0:T(8,128)} %get-tuple-element.46), calls=%async_computation.2 | async-start | bytes 131072 | tf_op jit(solution)/shard_map/all_to_all | solution.py:517

commit v10 on v7

--- a/solution.py
+++ b/solution.py
@@ -221,40 +221,32 @@
         store.wait()
 
 
-def far_kernel(q_hbm, far_hbm, near_hbm, near_lse_hbm, embedded_sum_ref, own_out, lent_out,
-               pack_ref, q_scr, far_scr, near_scr, near_lse_scr, mixed_scr, lse_scr, out_scr,
-               in_sems, out_sems, *, head_width):
+def far_kernel(q_hbm, far_hbm, near_hbm, near_lse_hbm, embedded_sum_ref, own_ref, lent_ref,
+               pack_ref, q_scr, far_scr, near_scr, near_lse_scr, mixed_scr, lse_scr, sems,
+               *, head_width):
     half = q_scr.shape[1]
-    rows = out_scr.shape[1]
-    spans = (pl.ds(0, rows), pl.ds(rows, rows))
-    sources, targets = [far_hbm], [far_scr]
-    for refs in ((q_hbm, q_scr), (near_hbm, near_scr), (near_lse_hbm, near_lse_scr)):
-        for span in spans:
-            sources.append(refs[0].at[span])
-            targets.append(refs[1].at[span])
-    loads = started(sources, targets, in_sems)
+    rows = own_ref.shape[0]
+    loads = started(
+        (far_hbm, q_hbm, near_hbm, near_lse_hbm), (far_scr, q_scr, near_scr, near_lse_scr), sems
+    )
     loads[0].wait()
-    stores = []
-    sums = []
-    for place, out in enumerate((own_out, lent_out)):
-        loads[1 + place].wait()
+    loads[1].wait()
+    total = jnp.zeros((1, half), F32)
+    for place, out_ref in enumerate((own_ref, lent_ref)):
         span = slice(place * rows, (place + 1) * rows)
         attend(q_scr[span, :], far_scr[:, :half], far_scr[:, half:], head_width,
                mixed_scr.at[place], lse_scr.at[place])
-        loads[3 + place].wait()
-        loads[5 + place].wait()
+        if place == 0:
+            loads[2].wait()
+            loads[3].wait()
         attended = merge_states(
             near_scr[span, :], near_lse_scr[span, :], mixed_scr[place], lse_scr[place]
         )
-        out_scr[place] = attended.astype(BF16)
-        stores += started((out_scr.at[place],), (out,), out_sems, place)
-        sums.append(jnp.sum(attended, axis=0, keepdims=True))
-    total = sums[0] + sums[1]
+        out_ref[...] = attended.astype(BF16)
+        total += jnp.sum(attended, axis=0, keepdims=True)
     pad = jnp.zeros((1, pack_ref.shape[1] * pack_ref.shape[2] - 3 * half), F32)
     packed = pack_row((embedded_sum_ref[...], total, pad))
     pack_ref[...] = jnp.broadcast_to(packed[None], pack_ref.shape)
-    for store in stores:
-        store.wait()
 
 
 def pack_row(pieces):
@@ -462,7 +454,7 @@
     own_half, lent_half, sums = pl.pallas_call(
         functools.partial(far_kernel, head_width=head_width),
         in_specs=[anywhere] * 4 + [vmem],
-        out_specs=[anywhere, anywhere, vmem],
+        out_specs=[vmem] * 3,
         out_shape=[half_rows, half_rows, jax.ShapeDtypeStruct((ranks,) + PACK, F32)],
         scratch_shapes=[
             pltpu.VMEM((2 * rows, half), BF16),
@@ -471,9 +463,7 @@
             pltpu.VMEM((2 * rows, half), F32),
             pltpu.VMEM((2, rows, half), F32),
             pltpu.VMEM((2, rows, half), F32),
-            pltpu.VMEM((2, rows, half), BF16),
-            pltpu.SemaphoreType.DMA((7,)),
-            pltpu.SemaphoreType.DMA((2,)),
+            pltpu.SemaphoreType.DMA((4,)),
         ],
         compiler_params=params,
         cost_estimate=pl.CostEstimate(

time: 93.9 us -> 93.5 us (level)
  transfers between devices with their start and end apart: 6 -> 6, of which waited for: 2 -> 2; matrix products, arithmetic and copies ran while one was open for 6% -> 6% of each run, Pallas kernels for 24% -> 25%
where the time goes in v10:
time: 93.5 us; the launch traced here: 93 us
  Pallas kernels  40.3 us (43%)
  starting transfers between devices  33.8 us (36%)
  waiting for transfers between devices  10.1 us (11%)
  matrix products  5.71 us (6%)
  between operations  2.13 us (2%)
    pallas_call x1, Pallas kernels, on_device(): pl.pallas_call(functools.partial(near_kernel, head_width=head_width, scor...  13.9 us
    pallas_call x1, Pallas kernels, on_device(): pl.pallas_call(functools.partial(far_kernel, head_width=head_width), in_s...  10.5 us
    ppermute x3, starting transfers between devices, swap_with(): lax.ppermute(x, axis, [(i, i ^ 1) for i in range(lax.axis_size(axis))])  9.88 us
    all_to_all x1, starting transfers between devices, on_device(): sums = lax.all_to_all(sums, SEQ_AXES, 0, 0, tiled=True)  9.47 us
    all_to_all x1, waiting for transfers between devices, on_device(): sums = lax.all_to_all(sums, SEQ_AXES, 0, 0, tiled=True)  7.87 us
    all_to_all x1, starting transfers between devices, on_device(): everyone = lax.all_to_all(packed, 'slide', 0, 0, tiled=True)  7.84 us
    all_to_all x1, starting transfers between devices, on_device(): lax.all_to_all(payload, ('x', 'y'), 0, 0, tiled=True)  6.64 us
    pallas_call x1, Pallas kernels, on_device(): pl.pallas_call(embed_kernel, in_specs=[anywhere, anywhere, vmem], out_spe...  6.02 us
  transfers between devices with their start and end apart: 6, of which 2 were waited for; matrix products, arithmetic and copies ran while one was open for 6% of the time, Pallas kernels for 25%

profile of v10, /device:TPU:1, one launch (start us, length us, event | category | flops | bytes accessed | tf_op | source)
XLA Modules:
  0.0 93.0 jit_solution(5855320064149239542)
XLA Ops:
  0.6 0.0 copy-start.1
  0.6 0.0 copy-start.2
  0.7 0.0 copy-start.5
  0.7 6.0 %embed.1 = (bf16[512,768]{1,0:T(8,128)(2,1)}, bf16[512,768]{1,0:T(8,128)(2,1)S(1)}, f32[1,768]{1,0:T(1,128)}) custom-call(bf16[512,1536]{1,0:T(8,128)(2,1)} %bitcast.13, bf16[1536,768]{1,0:T(8,128)(2,1)} %w_hbm.1, f32[768]{0:T(1024)} %gain_ref.1), custom_call_target="tpu_custom_call" | custom-call | tf_op jit(solution)/shard_map/embed/pallas_call | solution.py:357
  6.7 2.2 %collective-permute-start = (bf16[512,768]{1,0:T(8,128)(2,1)S(1)}, bf16[512,768]{1,0:T(8,128)(2,1)}, u32[]{:S(2)}, u32[]{:S(2)}) collective-permute-start(bf16[512,768]{1,0:T(8,128)(2,1)S(1)} %get-tuple-element.29.x_ref), channel_id=1, source_target_pairs={{0,8},{8,0},{16,24},{24,16},{1,9},{9,1},{17,25},{25,17},{2,10},{10... | collective-permute-start | bytes 2359304 | tf_op jit(solution)/shard_map/ppermute | solution.py:28
  8.9 0.0 copy-done.1
  8.9 0.0 copy-done.2
  8.9 2.0 %own_rows.1 = (bf16[2,16,768]{2,1,0:T(8,128)(2,1)S(1)}, bf16[512,384]{1,0:T(8,128)(2,1)S(1)}, bf16[512,384]{1,0:T(8,128)(2,1)S(1)}) custom-call(s32[1]{0:T(128)} %bitcast.part_ref, s32[16]{0:T(128)S(1)} %copy-done.5, bf16[512,768]{1,0:T(8,128)(2,1)S(1)} %get-tuple-element.29.x_ref, bf16[768,768]{1,0:T(8,128)(2,1)S(1)} %copy-done.1, ...), custom_call_target="tpu_custom_call" | custom-call | tf_op jit(solution)/shard_map/own_rows/pallas_call | solution.py:380
  10.9 7.0 %collective-permute-start.1 = (bf16[2,16,768]{2,1,0:T(8,128)(2,1)S(1)}, bf16[2,16,768]{2,1,0:T(8,128)(2,1)S(1)}, u32[]{:S(2)}, u32[]{:S(2)}) collective-permute-start(bf16[2,16,768]{2,1,0:T(8,128)(2,1)S(1)} %get-tuple-element.36.own_ref), channel_id=1, source_target_pairs={{0,32},{32,0},{1,33},{33,1},{2,34},{34,2},{3,35},{35,3},{4,36},{36... | collective-permute-start | bytes 147464 | tf_op jit(solution)/shard_map/ppermute | solution.py:28
  17.9 0.0 copy-done.6
  17.9 4.7 %own_attention.1 = (bf16[512,384]{1,0:T(8,128)(2,1)}, f32[512,384]{1,0:T(8,128)}, f32[512,384]{1,0:T(8,128)}) custom-call(s32[1]{0:T(128)} %bitcast.part_ref, bf16[512,768]{1,0:T(8,128)(2,1)S(1)} %get-tuple-element.29.x_ref, bf16[768,768]{1,0:T(8,128)(2,1)S(1)} %copy-done.6, bf16[512,384]{1,0:T(8,128)(2,1)S(1)} %get-tuple-element.30.k_ref.k_hbm, ...), custom_call_target="tpu_custom_call" | custom-call | flops 3000000000 | bytes 4000000 | tf_op jit(solution)/shard_map/own_attention/pallas_call | solution.py:404
  22.7 0.0 collective-permute-done.1.other_ref
  22.7 1.0 %payload.1 = bf16[8,2,2,16,768]{4,3,2,1,0:T(8,128)(2,1)} custom-call(bf16[2,16,768]{2,1,0:T(8,128)(2,1)S(1)} %get-tuple-element.36.own_ref, bf16[2,16,768]{2,1,0:T(8,128)(2,1)S(1)} %collective-permute-done.1.other_ref), custom_call_target="tpu_custom_call" | custom-call | tf_op jit(solution)/shard_map/payload/pallas_call | solution.py:393
  23.7 6.6 %all-to-all-start = ((bf16[16,32,768]{2,1,0:T(8,128)(2,1)}), bf16[16,32,768]{2,1,0:T(8,128)(2,1)S(1)}, u32[]{:S(2)}, u32[]{:S(2)}) async-start(bf16[16,32,768]{2,1,0:T(8,128)(2,1)} %bitcast.2), calls=%async_computation | async-start | bytes 1572864 | tf_op jit(solution)/shard_map/all_to_all | solution.py:400
  30.3 0.0 collective-permute-done.other_hbm
  30.3 13.9 %near_attention.1 = (bf16[1024,384]{1,0:T(8,128)(2,1)}, f32[1024,384]{1,0:T(8,128)}, f32[1024,384]{1,0:T(8,128)}) custom-call(s32[1]{0:T(128)} %bitcast.part_ref, bf16[512,768]{1,0:T(8,128)(2,1)} %collective-permute-done.other_hbm, bf16[512,384]{1,0:T(8,128)(2,1)} %copy-done.7, bf16[512,384]{1,0:T(8,128)(2,1)} %copy-done.8, ...), custom_call_target="tpu_custom_call" | custom-call | flops 8999999488 | bytes 8000000 | tf_op jit(solution)/shard_map/near_attention/pallas_call | solution.py:428
  44.2 0.0 all-to-all-done
  44.3 0.9 copy-done.9
  45.1 10.5 %far_attention.1 = (bf16[512,384]{1,0:T(8,128)(2,1)}, bf16[512,384]{1,0:T(8,128)(2,1)}, f32[32,8,256]{2,1,0:T(8,128)}) custom-call(bf16[1024,384]{1,0:T(8,128)(2,1)} %get-tuple-element.35.q_hbm, bf16[512,768]{1,0:T(8,128)(2,1)} %bitcast.14, f32[1024,384]{1,0:T(8,128)} %get-tuple-element.37.near_hbm, f32[1024,384]{1,0:T(8,128)} %get-tuple-element.38.near_lse_hbm, ...), custom_call_target="tpu_custom_call" | custom-call | flops 6000000000 | bytes 6000000 | tf_op jit(solution)/shard_map/far_attention/pallas_call | solution.py:454
  55.6 9.5 %all-to-all-start.1 = ((f32[32,8,256]{2,1,0:T(8,128)}), f32[32,8,256]{2,1,0:T(8,128)S(1)}, u32[]{:S(2)}, u32[]{:S(2)}) async-start(f32[32,8,256]{2,1,0:T(8,128)} %get-tuple-element.40), calls=%async_computation.1 | async-start | bytes 524288 | tf_op jit(solution)/shard_map/all_to_all | solution.py:475
  66.4 0.0 copy-start.3
  66.4 0.0 copy-start.4
  66.5 2.8 %convert_add_fusion = f32[512,768]{1,0:T(8,128)} fusion(bf16[512,768]{1,0:T(8,128)(2,1)S(1)} %copy-done.10, bf16[512,384]{1,0:T(8,128)(2,1)} %get-tuple-element.43, bf16[768,768]{1,0:T(8,128)(2,1)S(1)} %copy-done, s32[]{:T(128)S(6)} %select_n.22), kind=kOutput, calls=%fused_computation.1 | convolution fusion | flops 302776320 | bytes 3342340 | tf_op jit(solution)/shard_map/dot_general | solution.py:480
  69.3 7.9 %all-to-all-done.1.sums_ref = f32[32,8,256]{2,1,0:T(8,128)S(1)} async-done(((f32[32,8,256]{2,1,0:T(8,128)}), f32[32,8,256]{2,1,0:T(8,128)S(1)}, u32[]{:S(2)}, u32[]{:S(2)}) %all-to-all-start.1) | async-done | bytes 262176 | tf_op jit(solution)/shard_map/all_to_all | solution.py:475
  77.2 0.7 collective-permute-start.2
  77.9 0.0 copy-done.3
  77.9 1.3 %pooled.1 = (f32[1,768]{1,0:T(1,128)}, f32[8,8,256]{2,1,0:T(8,128)}) custom-call(f32[512]{0:T(512)S(1)} %select_convert_fusion.codes_ref, f32[32,8,256]{2,1,0:T(8,128)S(1)} %all-to-all-done.1.sums_ref, bf16[768,768]{1,0:T(8,128)(2,1)S(1)} %copy-done, bf16[768,768]{1,0:T(8,128)(2,1)S(1)} %copy-done.3, bf16[1,768]{1,0:T(2,128)(2,1)S(1)} %copy-done.4), custom_call_target="tpu_custom_call" | custom-call | tf_op jit(solution)/shard_map/pooled/pallas_call | solution.py:487
  79.2 7.8 %all-to-all-start.2 = ((f32[8,8,256]{2,1,0:T(8,128)}), f32[8,8,256]{2,1,0:T(8,128)S(1)}, u32[]{:S(2)}, u32[]{:S(2)}) async-start(f32[8,8,256]{2,1,0:T(8,128)} %get-tuple-element.46), calls=%async_computation.2 | async-start | bytes 131072 | tf_op jit(solution)/shard_map/all_to_all | solution.py:497
  87.0 0.0 collective-permute-done.2
  87.0 2.9 %fusion = bf16[1,512,768]{2,1,0:T(8,128)(2,1)} fusion(f32[512,768]{1,0:T(8,128)} %convert_add_fusion, bf16[512,384]{1,0:T(8,128)(2,1)S(1)} %collective-permute-done.2, bf16[768,768]{1,0:T(8,128)(2,1)S(1)} %copy-done, s32[]{:T(128)S(6)} %select_n.25), kind=kOutput, calls=%fused_computation.2 | convolution fusion | flops 302776320 | bytes 3342340 | tf_op jit(solution)/shard_map/dot_general | solution.py:483
  89.9 2.2 %all-to-all-done.2.all_ref = f32[8,8,256]{2,1,0:T(8,128)S(1)} async-done(((f32[8,8,256]{2,1,0:T(8,128)}), f32[8,8,256]{2,1,0:T(8,128)S(1)}, u32[]{:S(2)}, u32[]{:S(2)}) %all-to-all-start.2) | async-done | bytes 65568 | tf_op jit(solution)/shard_map/all_to_all | solution.py:497
  92.1 1.0 %contrast.1 = (f32[8,8]{1,0:T(8,128)}, f32[1,1]{1,0:T(1,128)}) custom-call(f32[8,8,256]{2,1,0:T(8,128)S(1)} %all-to-all-done.2.all_ref), custom_call_target="tpu_custom_call" | custom-call | tf_op jit(solution)/shard_map/contrast/pallas_call | solution.py:499
  (13 shorter events, 0.0 us)
Async XLA Ops:
  0.6 8.3 %copy-start.1 = (bf16[768,768]{1,0:T(8,128)(2,1)S(1)}, bf16[768,768]{1,0:T(8,128)(2,1)}, u32[]{:S(2)}) copy-start(bf16[768,768]{1,0:T(8,128)(2,1)} %wk_hbm.1) | copy-start | bytes 3538948
  0.6 8.3 %copy-start.2 = (bf16[768,768]{1,0:T(8,128)(2,1)S(1)}, bf16[768,768]{1,0:T(8,128)(2,1)}, u32[]{:S(2)}) copy-start(bf16[768,768]{1,0:T(8,128)(2,1)} %wv_hbm.1) | copy-start | bytes 3538948
  0.7 8.3 %copy-start.5 = (s32[16]{0:T(128)S(1)}, s32[16]{0:T(128)}, u32[]{:S(2)}) copy-start(s32[16]{0:T(128)} %offset_ref.1) | copy-start | bytes 196
  6.7 23.6 %collective-permute-start = (bf16[512,768]{1,0:T(8,128)(2,1)S(1)}, bf16[512,768]{1,0:T(8,128)(2,1)}, u32[]{:S(2)}, u32[]{:S(2)}) collective-permute-start(bf16[512,768]{1,0:T(8,128)(2,1)S(1)} %get-tuple-element.29.x_ref), channel_id=1, source_target_pairs={{0,8},{8,0},{16,24},{24,16},{1,9},{9,1},{17,25},{25,17},{2,10},{10... | collective-permute-start | bytes 2359304 | tf_op jit(solution)/shard_map/ppermute | solution.py:28
  8.9 9.0 %copy-start.6 = (bf16[768,768]{1,0:T(8,128)(2,1)S(1)}, bf16[768,768]{1,0:T(8,128)(2,1)}, u32[]{:S(2)}) copy-start(bf16[768,768]{1,0:T(8,128)(2,1)} %wq_hbm.1) | copy-start | bytes 3538948
  10.9 11.8 %copy-start.7 = (bf16[512,384]{1,0:T(8,128)(2,1)}, bf16[512,384]{1,0:T(8,128)(2,1)S(1)}, u32[]{:S(2)}) copy-start(bf16[512,384]{1,0:T(8,128)(2,1)S(1)} %get-tuple-element.30.k_ref.k_hbm) | copy-start | bytes 1179652
  10.9 11.8 %copy-start.8 = (bf16[512,384]{1,0:T(8,128)(2,1)}, bf16[512,384]{1,0:T(8,128)(2,1)S(1)}, u32[]{:S(2)}) copy-start(bf16[512,384]{1,0:T(8,128)(2,1)S(1)} %get-tuple-element.31.v_ref.v_hbm) | copy-start | bytes 1179652
  10.9 11.8 %collective-permute-start.1 = (bf16[2,16,768]{2,1,0:T(8,128)(2,1)S(1)}, bf16[2,16,768]{2,1,0:T(8,128)(2,1)S(1)}, u32[]{:S(2)}, u32[]{:S(2)}) collective-permute-start(bf16[2,16,768]{2,1,0:T(8,128)(2,1)S(1)} %get-tuple-element.36.own_ref), channel_id=1, source_target_pairs={{0,32},{32,0},{1,33},{33,1},{2,34},{34,2},{3,35},{35,3},{4,36},{36... | collective-permute-start | bytes 147464 | tf_op jit(solution)/shard_map/ppermute | solution.py:28
  23.7 20.6 %all-to-all-start = ((bf16[16,32,768]{2,1,0:T(8,128)(2,1)}), bf16[16,32,768]{2,1,0:T(8,128)(2,1)S(1)}, u32[]{:S(2)}, u32[]{:S(2)}) async-start(bf16[16,32,768]{2,1,0:T(8,128)(2,1)} %bitcast.2), calls=%async_computation | async-start | bytes 1572864 | tf_op jit(solution)/shard_map/all_to_all | solution.py:400
  44.2 0.9 copy-start.9
  45.1 21.3 %copy-start = (bf16[768,768]{1,0:T(8,128)(2,1)S(1)}, bf16[768,768]{1,0:T(8,128)(2,1)}, u32[]{:S(2)}) copy-start(bf16[768,768]{1,0:T(8,128)(2,1)} %w_out_ref.1) | copy-start | bytes 3538948
  45.1 21.3 %copy-start.10 = (bf16[512,768]{1,0:T(8,128)(2,1)S(1)}, bf16[512,768]{1,0:T(8,128)(2,1)}, u32[]{:S(2)}) copy-start(bf16[512,768]{1,0:T(8,128)(2,1)} %get-tuple-element.42) | copy-start | bytes 2359300
  55.6 21.6 %all-to-all-start.1 = ((f32[32,8,256]{2,1,0:T(8,128)}), f32[32,8,256]{2,1,0:T(8,128)S(1)}, u32[]{:S(2)}, u32[]{:S(2)}) async-start(f32[32,8,256]{2,1,0:T(8,128)} %get-tuple-element.40), calls=%async_computation.1 | async-start | bytes 524288 | tf_op jit(solution)/shard_map/all_to_all | solution.py:475
  66.4 11.4 %copy-start.3 = (bf16[768,768]{1,0:T(8,128)(2,1)S(1)}, bf16[768,768]{1,0:T(8,128)(2,1)}, u32[]{:S(2)}) copy-start(bf16[768,768]{1,0:T(8,128)(2,1)} %w_head_ref.1) | copy-start | bytes 3538948
  66.4 11.4 %copy-start.4 = (bf16[1,768]{1,0:T(2,128)(2,1)S(1)}, bf16[1,768]{1,0:T(2,128)(2,1)}, u32[]{:S(2)}) copy-start(bf16[1,768]{1,0:T(2,128)(2,1)} %report_ref.1) | copy-start | bytes 4612
  77.2 9.8 %collective-permute-start.2 = (bf16[512,384]{1,0:T(8,128)(2,1)}, bf16[512,384]{1,0:T(8,128)(2,1)S(1)}, u32[]{:S(2)}, u32[]{:S(2)}) collective-permute-start(bf16[512,384]{1,0:T(8,128)(2,1)} %get-tuple-element.48), channel_id=1, source_target_pairs={{0,8},{8,0},{16,24},{24,16},{1,9},{9,1},{17,25},{25,17},{2,10},{10... | collective-permute-start | bytes 1179656 | tf_op jit(solution)/shard_map/ppermute | solution.py:28
  79.2 12.9 %all-to-all-start.2 = ((f32[8,8,256]{2,1,0:T(8,128)}), f32[8,8,256]{2,1,0:T(8,128)S(1)}, u32[]{:S(2)}, u32[]{:S(2)}) async-start(f32[8,8,256]{2,1,0:T(8,128)} %get-tuple-element.46), calls=%async_computation.2 | async-start | bytes 131072 | tf_op jit(solution)/shard_map/all_to_all | solution.py:497
